TPU v7x, 32 devices: a whole 2x2x4 slice. The times are simulated.
32 devices in a mesh: wide: 16 (over z, x, core), narrow: 2 (over y).
Axes of the slice: x: 2, y: 2, z: 4, core: 2. Of those that a mesh axis runs over, the one named last changes fastest.
Arguments:
- layer_in: bfloat16 [16, 1280, 768], P('wide', 'narrow'), may hold values from -6 to 6
- pre_gain: float32 [768], replicated, may hold values from 0.5 to 1.5
- w_heads: bfloat16 [768, 24, 130], P(None, 'narrow'), may hold values from -0.21875 to 0.21875
- w_bc: bfloat16 [768, 256], replicated, may hold values from -0.21875 to 0.21875
- conv_x: float32 [7, 24, 64], P(None, 'narrow'), may hold values from -2 to 2
- conv_bc: float32 [7, 256], replicated, may hold values from -2 to 2
- dt_bias: float32 [24, 2], P('narrow'), may hold values from -7 to -3
- a_log: float32 [24], P('narrow'), may hold values from -1 to 1.5
- skip_d: float32 [24], P('narrow'), may hold values from 0.5 to 1.5
- norm_gain: float32 [24, 64], P('narrow'), may hold values from 0.5 to 1.5
- w_out: bfloat16 [24, 64, 768], P('narrow'), may hold values from -0.15625 to 0.15625
- cotangent: bfloat16 [16, 1280, 768], P('wide', 'narrow'), may hold values from -6 to 6
- starts: int32 [16, 4], P('wide'), may hold values from 0 to 1279, as said below
- live: int32 [16, 1280], P('wide'), may hold values from 0 to 1, as said below
Outputs:
- out: bfloat16 [16, 1280, 768], P('wide', 'narrow')
- grad_input: float32 [16, 1280, 768], P('wide', 'narrow')
- grad_pre_gain: float32 [768], P('wide')
- grad_w_heads: float32 [768, 24, 130], P('wide', 'narrow')
- grad_w_bc: float32 [768, 256], P('wide')
- grad_conv_x: float32 [7, 24, 64], P(None, 'narrow', 'wide')
- grad_conv_bc: float32 [7, 256], P(None, 'wide')
- grad_dt_bias: float32 [24, 2], P('narrow')
- grad_a_log: float32 [24], P('narrow')
- grad_skip_d: float32 [24], P('narrow')
- grad_norm_gain: float32 [24, 64], P('narrow', 'wide')
- grad_w_out: float32 [24, 64, 768], P('narrow', None, 'wide')
Inputs may be any that keep to these rules, and one draw needn't show every extreme that they name: Per row the starts are increasing and the first is 0; in every row the second document starts below 160 and the third at or beyond 1280 - 1280 / 16; in some row the last document starts at the row's last position. In every row the live positions are a prefix of the row, of 1200 or more positions.
All inputs are finite; a program needn't handle non-finite values.
Results may differ from a plain program's by a relative error of at most 0.0088.
Values may be sent and summed in bfloat16 or wider, within the bound.
A program may use at most 384 MiB of HBM per device.

v0:
```python
import functools

import jax
import jax.numpy as jnp
from jax import lax
from jax.experimental import pallas as pl
from jax.experimental.pallas import tpu as pltpu
from jax.sharding import PartitionSpec as P

H = 24
HD = 64
BLOCK = 128
SEQ_LEN = 1280


EPS = 1e-05
HIGH = lax.Precision.HIGHEST


def rounded(value):
    return value + lax.stop_gradient(value.astype(jnp.bfloat16).astype(jnp.float32) - value)


def segment_ids(starts):
    where_at = jnp.arange(SEQ_LEN, dtype=jnp.int32)
    hits = (starts[:, :, None] <= where_at[None, None, :]).astype(jnp.int32)
    return jnp.sum(hits, axis=1) - 1


def conv_doc(values, taps, seg):
    half = (taps.shape[0] - 1) // 2
    length = values.shape[1]
    padded = jnp.pad(values, ((0, 0), (half, half), (0, 0)))
    seg_pad = jnp.pad(seg, ((0, 0), (half, half)), constant_values=-1)
    total = jnp.zeros_like(values)
    for offset in range(taps.shape[0]):
        same = (seg_pad[:, offset : offset + length] == seg).astype(values.dtype)
        total = total + taps[offset] * padded[:, offset : offset + length] * same[:, :, None]
    return total


def ssd_forward(xc, steps, decays, bmat, cmat, seg, prec):
    rows, length, heads, hdim = xc.shape
    blocks = length // BLOCK
    xb = xc.reshape(rows, blocks, BLOCK, heads, hdim)
    stepb = steps.reshape(rows, blocks, BLOCK, heads)
    cum = jnp.cumsum(decays.reshape(rows, blocks, BLOCK, heads), axis=2)
    bb = bmat.reshape(rows, blocks, BLOCK, -1)
    cb = cmat.reshape(rows, blocks, BLOCK, -1)
    sb = seg.reshape(rows, blocks, BLOCK)
    order = jnp.arange(BLOCK, dtype=jnp.int32)
    causal = order[:, None] >= order[None, :]
    same = ((sb[:, :, :, None] == sb[:, :, None, :]) & causal)[..., None]
    diff = cum[:, :, :, None, :] - cum[:, :, None, :, :]
    weights = jnp.where(same, jnp.exp(jnp.where(same, diff, 0.0)), 0.0)
    inner = jnp.einsum("rbtn,rbsn->rbts", cb, bb, precision=prec)
    mix = weights * inner[..., None] * stepb[:, :, None, :, :]
    intra = jnp.einsum("rbtsh,rbshp->rbthp", mix, xb, precision=prec)
    last = sb[:, :, -1]
    cum_end = cum[:, :, -1, :]
    to_end = (
        (sb == last[:, :, None]).astype(cum.dtype)[..., None]
        * jnp.exp(cum_end[:, :, None, :] - cum)
        * stepb
    )
    states = jnp.einsum("rbshp,rbsn->rbhpn", to_end[..., None] * xb, bb, precision=prec)
    decay_end = jnp.exp(cum_end)

    def carry_step(carry, item):
        state, seg_prev = carry
        block_state, block_last, block_decay = item
        keep = (block_last == seg_prev).astype(state.dtype)[:, None, None, None]
        fresh = keep * block_decay[:, :, None, None] * state + block_state
        return ((fresh, block_last), (state, seg_prev))

    init = (
        jnp.zeros((rows, heads, hdim, bb.shape[-1]), xc.dtype),
        jnp.full((rows,), -1, jnp.int32),
    )
    items = (jnp.moveaxis(states, 1, 0), jnp.moveaxis(last, 1, 0), jnp.moveaxis(decay_end, 1, 0))
    _, (before, seg_before) = lax.scan(carry_step, init, items)
    before = jnp.moveaxis(before, 0, 1)
    seg_before = jnp.moveaxis(seg_before, 0, 1)
    enter = (sb == seg_before[:, :, None]).astype(cum.dtype)[..., None] * jnp.exp(cum)
    inter = jnp.einsum("rbtn,rbhpn->rbthp", cb, before, precision=prec) * enter[..., None]
    return (intra + inter).reshape(rows, length, heads, hdim)


def mixer(proj, bcproj, conv_x, conv_bc, dt_bias, a_log, skip_d, seg, mask, rounder, prec):
    rows, length, heads, width = proj.shape
    hdim = (width - 2) // 2
    state = bcproj.shape[-1] // 4
    gate = proj[..., :hdim]
    values = proj[..., hdim : 2 * hdim] * mask[:, :, None, None]
    mixed_x = conv_doc(
        values.reshape(rows, length, heads * hdim),
        conv_x.reshape(conv_x.shape[0], heads * hdim),
        seg,
    )
    xc = rounder(jax.nn.silu(mixed_x)).reshape(rows, length, heads, hdim)
    maps = rounder(jax.nn.silu(conv_doc(bcproj * mask[:, :, None], conv_bc, seg)))
    b_fwd = maps[..., :state]
    c_fwd = maps[..., state : 2 * state]
    b_bwd = maps[..., 2 * state : 3 * state]
    c_bwd = maps[..., 3 * state :]
    rate = -jnp.exp(a_log)
    dt_fwd = jax.nn.softplus(proj[..., 2 * hdim] + dt_bias[:, 0]) * mask[:, :, None]
    dt_bwd = jax.nn.softplus(proj[..., 2 * hdim + 1] + dt_bias[:, 1]) * mask[:, :, None]
    out_fwd = ssd_forward(xc, dt_fwd, dt_fwd * rate, b_fwd, c_fwd, seg, prec)

    def flip(v):
        return jnp.flip(v, axis=1)

    out_bwd = flip(
        ssd_forward(
            flip(xc), flip(dt_bwd), flip(dt_bwd * rate), flip(b_bwd), flip(c_bwd), flip(seg), prec
        )
    )
    keep_prev = (seg[:, 1:] == seg[:, :-1]).astype(xc.dtype)[:, :, None, None]
    shifted_fwd = jnp.pad(out_fwd[:, :-1] * keep_prev, ((0, 0), (1, 0), (0, 0), (0, 0)))
    shifted_bwd = jnp.pad(out_bwd[:, 1:] * keep_prev, ((0, 0), (0, 1), (0, 0), (0, 0)))
    return (shifted_fwd + shifted_bwd + skip_d[:, None] * xc, gate)


def shards(
    layer_in,
    pre_gain,
    w_heads,
    w_bc,
    conv_x,
    conv_bc,
    dt_bias,
    a_log,
    skip_d,
    norm_gain,
    w_out,
    cotangent,
    starts,
    live,
):
    seg = segment_ids(starts)
    mask = live.astype(jnp.float32)
    x_here = layer_in.astype(jnp.float32)
    scale = lax.rsqrt(jnp.mean(x_here * x_here, axis=-1, keepdims=True) + EPS)
    normed_here = (x_here * scale * pre_gain).astype(jnp.bfloat16)
    normed = lax.all_gather(normed_here, "narrow", axis=1, tiled=True)
    proj = jnp.einsum("rld,dhc->rlhc", normed, w_heads, preferred_element_type=jnp.float32)
    bcproj = jnp.einsum("rld,dc->rlc", normed, w_bc, preferred_element_type=jnp.float32)

    def mix_local(proj_in, bc_in, taps_x, taps_bc, bias_in, log_rate, diag_in):
        return mixer(
            proj_in, bc_in, taps_x, taps_bc, bias_in, log_rate, diag_in, seg, mask, rounded, HIGH
        )

    (ymix, gate), pull_mix = jax.vjp(
        mix_local, proj, bcproj, conv_x, conv_bc, dt_bias, a_log, skip_d
    )
    rows, length, heads, hdim = ymix.shape
    sigma = jax.nn.sigmoid(gate)
    act = gate * sigma
    gated = (ymix * act).reshape(rows, length, heads * hdim)
    squares = lax.psum(jnp.sum(gated * gated, axis=-1), "narrow")
    inv = lax.rsqrt(squares / (H * HD) + EPS)[..., None]
    gain_flat = norm_gain.reshape(-1)
    normalized = gated * inv
    hn = (normalized * gain_flat).astype(jnp.bfloat16)
    w_flat = w_out.reshape(heads * hdim, -1)
    partial_value = jnp.einsum("rlc,cd->rld", hn, w_flat, preferred_element_type=jnp.float32)
    branch = lax.psum_scatter(partial_value, "narrow", scatter_dimension=1, tiled=True)
    out = (x_here + branch).astype(jnp.bfloat16)
    grad_out = lax.all_gather(cotangent, "narrow", axis=1, tiled=True)
    g_w_out = jnp.einsum("rlc,rld->cd", hn, grad_out, preferred_element_type=jnp.float32)
    g_hn = jnp.einsum("rld,cd->rlc", grad_out, w_flat, preferred_element_type=jnp.float32)
    g_gain = jnp.sum(g_hn * normalized, axis=(0, 1))
    weighted = g_hn * gain_flat
    cross = lax.psum(jnp.sum(weighted * gated, axis=-1), "narrow")
    g_gated = inv * weighted - gated * (inv * inv * inv) * (cross / (H * HD))[..., None]
    g_gated = g_gated.reshape(rows, length, heads, hdim)
    g_ymix = g_gated * act
    g_gate = g_gated * ymix * (sigma * (1.0 + gate * (1.0 - sigma)))
    g_proj, g_bcproj, g_conv_x, g_conv_bc, g_dt_bias, g_a_log, g_skip = pull_mix((g_ymix, g_gate))
    g_proj_low = g_proj.astype(jnp.bfloat16)
    g_w_heads = jnp.einsum("rld,rlhc->dhc", normed, g_proj_low, preferred_element_type=jnp.float32)
    g_w_bc = jnp.einsum(
        "rld,rlc->dc", normed, g_bcproj, precision=HIGH, preferred_element_type=jnp.float32
    )
    g_normed = jnp.einsum("rlhc,dhc->rld", g_proj_low, w_heads, preferred_element_type=jnp.float32)
    g_normed = g_normed + jnp.einsum(
        "rlc,dc->rld", g_bcproj, w_bc, precision=HIGH, preferred_element_type=jnp.float32
    )
    g_normed_here = lax.psum_scatter(g_normed, "narrow", scatter_dimension=1, tiled=True)
    weighted_in = g_normed_here * pre_gain
    g_pre = jnp.sum(g_normed_here * x_here * scale, axis=(0, 1))
    g_x = scale * weighted_in - x_here * (scale * scale * scale) * jnp.mean(
        weighted_in * x_here, axis=-1, keepdims=True
    )
    grad_input = cotangent.astype(jnp.float32) + g_x
    g_pre, g_w_bc, g_conv_bc = lax.psum((g_pre, g_w_bc, g_conv_bc), "narrow")
    reduced = (
        lax.psum_scatter(g_w_heads, "wide", scatter_dimension=0, tiled=True),
        lax.psum_scatter(g_w_out.reshape(heads, hdim, -1), "wide", scatter_dimension=2, tiled=True),
        lax.psum_scatter(g_conv_x, "wide", scatter_dimension=2, tiled=True),
        lax.psum_scatter(g_gain.reshape(heads, hdim), "wide", scatter_dimension=1, tiled=True),
        lax.psum_scatter(g_pre, "wide", scatter_dimension=0, tiled=True),
        lax.psum_scatter(g_w_bc, "wide", scatter_dimension=0, tiled=True),
        lax.psum_scatter(g_conv_bc, "wide", scatter_dimension=1, tiled=True),
    )
    share_pre, share_bc, share_conv = (reduced[4], reduced[5], reduced[6])
    head_bias, head_rate, head_diag = lax.psum((g_dt_bias, g_a_log, g_skip), "wide")
    return (
        out,
        grad_input,
        share_pre,
        reduced[0],
        share_bc,
        reduced[2],
        share_conv,
        head_bias,
        head_rate,
        head_diag,
        reduced[3],
        reduced[1],
    )


HALO = 16
F32 = jnp.float32
BF16 = jnp.bfloat16
LOGZERO = -1e30


def mm(a, b, dims=((1,), (0,)), precision=None):
    return lax.dot_general(a, b, (dims, ((), ())), precision=precision, preferred_element_type=F32)


def nt(a, b):
    return mm(a, b, ((1,), (1,)))


def tn(a, b):
    return mm(a, b, ((0,), (0,)))


def seg_at(info, pos):
    seg = jnp.full(pos.shape, -1, jnp.int32)
    for j in range(4):
        seg = seg + (pos >= info[j]).astype(jnp.int32)
    return jnp.where(pos >= info[6], 99, seg)


def iota(shape, dim):
    return lax.broadcasted_iota(jnp.int32, shape, dim)


def silu_parts(v):
    sg = 0.5 * jnp.tanh(0.5 * v) + 0.5
    act = v * sg
    return act, sg + act * (1.0 - sg)


def thirds(v):
    hi = v.astype(BF16).astype(F32)
    rest = v - hi
    mid = rest.astype(BF16).astype(F32)
    return hi, mid, rest - mid


def column_terms(values):
    sub = iota((16, 128), 0)
    v = jnp.ones((16, 128), F32)
    for k, value in enumerate(values):
        v = jnp.where((sub >= 3 * k) & (sub < 3 * k + 3), value, v)
    hi, mid, low = thirds(v)
    part = sub % 3
    out = jnp.where(part == 0, hi, jnp.where(part == 1, mid, low))
    return jnp.where(sub < 3 * len(values), out, 1.0).astype(BF16)


def row_base(count, places):
    sub = iota((16, 384), 0)
    lane = iota((16, 384), 1)
    out = jnp.zeros((16, 384), F32)
    for k, spans in enumerate(places):
        for lo, hi in spans:
            out = jnp.where((sub >= 3 * k) & (sub < 3 * k + 3) & (lane >= lo) & (lane < hi), 1.0, out)
    return out


def row_terms(count, base, one, two):
    sub = iota((16, 128), 0)
    part = sub - 3 * count
    made = []
    for k, value in enumerate((one, two)):
        hi, mid, low = thirds(jnp.broadcast_to(value, (16, 128)))
        here = base[:, 128 * k : 128 * (k + 1)]
        made.append(
            jnp.where(part == 0, hi, jnp.where(part == 1, mid, jnp.where(part == 2, low, here))).astype(BF16)
        )
    return jnp.concatenate(made + [base[:, 256:].astype(BF16)], axis=1)


def conv_taps(src, seg_src, taps, first, rows):
    seg0 = seg_src[first : first + rows, :]
    total = src[first : first + rows, :] * taps[3:4, :]
    for k in (0, 1, 2, 4, 5, 6):
        lo = first + k - 3
        same = seg_src[lo : lo + rows, :] == seg0
        total = total + jnp.where(same, src[lo : lo + rows, :], 0.0) * taps[k : k + 1, :]
    return total


def front_kernel(
    length, hl, starts, live_ref, x_in, gain, wbc_ref, taps_ref, small_a, small_b,
    info, taps_o, gain_o, skip_o, wdt, wbc, taps, normed_o, rs_o, bcm_h, dsl_h, maps_h, ta_o, tb_o, tc_h, dpt_o, sig_h, seg_s, maps_s, cum_s, x_s, bcm_o, dsl_o, maps_o, tc_o, sig_o, sems,
):
    late = []

    def send(src, dst):
        late.append(pltpu.make_async_copy(src, dst, sems.at[len(late)]))
        late[-1].start()

    nb = length // BLOCK
    ext = length + 2 * HALO
    dm = x_in.shape[1]
    n = lax.axis_index("narrow")
    for i in range(4):
        info[i] = starts[0, i]
    count = jnp.sum(live_ref[...].astype(F32)).astype(jnp.int32)
    off = n * length
    info[4] = count
    info[5] = off
    info[6] = live_ref.shape[1]
    info[7] = n
    ch = small_a.shape[1]
    for k, small in enumerate((small_a, small_b)):
        cols = slice(k * ch, (k + 1) * ch)
        taps_o[:, cols] = small[0:8, :]
        gain_o[:, cols] = jnp.broadcast_to(small[7:8, :], (8, ch))
        skip_o[:, cols] = jnp.broadcast_to(small[8:9, :], (8, ch))
    dst = iota((128, 2 * hl), 0)
    src = iota((128, 2 * hl), 1)
    place = (src % 2) * 64 + src // 2
    at_a = jnp.where(dst == place, 1.0, 0.0).astype(BF16)
    at_b = jnp.where(dst == place + hl, 1.0, 0.0).astype(BF16)
    own_steps = small_a[16 : 16 + 2 * hl, :].astype(BF16)
    far_steps = small_b[16 : 16 + 2 * hl, :].astype(BF16)
    wdt[...] = (mm(at_a, own_steps) + mm(at_b, far_steps)).astype(BF16)
    wbc[...] = pack_columns(wbc_ref[...])
    taps[...] = pack_columns(taps_ref[...])

    bias = small_a[9:10, 0:128] + pltpu.roll(small_b[9:10, 0:128], hl, 1)
    alog = small_a[9:10, 128:256] + pltpu.roll(small_b[9:10, 128:256], hl, 1)
    edge = small_b[16 + 2 * hl : 24 + 2 * hl, :]
    zero_edge = jnp.zeros((8, dm), F32)
    before = jnp.concatenate([zero_edge, jnp.where(n == 1, edge, 0.0)], axis=0)
    behind = jnp.concatenate([jnp.where(n == 1, 0.0, edge), zero_edge], axis=0)
    x_s[0:HALO, :] = before.astype(BF16)
    x_s[HALO : HALO + length, :] = x_in[...]
    x_s[HALO + length : ext, :] = behind.astype(BF16)
    x = x_s[...].astype(F32)
    rs = lax.rsqrt(jnp.mean(x * x, axis=1, keepdims=True) + EPS)
    normed = (x * rs * gain[...]).astype(BF16)
    normed_o[...] = normed
    rs_o[...] = rs[HALO : HALO + length, :]
    pos256 = iota((ext, 256), 0) + (off - HALO)
    seg_s[...] = seg_at(info, pos256)
    live = pos256 < count
    bcm_o[...] = jnp.where(live, mm(normed, wbc[...]), 0.0)
    send(bcm_o, bcm_h)
    crows = length + HALO
    cfirst = HALO // 2
    mix = conv_taps(bcm_o, seg_s, taps, cfirst, crows)
    maps, dsl = silu_parts(mix)
    dsl_o[...] = jnp.zeros_like(dsl_o)
    dsl_o[cfirst : cfirst + crows, :] = dsl
    send(dsl_o, dsl_h)
    maps_s[...] = jnp.zeros_like(maps_s)
    maps_s[cfirst : cfirst + crows, :] = maps.astype(BF16).astype(F32)
    own = slice(HALO, HALO + length)
    segx = seg_s[own, 0:128]
    lane = iota((length, 128), 1)
    fwd = lane < 64
    segp = seg_s[HALO - 1 : HALO - 1 + length, 0:128]
    segn = seg_s[HALO + 1 : HALO + 1 + length, 0:128]
    bmap = maps_s[own, 0:128]
    cprev = jnp.where(segp == segx, maps_s[HALO - 1 : HALO - 1 + length, 128:256], 0.0)
    cnext = jnp.where(segn == segx, maps_s[HALO + 1 : HALO + 1 + length, 128:256], 0.0)
    cmap = jnp.where(fwd, cprev, cnext)
    maps_o[:, 0:128] = bmap.astype(BF16)
    maps_o[:, 128:256] = cmap.astype(BF16)
    send(maps_o, maps_h)
    raw = nt(normed[own, :], wdt[...]) + bias
    softp = jnp.maximum(raw, 0.0) + jnp.log(1.0 + jnp.exp(-jnp.abs(raw)))
    softp = jnp.where(raw < -15.0, jnp.exp(jnp.minimum(raw, 0.0)), softp)
    pos128 = iota((length, 128), 0) + off
    m = pos128 < count
    dt = jnp.where(m, softp, 0.0)
    sg = jnp.where(m, 1.0 / (1.0 + jnp.exp(-raw)), 0.0)
    ratio = jnp.where(m, jnp.where(raw < -15.0, 1.0, sg / jnp.maximum(softp, 1e-30)), 0.0)
    rate = -jnp.exp(alog)
    a = dt * rate
    sig_o[:, 256:384] = a
    sig_o[:, 0:128] = sg * rate
    sig_o[:, 128:256] = ratio
    tri = (iota((BLOCK, BLOCK), 0) >= iota((BLOCK, BLOCK), 1)).astype(F32)
    logdt = jnp.maximum(jnp.log(dt), LOGZERO)
    sub = iota((BLOCK, BLOCK), 0)
    ln = iota((BLOCK, BLOCK), 1)
    fwdb = ln < 64
    cum_s[...] = jnp.zeros_like(cum_s)
    dvals, ends = [], []
    for b in range(nb):
        blk = slice(b * BLOCK, (b + 1) * BLOCK)
        ab = a[blk, :]
        cum = mm(tri, ab, precision=HIGH)
        cx = cum - ab
        end = cum[BLOCK - 1 : BLOCK, :]
        colt = jnp.where(fwdb, cx, end - cum)
        rows = jnp.where(fwdb, logdt[blk, :] - cum, cx + logdt[blk, :] - end)
        tb_o[0, b] = colt.T
        tb_o[1, b] = rows.T
        ta_o[0, b] = jnp.minimum(rows + end, 60.0).T
        first_pos = off + b * BLOCK
        sp = seg_at(info, sub + first_pos)
        st = seg_at(info, ln + first_pos)
        before = seg_at(info, sub * 0 + (first_pos - 1))
        begin = seg_at(info, sub * 0 + first_pos)
        last = seg_at(info, sub * 0 + (first_pos + BLOCK - 1))
        after = seg_at(info, sub * 0 + (first_pos + BLOCK))
        enter = jnp.where(fwdb, (sp == before).astype(F32), (sp == after).astype(F32))
        keep = jnp.where(fwdb, (sp == last).astype(F32), (sp == begin).astype(F32))
        ce = cmap[blk, :] * enter
        bk = bmap[blk, :] * keep
        tb_o[3, b] = ce
        tc_o[1, b] = bk
        tc_o[2, b] = ce.T
        ta_o[1, b] = bk.T
        chain = jnp.where(fwdb[0:1, :], (last == before).astype(F32)[0:1, :], (begin == after).astype(F32)[0:1, :])
        dvals.append(jnp.exp(end) * chain)
        ends.append(end)
        cb = cmap[blk, :].astype(BF16)
        bb = bmap[blk, :].astype(BF16)
        zero = jnp.zeros_like(bb)
        same = sp == st
        low = same & (sub > ln)
        high = same & (sub < ln)
        bf = jnp.where(fwdb, bb, zero)
        br = jnp.where(fwdb, zero, bb)
        tb_o[2, b] = jnp.where(low, nt(cb, bf), jnp.where(high, nt(cb, br), 0.0))
        tc_o[0, b] = jnp.where(high, nt(bf, cb), jnp.where(low, nt(br, cb), 0.0))
    ones = jnp.ones((1, 128), F32)
    prefix, suffix = [ones], [ones]
    for b in range(nb):
        prefix.append(prefix[-1] * dvals[b])
        suffix.append(suffix[-1] * dvals[nb - 1 - b])
    suffix = suffix[::-1]
    f1 = fwdb[0:1, :]
    for b in range(nb):
        cum_s[b : b + 1, :] = dvals[b]
        cum_s[48 + b : 49 + b, :] = ends[b]
    for i in range(nb + 1):
        cum_s[16 + i : 17 + i, :] = jnp.where(f1, prefix[i], suffix[i])
        cum_s[32 + i : 33 + i, :] = jnp.where(f1, suffix[i], prefix[i])
    dpt_o[...] = cum_s[...].T
    send(sig_o, sig_h)
    send(tc_o, tc_h)
    for one in late:
        one.wait()


def pair_rows(dpt, j, base, i, half):
    lane = iota((1, 128), 1)
    one = dpt[pl.ds(half * 64 + 2 * j, 1), :][:, base + i : base + i + 1]
    two = dpt[pl.ds(half * 64 + 2 * j + 1, 1), :][:, base + i : base + i + 1]
    return jnp.where(lane < 64, one, two)


def assemble(dst, pieces):
    quarter = dst.shape[0] // 4
    q = lax.axis_index("wide") % 4
    cbit = q % 2
    xbit = q // 2
    places = (q, (1 - xbit) * 2 + cbit, xbit * 2 + 1 - cbit, (1 - xbit) * 2 + 1 - cbit)
    for place, piece in zip(places, pieces):
        dst[pl.ds(pl.multiple_of(place * quarter, quarter), quarter), :] = piece[...]


def vals_kernel(length, other, info, normed, *refs):
    nb = length // BLOCK
    ext = length + 2 * HALO
    step = pl.program_id(0)
    first = step
    if other:
        p0, p1, p2, p3, taps, ta, dpt = refs[:7]
        xc_o, vm_o, ds_o, s_o, bnd_o, wvo_o, vm_a, vm_b, seg_s = refs[11:]
        first = step + pl.num_programs(0)

        @pl.when(step == 0)
        def _():
            assemble(wvo_o, (p0, p1, p2, p3))

        wv = wvo_o[pl.ds(pl.multiple_of(step * 256, 256), 256), :]
    else:
        w_ref, taps, ta, dpt, xc_o, vm_o, ds_o, s_o, bnd_o, vm_a, vm_b, seg_s = refs
        wv = jnp.concatenate([w_ref[h, HD : 2 * HD, :] for h in range(4)], axis=0)
    off, count = info[5], info[4]

    @pl.when(step == 0)
    def _():
        seg_s[...] = seg_at(info, iota((ext, 128), 0) + (off - HALO))

    live = iota((ext, 128), 0) + (off - HALO) < count
    both = nt(normed[...], wv)
    lane = iota((BLOCK, 128), 1)
    top = iota((BLOCK, 128), 0) < 64
    for p, vm_s in enumerate((vm_a, vm_b)):
        j = 2 * first + p
        here = slice(128 * p, 128 * (p + 1))
        vm = jnp.where(live, both[:, here], 0.0)
        vm_s[...] = vm
        vm_o[:, here] = vm.astype(BF16)
        act, ds = silu_parts(conv_taps(vm_s, seg_s, taps[:, here], HALO, length))
        xc = act.astype(BF16)
        xc_o[:, here] = xc
        ds_o[:, here] = ds.astype(BF16)
        loc = []
        for b in range(nb):
            blk = slice(b * BLOCK, (b + 1) * BLOCK)
            got = []
            for i in range(2):
                h = 2 * j + i
                w = jnp.where(top, jnp.exp(ta[0, b, pl.ds(h, 1), :]), jnp.exp(ta[0, b, pl.ds(64 + h, 1), :]))
                got.append((ta[1, b] * w).astype(BF16))
            got = mm(jnp.concatenate(got, axis=0), xc[blk, :])
            loc.append(jnp.where(lane < 64, got[0:BLOCK, :], got[BLOCK:, :]))
        state = jnp.zeros((64, 128), F32)
        s_o[p, 0, 0:64, :] = state.astype(BF16)
        for b in range(nb):
            state = pair_rows(dpt, j, 0, b, 0) * state + loc[b][0:64, :]
            s_o[p, b + 1, 0:64, :] = state.astype(BF16)
        end_f = state
        state = jnp.zeros((64, 128), F32)
        s_o[p, nb, 64:128, :] = state.astype(BF16)
        for b in range(nb - 1, -1, -1):
            state = pair_rows(dpt, j, 0, b, 1) * state + loc[b][64:128, :]
            s_o[p, b, 64:128, :] = state.astype(BF16)
        bnd_o[p] = jnp.where(info[7] == 0, end_f, state).astype(BF16)


def scan_kernel(length, first_pair, info, xc_ref, s_ref, s0_ref, dpt, tb, skip, *refs):
    nb = length // BLOCK
    y_o, st_o = refs[-2:]
    j = pl.program_id(0) + first_pair
    right = (info[7] == 1).astype(F32)
    s0 = s0_ref[0].astype(F32)
    lane = iota((BLOCK, 128), 1)
    first = lane < 64
    low = iota((BLOCK, BLOCK), 0) > lane
    base = row_base(2, [[(0, 128), (256, 320)], [(128, 256), (320, 384)]])
    for i in range(nb + 1):
        f = s_ref[0, i, 0:64, :].astype(F32) + pair_rows(dpt, j, 16, i, 0) * (s0 * right)
        r = s_ref[0, i, 64:128, :].astype(F32) + pair_rows(dpt, j, 16, i, 1) * (s0 * (1.0 - right))
        st_o[0, i, 0:64, :] = f.astype(BF16)
        st_o[0, i, 64:128, :] = r.astype(BF16)
    for b in range(nb):
        blk = slice(b * BLOCK, (b + 1) * BLOCK)
        xb = xc_ref[blk, :]
        rhs = jnp.concatenate([xb, st_o[0, b, 0:64, :], st_o[0, b + 1, 64:128, :]], axis=0)
        got = []
        for i in range(2):
            h = 2 * j + i
            terms = column_terms([tb[0, b, pl.ds(h, 1), :], tb[0, b, pl.ds(64 + h, 1), :]])
            expo = tn(terms, row_terms(2, base, tb[1, b, pl.ds(h, 1), :], tb[1, b, pl.ds(64 + h, 1), :]))
            diff = jnp.where(low, expo[:, 0:128], expo[:, 128:256])
            mix = jnp.exp(jnp.minimum(diff, 60.0)) * tb[2, b]
            ct = tb[3, b] * jnp.exp(expo[:, 256:])
            lhs = jnp.concatenate([mix.astype(BF16), ct.astype(BF16)], axis=1)
            got.append(lhs)
        got = mm(jnp.concatenate(got, axis=0), rhs)
        y = jnp.where(first, got[0:BLOCK, :], got[BLOCK:, :]) + skip[0:1, :] * xb.astype(F32)
        y_o[blk, :] = y.astype(BF16)


def by_core(v, keep, send):
    share = v.shape[0] // 16
    cbit = lax.axis_index("wide") % 2
    v = v.astype(BF16).reshape(8, 2, share, v.shape[1])
    keep[...] = jnp.where(cbit == 0, v[:, 0], v[:, 1]).reshape(8 * share, v.shape[3])
    send[...] = jnp.where(cbit == 0, v[:, 1], v[:, 0]).reshape(8 * share, v.shape[3])


def gate_kernel(
    tiles, x_ref, g_ref, normed, y_ref, wout_a, w_ref, p0, p1, p2, p3, gain,
    out_h, gy_o, keep_h, send_h, ggate_h, ggain_o, wgo_h, hn_s, other_s, gated_s, act_s, dact_s, ghn_s,
    out_o, keep_o, send_o, ggate_o, sems,
):
    late = []

    def send(src, dst):
        late.append(pltpu.make_async_copy(src, dst, sems.at[len(late)]))
        late[-1].start()

    dm = x_ref.shape[1]
    chans = y_ref.shape[1]
    half = chans // 2
    step = 256
    assemble(other_s, (p0, p1, p2, p3))
    send(other_s.at[:, dm:], wgo_h)
    ggain_o[...] = jnp.zeros_like(ggain_o)

    @pl.loop(0, tiles)
    def _(i):
        start = pl.multiple_of(i * BLOCK, BLOCK)
        rows = pl.ds(start, BLOCK)
        nrows = normed[pl.ds(pl.multiple_of(start + HALO, HALO), BLOCK), :]
        squares = jnp.zeros((BLOCK, 128), F32)
        for lo in range(0, chans, step):
            if lo < half:
                heads = range(lo // HD, (lo + step) // HD)
                wg = jnp.concatenate([w_ref[h, 0:HD, :] for h in heads], axis=0)
            else:
                wg = other_s[lo - half : lo - half + step, dm:]
            gates = nt(nrows, wg)
            for at in range(0, step, 128):
                cols = slice(lo + at, lo + at + 128)
                act, dact = silu_parts(gates[:, at : at + 128])
                gated = y_ref[rows, cols].astype(F32) * act
                squares = squares + gated * gated
                gated_s[:, cols] = gated
                act_s[:, cols] = act
                dact_s[:, cols] = dact
        inv = lax.rsqrt(jnp.sum(squares, axis=1, keepdims=True) * (1.0 / chans) + EPS)
        inv = jnp.broadcast_to(inv, (BLOCK, 128))
        g = g_ref[rows, :]
        across = jnp.zeros((BLOCK, 128), F32)
        for lo in range(0, chans, step):
            wo = wout_a[lo : lo + step, :] if lo < half else other_s[lo - half : lo - half + step, 0:dm]
            ghns = nt(g, wo)
            for at in range(0, step, 128):
                cols = slice(lo + at, lo + at + 128)
                gainv = gain[0:1, cols]
                gated = gated_s[:, cols]
                nrm = gated * inv
                hn_s[rows, cols] = (nrm * gainv).astype(BF16)
                ghn = ghns[:, at : at + 128]
                ggain_o[0:1, cols] += jnp.sum(ghn * nrm, axis=0, keepdims=True)
                wgt = ghn * gainv
                ghn_s[:, cols] = wgt
                across = across + wgt * gated
        cross = jnp.sum(across, axis=1, keepdims=True) * (1.0 / chans)
        cross = jnp.broadcast_to(cross, (BLOCK, 128)) * (inv * inv * inv)
        hn = hn_s[rows, :]
        branch = mm(hn[:, 0:half], wout_a[...]) + mm(hn[:, half:], other_s[:, 0:dm])
        out_o[rows, :] = (x_ref[rows, :].astype(F32) + branch).astype(BF16)
        for lo in range(0, chans, 128):
            cols = slice(lo, lo + 128)
            ggated = inv * ghn_s[:, cols] - gated_s[:, cols] * cross
            gy_o[rows, cols] = (ggated * act_s[:, cols]).astype(BF16)
            ggate_o[rows, cols] = (ggated * y_ref[rows, cols].astype(F32) * dact_s[:, cols]).astype(BF16)

    send(out_o, out_h)
    send(ggate_o, ggate_h)
    length = g_ref.shape[0]
    gt = g_ref[...].T
    nt_ = normed[HALO : HALO + length, :].T
    for k in range(2):
        for p in range(half // 256):
            cols = slice(k * half + p * 256, k * half + (p + 1) * 256)
            dst = slice(p * 256, (p + 1) * 256)
            dst2 = slice(half + p * 256, half + (p + 1) * 256)
            by_core(mm(gt, hn_s[:, cols]), keep_o.at[k, :, dst], send_o.at[k, :, dst])
            by_core(mm(nt_, ggate_o[:, cols]), keep_o.at[k, :, dst2], send_o.at[k, :, dst2])
        send(send_o.at[k], send_h.at[k])
        send(keep_o.at[k], keep_h.at[k])
    for one in late:
        one.wait()


def gstate_kernel(length, first_pair, info, gy_ref, coltt, cet, dpt, *refs):
    nb = length // BLOCK
    gs_o, bnd_o = refs[-2:]
    j = pl.program_id(0) + first_pair
    lane = iota((BLOCK, 128), 1)
    top = iota((BLOCK, 128), 0) < 64
    loc = []
    for b in range(nb):
        blk = slice(b * BLOCK, (b + 1) * BLOCK)
        gy = gy_ref[blk, :]
        got = []
        for i in range(2):
            h = 2 * j + i
            e = jnp.where(top, jnp.exp(coltt[b, pl.ds(h, 1), :]), jnp.exp(coltt[b, pl.ds(64 + h, 1), :]))
            got.append((cet[b] * e).astype(BF16))
        got = mm(jnp.concatenate(got, axis=0), gy)
        loc.append(jnp.where(lane < 64, got[0:BLOCK, :], got[BLOCK:, :]))
    state = jnp.zeros((64, 128), F32)
    gs_o[0, nb, 0:64, :] = state.astype(BF16)
    for b in range(nb - 1, -1, -1):
        state = pair_rows(dpt, j, 0, b, 0) * state + loc[b][0:64, :]
        gs_o[0, b, 0:64, :] = state.astype(BF16)
    end_f = state
    state = jnp.zeros((64, 128), F32)
    gs_o[0, 0, 64:128, :] = state.astype(BF16)
    for b in range(nb):
        state = pair_rows(dpt, j, 0, b, 1) * state + loc[b][64:128, :]
        gs_o[0, b + 1, 64:128, :] = state.astype(BF16)
    bnd_o[0] = jnp.where(info[7] == 1, end_f, state).astype(BF16)


def gscan_kernel(
    length, first_pair, info, xc_ref, ds_ref, gy_ref, st_ref, gs_ref, gs0_ref, dpt, rowst, wt, coltt, tc, skip,
    *refs,
):
    nb = length // BLOCK
    gmix_o, ggt_o, gb_o, gct_o, k_o, r_o, phi_o, gskip_o, edge_o, gst_s = refs[-10:]
    step = pl.program_id(0)
    j = step + first_pair
    right = (info[7] == 1).astype(F32)
    s0 = gs0_ref[0].astype(F32)
    sub = iota((BLOCK, BLOCK), 0)
    lane = iota((BLOCK, 128), 1)
    first = lane < 64
    later = lane > sub
    top = sub < 64

    @pl.when(step == 0)
    def _():
        for k, acc in enumerate((ggt_o, gb_o, gct_o, k_o, r_o)):
            acc[...] = jnp.zeros_like(acc) if first_pair else refs[3 + k][...]

    base = row_base(4, [[(0, 128)], [(128, 256)], [(256, 320)], [(320, 384)]])

    phi_o[...] = jnp.zeros_like(phi_o)
    for i in range(nb + 1):
        f = gs_ref[0, i, 0:64, :].astype(F32) + pair_rows(dpt, j, 32, i, 0) * (s0 * (1.0 - right))
        r = gs_ref[0, i, 64:128, :].astype(F32) + pair_rows(dpt, j, 32, i, 1) * (s0 * right)
        f = f.astype(BF16)
        r = r.astype(BF16)
        gst_s[i, 0:64, :] = f
        gst_s[i, 64:128, :] = r
        if i > 0:
            phi_o[i - 1 : i, :] = jnp.sum(f.astype(F32) * st_ref[0, i, 0:64, :].astype(F32), axis=0, keepdims=True)
        if i < nb:
            phi_o[8 + i : 9 + i, :] = jnp.sum(
                r.astype(F32) * st_ref[0, i, 64:128, :].astype(F32), axis=0, keepdims=True
            )
    gskip = jnp.zeros((1, 128), F32)
    for b in range(nb):
        blk = slice(b * BLOCK, (b + 1) * BLOCK)
        xb = xc_ref[blk, :]
        gy = gy_ref[blk, :]
        gyf = gy.astype(F32)
        gskip = gskip + jnp.sum(gyf * xb.astype(F32), axis=0, keepdims=True)
        rhs = jnp.concatenate([gy, gst_s[b + 1, 0:64, :], gst_s[b, 64:128, :]], axis=0)
        left = jnp.concatenate([xb, st_ref[0, b, 0:64, :], st_ref[0, b + 1, 64:128, :]], axis=0)
        first2 = iota((2 * BLOCK, 128), 1) < 64
        none = jnp.zeros_like(left)
        big2 = nt(jnp.concatenate([jnp.where(first2, left, none), jnp.where(first2, none, left)], axis=0), rhs)
        got = []
        sum_ge, sum_gct, sum_gb, kparts = [], [], [], []
        for i in range(2):
            h = 2 * j + i
            terms = column_terms([v[b, pl.ds(at + h, 1), :] for v in (rowst, wt) for at in (0, 64)])
            expo = tn(terms, row_terms(4, base, coltt[b, pl.ds(h, 1), :], coltt[b, pl.ds(64 + h, 1), :]))
            diff = jnp.where(later, expo[:, 0:128], expo[:, 128:256])
            et_m = jnp.exp(jnp.minimum(diff, 60.0))
            mt = et_m * tc[0, b]
            w = jnp.exp(expo[:, 256:])
            bt = tc[1, b] * w
            big = big2[2 * BLOCK * i : 2 * BLOCK * (i + 1), :]
            gmt = big[0:BLOCK, 0:BLOCK]
            gbt = big[0:BLOCK, BLOCK:]
            gctt = big[BLOCK:, 0:BLOCK]
            ge = gmt * et_m
            sum_ge.append(ge)
            q = gmt * mt
            qf = jnp.where(later, q, 0.0)
            e = jnp.where(top, jnp.exp(coltt[b, pl.ds(h, 1), :]), jnp.exp(coltt[b, pl.ds(64 + h, 1), :]))
            gce = gctt * e
            sum_gct.append(gce)
            ct = gce * tc[2, b]
            rf = jnp.sum(qf, axis=0, keepdims=True)
            rall = jnp.sum(q, axis=0, keepdims=True)
            r_o[b, pl.ds(h, 1), :] = rf + jnp.sum(ct[0:64, :], axis=0, keepdims=True)
            r_o[b, pl.ds(64 + h, 1), :] = rall - rf + jnp.sum(ct[64:128, :], axis=0, keepdims=True)
            gbw = gbt * w
            sum_gb.append(gbw)
            u = gbw * tc[1, b]
            kf = jnp.sum(qf + jnp.where(first, u, 0.0), axis=1, keepdims=True)
            kb = jnp.sum(q + u, axis=1, keepdims=True) - kf
            kparts += [kf, kb]
            lhs = jnp.concatenate([mt.astype(BF16), bt.astype(BF16)], axis=1)
            got.append(lhs)
        ggt_o[b] += sum_ge[0] + sum_ge[1]
        gct_o[b] += sum_gct[0] + sum_gct[1]
        gb_o[b] += sum_gb[0] + sum_gb[1]
        two = jnp.where(lane % 64 == 0, jnp.where(first, kparts[0], kparts[1]), jnp.where(first, kparts[2], kparts[3]))
        k_o[blk, :] += pltpu.roll(jnp.where(lane % 64 < 2, two, 0.0), 2 * j, 1)
        got = mm(jnp.concatenate(got, axis=0), rhs)
        gx = jnp.where(first, got[0:BLOCK, :], got[BLOCK:, :]) + skip[0:1, :] * gyf
        gmix = (gx * ds_ref[blk, :].astype(F32)).astype(BF16)
        gmix_o[blk, :] = gmix
        if b == 0:
            edge_o[...] = gmix[0:HALO, :]
        if b == nb - 1:
            edge_o[...] = jnp.where(info[7] == 0, gmix[BLOCK - HALO :, :], edge_o[...])
    gskip_o[...] = jnp.broadcast_to(gskip, (8, 128))


def join_kernel(
    length, heads, info, ggt, gb, gct, k_ref, r_ref, phi, maps, dsl, sig,
    gmb_o, gv_o, small_o, edge_o, gc_s, gm_s,
):
    nb = length // BLOCK
    off = info[5]
    chans = phi.shape[1]
    sub = iota((BLOCK, BLOCK), 0)
    lane = iota((BLOCK, 128), 1)
    first = lane < 64
    low = sub > lane
    high = sub < lane
    upper_strict = high.astype(F32)
    upper = (sub <= lane).astype(F32)
    lower_strict = low.astype(F32)
    lower = (sub >= lane).astype(F32)
    owner = iota((chans, 128), 0) // 64
    to_f = (owner == iota((chans, 128), 1)).astype(F32)
    to_b = (owner + 64 == iota((chans, 128), 1)).astype(F32)
    phi_f = mm(phi[0:8, :], to_f, precision=HIGH)
    phi_b = mm(phi[8:16, :], to_b, precision=HIGH)
    gc_s[...] = jnp.zeros_like(gc_s)
    gm_s[...] = jnp.zeros_like(gm_s)
    sum_bias = jnp.zeros((1, 128), F32)
    sum_rate = jnp.zeros((1, 128), F32)
    for b in range(nb):
        blk = slice(b * BLOCK, (b + 1) * BLOCK)
        ext = slice(HALO + b * BLOCK, HALO + (b + 1) * BLOCK)
        first_pos = off + b * BLOCK
        sp = seg_at(info, sub + first_pos)
        st = seg_at(info, lane + first_pos)
        before = seg_at(info, sub * 0 + (first_pos - 1))
        begin = seg_at(info, sub * 0 + first_pos)
        last = seg_at(info, sub * 0 + (first_pos + BLOCK - 1))
        after = seg_at(info, sub * 0 + (first_pos + BLOCK))
        enter = jnp.where(first, (sp == before).astype(F32), (sp == after).astype(F32))
        keep = jnp.where(first, (sp == last).astype(F32), (sp == begin).astype(F32))
        same = sp == st
        gg = ggt[b]
        gf = jnp.where(same & high, gg, 0.0).astype(BF16)
        gr = jnp.where(same & low, gg, 0.0).astype(BF16)
        cm = maps[blk, 128:256]
        bm = maps[blk, 0:128]
        gm_s[ext, 0:128] = jnp.where(first, mm(gf, cm), mm(gr, cm)) + gb[b] * keep
        gc_s[ext, :] = jnp.where(first, tn(gf, bm), tn(gr, bm)) + gct[b].T * enter
        kb = k_ref[blk, :]
        rb = r_ref[b].T
        ga_f = mm(upper_strict, rb, precision=HIGH) - mm(upper, kb, precision=HIGH) + phi_f[b : b + 1, :]
        ga_b = mm(lower_strict, rb, precision=HIGH) - mm(lower, kb, precision=HIGH) + phi_b[b : b + 1, :]
        ga = jnp.where(first, ga_f, ga_b)
        gv = kb * sig[blk, 128:256] + ga * sig[blk, 0:128]
        gv_o[blk, :] = gv.astype(BF16)
        sum_bias = sum_bias + jnp.sum(gv, axis=0, keepdims=True)
        sum_rate = sum_rate + jnp.sum(ga * sig[blk, 256:384], axis=0, keepdims=True)
    small_o[...] = jnp.zeros_like(small_o)
    small_o[0:1, :] = sum_bias
    small_o[1:2, :] = sum_rate
    small_o[8:9, :] = pltpu.roll(sum_bias, 128 - heads // 2, 1)
    small_o[9:10, :] = pltpu.roll(sum_rate, 128 - heads // 2, 1)
    mid = length + HALO
    lo = HALO // 2
    pos = iota((mid, 128), 0) + (off - HALO + lo)
    seg0 = seg_at(info, pos)
    segn = seg_at(info, pos + 1)
    segp = seg_at(info, pos - 1)
    from_next = jnp.where(seg0 == segn, gc_s[lo + 1 : lo + 1 + mid, :], 0.0)
    from_prev = jnp.where(seg0 == segp, gc_s[lo - 1 : lo - 1 + mid, :], 0.0)
    gm_s[lo : lo + mid, 128:256] = jnp.where(iota((mid, 128), 1) < 64, from_next, from_prev)
    gmb_o[...] = gm_s[...] * dsl[...]
    lo = HALO // 2
    edge_o[...] = jnp.where(
        info[7] == 0, gmb_o[length + lo : length + lo + HALO, :], gmb_o[lo : lo + HALO, :]
    )


def back_conv(length, seg_s, live, grad, data, tap):
    own = slice(HALO, HALO + length)
    seg0 = seg_s[own, :]
    mine = grad[own, :]
    total = mine * tap[3:4, :]
    gtap = [None] * 7
    gtap[3] = jnp.sum(mine * data[own, :], axis=0, keepdims=True)
    for k in (0, 1, 2, 4, 5, 6):
        lo = HALO + 3 - k
        same = seg_s[lo : lo + length, :] == seg0
        total = total + jnp.where(same, grad[lo : lo + length, :], 0.0) * tap[k : k + 1, :]
        up = HALO + k - 3
        same = seg_s[up : up + length, :] == seg0
        gtap[k] = jnp.sum(jnp.where(same, data[up : up + length, :], 0.0) * mine, axis=0, keepdims=True)
    return jnp.where(live, total, 0.0), gtap


def back_kernel(
    length, steps, info, gmix, edge_a, edge_b, vm, normed, taps, ggain, gskip,
    gvals_o, keep_o, send_o, tiny_o, ext_s, vm_s, seg_s, turned_s,
):
    ext = length + 2 * HALO
    off, count = info[5], info[4]
    own = slice(HALO, HALO + length)
    seg_s[...] = seg_at(info, iota((ext, 128), 0) + (off - HALO))
    tiny_o[...] = jnp.zeros_like(tiny_o)
    turned_s[...] = normed[own, :].T
    live = iota((length, 128), 0) + off < count
    right = info[7] == 1
    per = steps // 2

    @pl.loop(0, steps)
    def _(j):
        near = j < per
        half = j // per
        at = (j % per) * 256
        both = []
        for p in range(2):
            here = pl.ds(pl.multiple_of(at + 128 * p, 128), 128)
            cols = pl.ds(pl.multiple_of(j * 256 + 128 * p, 128), 128)
            ext_s[own, :] = gmix[:, cols].astype(F32)
            halo = jnp.where(near, edge_a[:, here].astype(F32), edge_b[:, here].astype(F32))
            ext_s[0:HALO, :] = jnp.where(right, halo, 0.0)
            ext_s[HALO + length : ext, :] = jnp.where(right, 0.0, halo)
            vm_s[...] = vm[:, cols].astype(F32)
            gvals, gtap = back_conv(length, seg_s, live, ext_s, vm_s, taps[:, cols])
            both.append(gvals.astype(BF16))
            for t in range(7):
                tiny_o[half, t : t + 1, here] = gtap[t]
            tiny_o[half, 7:8, here] = ggain[0:1, cols]
            tiny_o[half, 8:9, here] = gskip[0:1, cols]
        both = jnp.concatenate(both, axis=1)
        gvals_o[:, pl.ds(pl.multiple_of(j * 256, 256), 256)] = both
        here = pl.ds(pl.multiple_of(at, 256), 256)
        by_core(mm(turned_s[...], both), keep_o.at[half, :, here], send_o.at[half, :, here])


def last_kernel(
    length, hl, info, gvals, ggate, w_ref, wv_b, wg_b, normed, gmb, edge, bcm, taps_bc, gv, wdt, wbc, x_ref, g_ref, rs, pre,
    small, tiny, keep_o, send_o, tiny_o, gin_o, ext_s, vm_s, seg_s,
):
    ext = length + 2 * HALO
    ch = hl * HD
    off, count = info[5], info[4]
    own = slice(HALO, HALO + length)
    seg_s[...] = seg_at(info, iota((ext, 128), 0) + (off - HALO))
    live = iota((length, 128), 0) + off < count
    tiny_o[...] = tiny[...]
    for half in range(2):
        tiny_o[half, 10:11, 0:128] = small[8 * half : 8 * half + 1, :]
        tiny_o[half, 10:11, 128:256] = small[8 * half + 1 : 8 * half + 2, :]
    both = []
    for k in range(2):
        cols = slice(k * 128, (k + 1) * 128)
        ext_s[...] = gmb[:, cols]
        lo = HALO // 2
        hi = length + lo
        got = edge[:, cols]
        ext_s[lo : lo + HALO, :] += jnp.where(info[7] == 1, got, 0.0)
        ext_s[hi : hi + HALO, :] += jnp.where(info[7] == 1, 0.0, got)
        vm_s[...] = bcm[:, cols]
        gbc, gtap = back_conv(length, seg_s, live, ext_s, vm_s, taps_bc[:, cols])
        for t in range(7):
            at = (t % 3) * 256 + k * 128
            for half in range(2):
                tiny_o[half, 11 + t // 3 : 12 + t // 3, at : at + 128] = gtap[t]
        both.append(gbc.astype(BF16))
    gbc = jnp.concatenate(both + [gv[...]], axis=1)
    gw = tn(normed[own, :], gbc)
    by_core(gw, keep_o.at[0], send_o.at[0])
    turned = pltpu.roll(gw[:, 256:], 128 - hl, 1)
    by_core(jnp.concatenate([gw[:, 0:256], turned], axis=1), keep_o.at[1], send_o.at[1])
    wv_a = jnp.concatenate([w_ref[h, HD : 2 * HD, :] for h in range(hl)], axis=0)
    wg_a = jnp.concatenate([w_ref[h, 0:HD, :] for h in range(hl)], axis=0)
    gn = mm(gvals[:, 0:ch], wv_a) + mm(gvals[:, ch:], wv_b[...])
    gn = gn + mm(ggate[:, 0:ch], wg_a) + mm(ggate[:, ch:], wg_b[...])
    gn = gn + nt(gbc[:, 0:256], wbc[...]) + mm(gv[...], wdt[...])
    x = x_ref[...].astype(F32)
    r = rs[...]
    wp = gn * pre[...]
    mean = jnp.mean(wp * x, axis=1, keepdims=True)
    gin_o[...] = g_ref[...].astype(F32) + r * wp - x * (r * r * r * mean)
    gpre = jnp.sum(gn * x * r, axis=0, keepdims=True)
    for half in range(2):
        tiny_o[half, 9:10, 0 : gpre.shape[1]] = gpre


def finish_kernel(hl, tiny, total, wb, heads_o, wout_o, bc_o, conv_o, convbc_o, pre_o, bias_o, rate_o, skip_o, gain_o):
    ch = tiny.shape[1]
    w = lax.axis_index("wide")
    share = pre_o.shape[1]
    lanes = gain_o.shape[0]
    dm = total.shape[1] - ch
    for h in range(hl):
        cols = slice(h * HD, (h + 1) * HD)
        wout_o[h] = total[:, cols]
        heads_o[h, :, 0:HD] = total[:, dm + h * HD : dm + (h + 1) * HD]
        heads_o[h, :, HD : 2 * HD] = wb[:, cols]
        heads_o[h, :, 2 * HD : 2 * HD + 1] = wb[:, ch + 256 + h : ch + 257 + h]
        heads_o[h, :, 2 * HD + 1 :] = wb[:, ch + 320 + h : ch + 321 + h]
    bc_o[...] = pack_columns(wb[:, ch : ch + 256])
    rows = tiny[...]
    src = iota((ch, 128), 0)
    dst = iota((ch, 128), 1)
    for q in range(lanes):
        chosen = ((src == dst * HD + lanes * w + q) & (dst < hl)).astype(F32)
        got = mm(rows, chosen, precision=HIGH)
        for k in range(7):
            conv_o[k, q : q + 1, :] = got[k : k + 1, 0:hl]
        gain_o[q : q + 1, :] = got[7:8, 0:hl]
    chosen = ((src == share * w + dst) & (dst < share)).astype(F32)
    pre_o[...] = mm(rows[8:16, :], chosen, precision=HIGH)[1:2, 0:share]
    per = (src // HD == dst).astype(F32)
    skip_o[...] = mm(rows[8:16, :], per, precision=HIGH)[0:1, 0:hl]
    size = convbc_o.shape[1]
    group = (size * w) // 64
    start = ((group % 2) * 2 + group // 2) * 64 + (size * w) % 64
    src = iota((256, 128), 0)
    dst = iota((256, 128), 1)
    chosen = ((src == start + dst) & (dst < size)).astype(F32)
    for k in range(3):
        part = mm(rows[8:16, 256 * k : 256 * (k + 1)], chosen, precision=HIGH)
        for r in range(3):
            if 3 * r + k < 7:
                convbc_o[3 * r + k : 3 * r + k + 1, :] = part[3 + r : 4 + r, 0:size]
    both = rows[10:11, 0:128]
    bias_o[0:1, :] = both[:, 0:hl]
    bias_o[1:2, :] = pltpu.roll(both, 64, 1)[:, 0:hl]
    rate = rows[10:11, 128:256]
    rate_o[...] = (rate + pltpu.roll(rate, 64, 1))[:, 0:hl]


def collect_kernel(
    keep, got_v, keep_bc, send_bc, tiny, plane_a, out_o, tiny_o, a_o,
    core_s, left_s, right_s, left_out, left_in, right_out, right_in, left2_out, left2_in, right2_out, right2_in,
    zsend_s, zgot_s, tcore_s, tsum_s, tgot_s, tz_s, tzgot_s, agot_s,
    core_sem, one_sem, two_sem, tiny_sem, z_sem, core_rem, one_rem, two_rem, tiny_rem, z_rem,
):
    w = lax.axis_index("wide")
    n = lax.axis_index("narrow")
    c, xx, z = w % 2, (w // 2) % 2, w // 4
    share, cols = out_o.shape
    chv = keep.shape[2]
    cut = left_s.shape[3]
    core = (w + 1 - 2 * c, n)
    over_x = (w + 2 - 4 * xx, n)
    over_y = (w, 1 - n)
    over_d = (w + 2 - 4 * xx, 1 - n)
    steps = (2, 1, 3)
    over_z = [(((z + d) % 4) * 4 + w % 4, n) for d in steps]
    mesh_ids = pl.DeviceIdType.MESH
    barrier = pltpu.get_barrier_semaphore()
    for other in [core, over_x, over_y, over_d] + over_z:
        pl.semaphore_signal(barrier, inc=1, device_id=other, device_id_type=mesh_ids)
    pl.semaphore_wait(barrier, 7)

    def copy(src, dst, out_sem, in_sem, other):
        got = pltpu.make_async_remote_copy(
            src_ref=src, dst_ref=dst, send_sem=out_sem, recv_sem=in_sem, device_id=other, device_id_type=mesh_ids
        )
        got.start()
        return got

    rows = [pl.ds(pl.multiple_of(((z + d) % 4) * (2 * share), 2 * share), 2 * share) for d in steps + (0,)]
    first = [copy(tiny, tcore_s, core_sem.at[4], core_rem.at[4], core)]
    for i in range(4):
        first.append(copy(send_bc.at[:, rows[i], :], core_s.at[i], core_sem.at[i], core_rem.at[i], core))
    a_copies = [
        copy(plane_a.at[(z + steps[k]) % 4], agot_s.at[k], z_sem.at[2, k], z_rem.at[2, k], over_z[k]) for k in range(3)
    ]
    first[0].wait()
    tsum_s[...] = tiny[...] + tcore_s[...]
    small = []
    for k, other in enumerate((over_x, over_y, over_d)):
        half = 0 if k == 0 else 1
        small.append(copy(tsum_s.at[half], tgot_s.at[k], tiny_sem.at[k], tiny_rem.at[k], other))
    second = []
    for i in range(4):
        first[i + 1].wait()
        both = jnp.concatenate(
            [
                keep[:, rows[i], :].astype(F32) + got_v[:, rows[i], :].astype(F32),
                keep_bc[:, rows[i], :].astype(F32) + core_s[i].astype(F32),
            ],
            axis=2,
        )
        low, high = both[:, 0:share, :], both[:, share:, :]
        near = jnp.where(xx == 0, low, high)
        far = jnp.where(xx == 0, high, low)
        left_s[i] = near[:, :, 0:cut]
        right_s[i, 0] = near[0, :, cut:]
        right_s[i, 1] = far[0, :, cut:]
        left_out[i] = far[:, :, 0:cut].astype(BF16)
        right_out[i, 0] = near[1, :, cut:].astype(BF16)
        right_out[i, 1] = far[1, :, cut:].astype(BF16)
        second.append(
            (
                copy(left_out.at[i], left_in.at[i], one_sem.at[i, 0], one_rem.at[i, 0], over_x),
                copy(right_out.at[i], right_in.at[i], one_sem.at[i, 1], one_rem.at[i, 1], over_y),
            )
        )
    for one in small:
        one.wait()
    tsum = tsum_s[0] + tgot_s[0] + tgot_s[1] + tgot_s[2]
    tz_s[...] = tsum
    last = [copy(tz_s, tzgot_s.at[k], z_sem.at[1, k], z_rem.at[1, k], over_z[k]) for k in range(3)]
    third = []
    for i in range(4):
        second[i][0].wait()
        left_s[i] = left_s[i] + left_in[i].astype(F32)
        left2_out[i] = left_s[i, 1].astype(BF16)
        go_left = copy(left2_out.at[i], left2_in.at[i], two_sem.at[i, 0], two_rem.at[i, 0], over_y)
        second[i][1].wait()
        right_s[i] = right_s[i] + right_in[i].astype(F32)
        right2_out[i] = right_s[i, 1].astype(BF16)
        go_right = copy(right2_out.at[i], right2_in.at[i], two_sem.at[i, 1], two_rem.at[i, 1], over_x)
        third.append((go_left, go_right))
    for i in range(4):
        third[i][0].wait()
        third[i][1].wait()
        left = left_s[i, 0] + left2_in[i].astype(F32)
        right = right_s[i, 0] + right2_in[i].astype(F32)
        if i < 3:
            zsend_s[i, :, 0:cut] = left.astype(BF16)
            zsend_s[i, :, cut:] = right.astype(BF16)
            last.append(copy(zsend_s.at[i], zgot_s.at[i], z_sem.at[0, i], z_rem.at[0, i], over_z[i]))
        else:
            out_o[:, 0:cut] = left
            out_o[:, cut:] = right
    for one in a_copies:
        one.wait()
    a_o[...] = plane_a[z].astype(F32) + agot_s[0].astype(F32) + agot_s[1].astype(F32) + agot_s[2].astype(F32)
    for one in last:
        one.wait()
    out_o[...] = out_o[...] + zgot_s[0].astype(F32) + zgot_s[1].astype(F32) + zgot_s[2].astype(F32)
    tiny_o[...] = tsum + tzgot_s[0] + tzgot_s[1] + tzgot_s[2]


def whole(shape, grid):
    zeros = (0,) * len(shape)
    if grid:
        return pl.BlockSpec(shape, lambda j: zeros)
    return pl.BlockSpec(shape, lambda: zeros)


def columns(rows, first=0):
    return pl.BlockSpec((rows, 128), lambda j: (0, first + j))


SMEM = pl.BlockSpec(memory_space=pltpu.SMEM)
VMEM = pl.BlockSpec(memory_space=pltpu.VMEM)
ANY = pl.BlockSpec(memory_space=pl.ANY)
HBM = pl.BlockSpec(memory_space=pltpu.HBM)


def sds(shape, dtype):
    return jax.ShapeDtypeStruct(shape, dtype)


def params(grid, mib):
    if grid:
        return pltpu.CompilerParams(vmem_limit_bytes=mib * 2**20, dimension_semantics=("arbitrary",))
    return pltpu.CompilerParams(vmem_limit_bytes=mib * 2**20)


def cost(us):
    return pl.CostEstimate(flops=int(us * 1.1e9), bytes_accessed=int(us * 1e6), transcendentals=0)


def pack_columns(v):
    n = v.shape[-1] // 4
    return jnp.concatenate([v[..., 0:n], v[..., 2 * n : 3 * n], v[..., n : 2 * n], v[..., 3 * n :]], axis=-1)


def small_kernel(hl, conv, gain, dtb, alog, skip, wdt, start_ref, end_ref, out_o):
    ch = out_o.shape[1]
    lane = iota((1, 128), 1)
    wide_lane = iota((1, ch), 1)
    bias = jnp.zeros((1, 128), F32)
    rate = jnp.zeros((1, 128), F32)
    diag = jnp.zeros((1, ch), F32)
    out_o[0:16, :] = jnp.zeros((16, ch), F32)
    for h in range(hl):
        cols = slice(h * HD, (h + 1) * HD)
        out_o[0:7, cols] = conv[h]
        out_o[7:8, cols] = gain[h : h + 1, :]
        bias = jnp.where(lane == h, dtb[0, h], jnp.where(lane == 64 + h, dtb[1, h], bias))
        rate = jnp.where((lane == h) | (lane == 64 + h), alog[h], rate)
        diag = jnp.where(wide_lane // HD == h, skip[h], diag)
        out_o[16 + 2 * h : 18 + 2 * h, :] = wdt[h].astype(F32)[0:2, :]
    out_o[8:9, :] = diag
    out_o[9:10, 0:128] = bias
    out_o[9:10, 128:256] = rate
    n = lax.axis_index("narrow")
    start, end = start_ref[...].astype(F32), end_ref[...].astype(F32)
    out_o[16 + 2 * hl :, :] = jnp.where(n == 0, end[8:16, :], start[0:8, :])


def swap(v):
    return lax.ppermute(v, "narrow", [(0, 1), (1, 0)])


def flip(v, bit, wide):
    return lax.ppermute(v, "wide", [(i, i ^ bit) for i in range(wide)])


def cross(v, bit, wide):
    pairs = [(i * 2 + k, (i ^ bit) * 2 + 1 - k) for i in range(wide) for k in range(2)]
    return lax.ppermute(v, ("wide", "narrow"), pairs)


def total(*parts):
    acc = parts[0].astype(F32)
    for v in parts[1:]:
        acc = acc + v.astype(F32)
    return acc


def split_positions(
    wide, layer_in, pre_gain, w_heads, w_bc, conv_x, conv_bc, dt_bias, a_log, skip_d, norm_gain, w_out, cotangent, starts, live
):
    n = lax.axis_index("narrow")
    w = lax.axis_index("wide")
    left = n == 0
    _, length, dm = layer_in.shape
    hl = w_heads.shape[1]
    heads = 2 * hl
    ch = hl * HD
    chans = 2 * ch
    pairs = heads // 2
    hp = pairs // 2
    nb = length // BLOCK
    ext = length + 2 * HALO
    share = dm // wide
    x = layer_in[0]
    g = cotangent[0]
    xbit = (w // 2) % 2

    w_turned = jnp.transpose(w_heads, (1, 2, 0))
    small_own = pl.pallas_call(
        functools.partial(small_kernel, hl),
        grid=(1,),
        out_shape=sds((24 + 2 * hl, ch), F32),
        in_specs=[
            whole((hl, 7, HD), 1), whole((hl, HD), 1), SMEM, SMEM, SMEM, pl.BlockSpec((hl, 16, dm), lambda j: (0, 8, 0)),
            pl.BlockSpec((HALO, dm), lambda j: (0, 0)), pl.BlockSpec((HALO, dm), lambda j: (length // HALO - 1, 0)),
        ],
        out_specs=whole((24 + 2 * hl, ch), 1),
        cost_estimate=cost(2),
        name="small",
    )(jnp.transpose(conv_x, (1, 0, 2)), norm_gain, dt_bias.T, a_log, skip_d, w_turned, x, x)
    small_other = swap(small_own)

    quarter = ch // 4
    q = w % 4

    def gather(p0):
        p1 = flip(p0, 2, wide)
        return p0, p1, flip(p0, 1, wide), flip(p1, 1, wide)

    def heads_rows(lo):
        return lax.dynamic_slice(w_turned, (q * (hl // 4), lo, 0), (hl // 4, HD, dm)).reshape(quarter, dm)

    wo = w_out.reshape(ch, dm)
    wv_first = swap(heads_rows(HD))
    wo_rows = lax.dynamic_slice(wo, (q * quarter, 0), (quarter, dm))
    wog_pieces = gather(swap(jnp.concatenate([wo_rows, heads_rows(0)], axis=1)))

    pos = (length, 128)
    sq = (nb, BLOCK, BLOCK)
    front_shapes = [
        ((8, chans), F32), ((8, chans), F32), ((8, chans), F32), ((128, dm), BF16), ((dm, 256), BF16), ((7, 256), F32),
        ((ext, dm), BF16), ((length, 1), F32), ((ext, 256), F32), ((ext, 256), F32), ((length, 256), BF16),
        ((2,) + sq, F32), ((4,) + sq, F32), ((3,) + sq, F32), ((128, 128), F32), ((length, 384), F32),
    ]
    late_front = (8, 9, 10, 13, 15)
    (
        info, taps, gain, skip, wdt_all, wbc, taps_bc, normed, rs, bcm, dsl, maps, tab_a, tab_b, tab_c, dpt, sig,
    ) = pl.pallas_call(
        functools.partial(front_kernel, length, hl),
        out_shape=[sds((8,), jnp.int32)]
        + [pltpu.HBM(*v) if k in late_front else sds(*v) for k, v in enumerate(front_shapes)],
        in_specs=[SMEM] + [VMEM] * 7,
        out_specs=[SMEM] + [HBM if k in late_front else VMEM for k in range(len(front_shapes))],
        scratch_shapes=[
            pltpu.VMEM((ext, 256), jnp.int32), pltpu.VMEM((ext, 256), F32), pltpu.VMEM((128, 128), F32),
            pltpu.VMEM((ext, dm), BF16),
        ]
        + [pltpu.VMEM(*front_shapes[k]) for k in late_front]
        + [pltpu.SemaphoreType.DMA((len(late_front),))],
        compiler_params=params(False, 14),
        cost_estimate=cost(6),
        name="front",
    )(starts, live, x, pre_gain.reshape(1, dm), w_bc, conv_bc, small_own, small_other)

    wv_first, normed = lax.optimization_barrier((wv_first, normed))
    wv_over_x = flip(wv_first, 2, wide)

    def states(first):
        return pl.BlockSpec((1, nb + 1, 128, 128), lambda j: (j + first, 0, 0, 0))

    bnd_spec = pl.BlockSpec((1, 64, 128), lambda j: (j, 0, 0))
    state_shape = sds((pairs, nb + 1, 128, 128), BF16)
    bnd_shape = sds((hp, 64, 128), BF16)
    act_shape = sds((length, chans), BF16)
    def twin(rows, first):
        return pl.BlockSpec((rows, 256), lambda j: (0, first + j))

    def vals(other, weights, before):
        steps = hp // 2
        first = steps if other else 0
        specs = [SMEM, whole((ext, dm), 1)]
        specs += [whole((quarter, dm), 1)] * 4 if other else [pl.BlockSpec((4, 2 * HD + 2, dm), lambda j: (j, 0, 0))]
        specs += [twin(8, first), whole((2,) + sq, 1), whole((128, 128), 1)] + [ANY] * len(before)
        return pl.pallas_call(
            functools.partial(vals_kernel, length, other),
            grid=(steps,),
            out_shape=[act_shape, sds((ext, chans), BF16), act_shape, state_shape, bnd_shape] + [sds((ch, dm), BF16)] * other,
            in_specs=specs,
            out_specs=[
                twin(length, first), twin(ext, first), twin(length, first),
                pl.BlockSpec((2, nb + 1, 128, 128), lambda j: (j + first, 0, 0, 0)),
                pl.BlockSpec((2, 64, 128), lambda j: (j, 0, 0)),
            ] + [whole((ch, dm), 1)] * other,
            scratch_shapes=[pltpu.VMEM((ext, 128), F32), pltpu.VMEM((ext, 128), F32), pltpu.VMEM((ext, 128), jnp.int32)],
            input_output_aliases={len(specs) - len(before) + i: i for i in range(len(before))},
            compiler_params=params(True, 10),
            cost_estimate=cost(9),
            name="vals_other" if other else "vals_own",
        )(info, normed, *weights, taps, tab_a, dpt, *before)

    *own_vals, bnd_own = vals(False, (w_turned,), ())
    bnd_own, wv_over_x = lax.optimization_barrier((bnd_own, wv_over_x))
    wv_pieces = wv_first, wv_over_x, flip(wv_first, 1, wide), flip(wv_over_x, 1, wide)
    xc, vm, ds, s_loc, bnd_other, wv_other = vals(True, wv_pieces, own_vals)

    def aliases(specs, before):
        return {len(specs) - len(before) + i: i for i in range(len(before))}

    def scan(first, s0, before):
        specs = [
            SMEM, columns(length, first), states(first), bnd_spec, whole((128, 128), 1), whole((4,) + sq, 1), columns(8, first),
        ] + [ANY] * len(before)
        return pl.pallas_call(
            functools.partial(scan_kernel, length, first),
            grid=(hp,),
            out_shape=[act_shape, state_shape],
            in_specs=specs,
            out_specs=[columns(length, first), states(first)],
            input_output_aliases=aliases(specs, before),
            compiler_params=params(True, 5),
            cost_estimate=cost(10),
            name="scan_other" if first else "scan_own",
        )(info, xc, s_loc, s0, dpt, tab_b, skip, *before)

    y, s_true = scan(0, swap(bnd_other), scan(hp, swap(bnd_own), ()))

    gw_shape = (2, dm // 2, dm + ch)
    out, gy, keep_a, send_a, ggate, ggain, wg_other = pl.pallas_call(
        functools.partial(gate_kernel, nb),
        out_shape=[
            pltpu.HBM((length, dm), BF16), act_shape, pltpu.HBM(gw_shape, BF16), pltpu.HBM(gw_shape, BF16),
            pltpu.HBM((length, chans), BF16), sds((8, chans), F32), pltpu.HBM((ch, dm), BF16),
        ],
        in_specs=[VMEM] * 11,
        out_specs=[HBM, VMEM, HBM, HBM, HBM, VMEM, HBM],
        scratch_shapes=[pltpu.VMEM((length, chans), BF16), pltpu.VMEM((ch, 2 * dm), BF16)]
        + [pltpu.VMEM((BLOCK, chans), F32)] * 4
        + [pltpu.VMEM((length, dm), BF16), pltpu.VMEM(gw_shape, BF16), pltpu.VMEM(gw_shape, BF16)]
        + [pltpu.VMEM((length, chans), BF16), pltpu.SemaphoreType.DMA((7,))],
        compiler_params=params(False, 22),
        cost_estimate=cost(17),
        name="gated",
    )(x, g, normed, y, wo, w_turned, *wog_pieces, gain)

    def meet(keep, got):
        cols = keep.shape[-1]
        keep = keep.reshape(2, wide // 4, 2, share, cols)
        got = got.reshape(2, wide // 4, 2, share, cols)

        def piece(half, xx):
            def cut(v):
                return lax.dynamic_slice(v, (half, 0, xx, 0, 0), (1, wide // 4, 1, share, cols)).reshape(-1, share, cols)

            return total(cut(keep), cut(got)).astype(BF16)

        return piece(0, xbit), piece(0, 1 - xbit), piece(1, xbit), piece(1, 1 - xbit)

    def plane(mine, to_x, to_y, to_d):
        return total(mine, flip(to_x, 2, wide), swap(to_y), cross(to_d, 2, wide)).astype(mine.dtype)

    a_pieces = meet(keep_a, flip(send_a, 1, wide))

    def table(k):
        return pl.BlockSpec((None,) + sq, lambda j: (k, 0, 0, 0))

    def gstate(first, before):
        specs = [SMEM, columns(length, first), table(0), table(2), whole((128, 128), 1)] + [ANY] * len(before)
        return pl.pallas_call(
            functools.partial(gstate_kernel, length, first),
            grid=(hp,),
            out_shape=[state_shape, bnd_shape],
            in_specs=specs,
            out_specs=[states(first), bnd_spec],
            input_output_aliases=aliases(specs, before),
            compiler_params=params(True, 4),
            cost_estimate=cost(5),
            name="gstate_other" if first else "gstate_own",
        )(info, gy, tab_b, tab_c, dpt, *before)

    gs_loc, gbnd_own = gstate(0, ())
    gs_loc, gbnd_other = gstate(hp, (gs_loc,))

    gs_loc, gbnd_other, *a_pieces = lax.optimization_barrier((gs_loc, gbnd_other, *a_pieces))
    a_plane = plane(*a_pieces)

    def gscan(first, gs0, before):
        sums = [whole(sq, 1), whole(sq, 1), whole(sq, 1), whole(pos, 1), whole(sq, 1)]
        specs = [
            SMEM, columns(length, first), columns(length, first), columns(length, first), states(first), states(first),
            bnd_spec, whole((128, 128), 1), table(1), table(0), table(0), whole((3,) + sq, 1), columns(8, first),
        ]
        at = len(specs)
        if before:
            specs += [ANY] * 3 + sums
        return pl.pallas_call(
            functools.partial(gscan_kernel, length, first),
            grid=(hp,),
            out_shape=[
                act_shape, sds(sq, F32), sds(sq, F32), sds(sq, F32), sds(pos, F32), sds(sq, F32), sds((16, chans), F32),
                sds((8, chans), F32), sds((HALO, ch), BF16),
            ],
            in_specs=specs,
            out_specs=[columns(length, first)] + sums + [columns(16, first), columns(8, first), columns(HALO)],
            scratch_shapes=[pltpu.VMEM((nb + 1, 128, 128), BF16)],
            input_output_aliases={at: 0, at + 1: 6, at + 2: 7} if before else {},
            compiler_params=params(True, 7),
            cost_estimate=cost(17),
            name="gscan_other" if first else "gscan_own",
        )(info, xc, ds, gy, s_true, gs_loc, gs0, dpt, tab_b, tab_a, tab_b, tab_c, skip, *before)

    gmix, ggt, gb, gct, ksum, rsum, phi, gskip, edge_other = gscan(hp, swap(gbnd_own), ())
    gmix, ggt, gb, gct, ksum, rsum, phi, gskip, edge_own = gscan(
        0, swap(gbnd_other), (gmix, phi, gskip, ggt, gb, gct, ksum, rsum)
    )

    gmix, ggt, a_plane = lax.optimization_barrier((gmix, ggt, a_plane))

    gmb, gv, small, edge_bc = pl.pallas_call(
        functools.partial(join_kernel, length, heads),
        out_shape=[sds((ext, 256), F32), sds(pos, BF16), sds((16, 128), F32), sds((HALO, 256), F32)],
        in_specs=[SMEM] + [VMEM] * 9,
        out_specs=[VMEM] * 4,
        scratch_shapes=[pltpu.VMEM((ext, 128), F32), pltpu.VMEM((ext, 256), F32)],
        compiler_params=params(False, 6),
        cost_estimate=cost(6),
        name="join",
    )(info, ggt, gb, gct, ksum, rsum, phi, maps, dsl, sig)

    edge_a, edge_b = swap(edge_other), swap(edge_own)
    edge_bc = swap(edge_bc)
    sum_shape = (2, dm // 2, ch)
    gvals, keep_v, send_v, tiny = pl.pallas_call(
        functools.partial(back_kernel, length, pairs // 2),
        out_shape=[act_shape, sds(sum_shape, BF16), sds(sum_shape, BF16), sds((2, 16, ch), F32)],
        in_specs=[SMEM] + [VMEM] * 8,
        out_specs=[VMEM] * 4,
        scratch_shapes=[
            pltpu.VMEM((ext, 128), F32), pltpu.VMEM((ext, 128), F32), pltpu.VMEM((ext, 128), jnp.int32),
            pltpu.VMEM((dm, length), BF16),
        ],
        compiler_params=params(False, 10),
        cost_estimate=cost(12),
        name="back",
    )(info, gmix, edge_a, edge_b, vm, normed, taps, ggain, gskip)

    got_v = flip(send_v, 1, wide)
    keep_bc, send_bc, tiny, grad_in = pl.pallas_call(
        functools.partial(last_kernel, length, hl),
        out_shape=[
            sds((2, dm // 2, 384), BF16), sds((2, dm // 2, 384), BF16), sds((2, 16, ch), F32), sds((length, dm), F32),
        ],
        in_specs=[SMEM] + [VMEM] * 19,
        out_specs=[VMEM] * 4,
        scratch_shapes=[pltpu.VMEM((ext, 128), F32), pltpu.VMEM((ext, 128), F32), pltpu.VMEM((ext, 128), jnp.int32)],
        compiler_params=params(False, 12),
        cost_estimate=cost(8),
        name="last",
    )(
        info, gvals, ggate, w_turned, wv_other, wg_other, normed, gmb, edge_bc, bcm, taps_bc, gv, wdt_all, wbc, x, g, rs,
        pre_gain.reshape(1, dm), small, tiny,
    )

    cols = ch + 384
    cut = 5 * cols // 9
    rest = cols - cut
    wb, tiny, wa = pl.pallas_call(
        collect_kernel,
        out_shape=[sds((share, cols), F32), sds((16, ch), F32), sds((share, dm + ch), F32)],
        in_specs=[VMEM] * 6,
        out_specs=[VMEM] * 3,
        scratch_shapes=[
            pltpu.VMEM((4, 2, 2 * share, 384), BF16),
            pltpu.VMEM((4, 2, share, cut), F32),
            pltpu.VMEM((4, 2, share, rest), F32),
        ]
        + [pltpu.VMEM((4, 2, share, cut), BF16)] * 2
        + [pltpu.VMEM((4, 2, share, rest), BF16)] * 2
        + [pltpu.VMEM((4, share, cut), BF16)] * 2
        + [pltpu.VMEM((4, share, rest), BF16)] * 2
        + [
            pltpu.VMEM((3, share, cols), BF16),
            pltpu.VMEM((3, share, cols), BF16),
            pltpu.VMEM((2, 16, ch), F32),
            pltpu.VMEM((2, 16, ch), F32),
            pltpu.VMEM((3, 16, ch), F32),
            pltpu.VMEM((16, ch), F32),
            pltpu.VMEM((3, 16, ch), F32),
            pltpu.VMEM((3, share, dm + ch), BF16),
        ]
        + [pltpu.SemaphoreType.DMA(v) for v in ((5,), (4, 2), (4, 2), (3,), (3, 3)) * 2],
        compiler_params=pltpu.CompilerParams(collective_id=0, has_side_effects=True, vmem_limit_bytes=14 * 2**20),
        name="collect",
    )(keep_v, got_v, keep_bc, send_bc, tiny, a_plane)

    g_w_heads, g_w_out, g_w_bc, g_conv_x, g_conv_bc, g_pre, g_bias, g_rate, g_skip, g_gain = pl.pallas_call(
        functools.partial(finish_kernel, hl),
        out_shape=[
            sds((hl, share, 2 * HD + 2), F32), sds((hl, share, HD), F32), sds((share, 256), F32), sds((7, HD // wide, hl), F32),
            sds((7, 256 // wide), F32), sds((1, share), F32), sds((2, hl), F32), sds((1, hl), F32), sds((1, hl), F32),
            sds((HD // wide, hl), F32),
        ],
        in_specs=[VMEM] * 3,
        out_specs=[VMEM] * 10,
        compiler_params=params(False, 8),
        name="finish",
    )(tiny, wa, wb)
    return (
        out[None],
        grad_in[None],
        g_pre[0],
        jnp.transpose(g_w_heads, (1, 0, 2)),
        g_w_bc,
        jnp.transpose(g_conv_x, (0, 2, 1)),
        g_conv_bc,
        g_bias.T,
        g_rate[0],
        g_skip[0],
        g_gain.T,
        jnp.transpose(g_w_out, (0, 2, 1)),
    )


def solution(mesh):
    body = shards
    if mesh.shape["narrow"] == 2 and mesh.shape["wide"] == 16:
        body = functools.partial(split_positions, mesh.shape["wide"])
    return jax.shard_map(
        body,
        mesh=mesh,
        in_specs=(
            P("wide", "narrow", None),
            P(),
            P(None, "narrow", None),
            P(),
            P(None, "narrow", None),
            P(),
            P("narrow", None),
            P("narrow"),
            P("narrow"),
            P("narrow", None),
            P("narrow", None, None),
            P("wide", "narrow", None),
            P("wide", None),
            P("wide", None),
        ),
        out_specs=(
            P("wide", "narrow", None),
            P("wide", "narrow", None),
            P("wide"),
            P("wide", "narrow", None),
            P("wide", None),
            P(None, "narrow", "wide"),
            P(None, "wide"),
            P("narrow", None),
            P("narrow"),
            P("narrow"),
            P("narrow", "wide"),
            P("narrow", None, "wide"),
        ),
        check_vma=False,
    )
```

profile of v0, /device:TPU:0, one launch (start us, length us, event | category | flops | bytes accessed | tf_op | source)
XLA Modules:
  0.0 184.4 jit_solution(5281809256652694099)
XLA Ops:
  0.7 1.9 %small.1.small_a = f32[48,768]{1,0:T(8,128)} custom-call(f32[12,7,64]{2,1,0:T(8,128)} %bitcast.65, f32[12,64]{1,0:T(8,128)} %gain.1, f32[2,12]{1,0:T(2,128)} %bitcast.68, f32[12]{0:T(128)} %alog.1, f32[12]{0:T(128)} %skip.1, bf16[12,130,768]{2,1,0:T(8,128)(2,1)} %bitcast.48, bf16[640,768]{1,0:T(8,128)(2,1)} %bitcast.54, bf16[640,768]{1,0:T(8,128)(2,1)} %bitcast.55), custom_call_target="tpu_custom_call" | custom-call | flops 2200000000 | bytes 2000000 | tf_op jit(solution)/shard_map/small/pallas_call | solution.py:1244
  2.5 3.0 %collective-permute-start.1 = (f32[48,768]{1,0:T(8,128)}, f32[48,768]{1,0:T(8,128)}, u32[]{:S(2)}, u32[]{:S(2)}) collective-permute-start(f32[48,768]{1,0:T(8,128)} %small.1.small_a), channel_id=1, source_target_pairs={{0,1},{1,0},{2,3},{3,2},{4,5},{5,4},{6,7},{7,6},{8,9},{9,8},{10,11... | collective-permute-start | bytes 442376 | tf_op jit(solution)/shard_map/ppermute | solution.py:1204
  5.5 0.9 constant_dynamic-slice_fusion
  6.4 0.0 copy-start.9
  6.4 0.1 collective-permute-start
  6.5 0.0 copy-start.5
  6.5 0.0 copy-start.6
  6.5 1.1 constant_dynamic-slice_fusion.1
  7.6 1.0 pad_maximum_fusion
  8.6 2.0 %collective-permute-start.7 = (bf16[192,1536]{1,0:T(8,128)(2,1)S(1)}, bf16[192,1536]{1,0:T(8,128)(2,1)S(1)}, u32[]{:S(2)}, u32[]{:S(2)}) collective-permute-start(bf16[192,1536]{1,0:T(8,128)(2,1)S(1)} %pad_maximum_fusion), channel_id=1, source_target_pairs={{0,1},{1,0},{2,3},{3,2},{4,5},{5,4},{6,7},{7,6},{8,9},{9,8},{10,11... | collective-permute-start | bytes 1769480 | tf_op jit(solution)/shard_map/ppermute | solution.py:1204
  10.6 7.1 %front.1 = (s32[8]{0:T(128)S(1)}, f32[8,1536]{1,0:T(8,128)S(1)}, f32[8,1536]{1,0:T(8,128)S(1)}, f32[8,1536]{1,0:T(8,128)S(1)}, bf16[128,768]{1,0:T(8,128)(2,1)S(...) custom-call(s32[1,4]{1,0:T(1,128)S(1)} %copy-done.9, ...), custom_call_target="tpu_custom_call" | custom-call | flops 6600000000 | bytes 6000000 | tf_op jit(solution)/shard_map/front/pallas_call | solution.py:1283
  17.7 0.0 copy-start.42
  17.8 0.7 copy-done.42
  18.4 0.0 copy-start.48
  18.5 0.1 collective-permute-start.3
  18.6 1.8 collective-permute-start.2
  20.3 6.0 %vals_own.1 = (bf16[640,1536]{1,0:T(8,128)(2,1)S(1)}, bf16[672,1536]{1,0:T(8,128)(2,1)S(1)}, bf16[640,1536]{1,0:T(8,128)(2,1)S(1)}, bf16[12,6,128,128]{3,2,1,0:T(8,128)(2,1)S(1)}, bf16[6,64,128]{2,1,0:T(8,128)(2,1)S(1)}) custom-call(s32[8]{0:T(128)S(1)} %get-tuple-element.113.info, bf16[672,768]{1,0:T(8,128)(2,1)S(1)} %get-tuple-element.112.normed, ...), custom_call_target="tpu_custom_call" | custom-call | flops 9900000256 | bytes 9000000 | tf_op jit(solution)/shard_map/vals_own/pallas_call | solution.py:1319
  26.3 1.9 %collective-permute-done.2.refs_1_ = bf16[192,768]{1,0:T(8,128)(2,1)S(1)} collective-permute-done((bf16[192,768]{1,0:T(8,128)(2,1)}, bf16[192,768]{1,0:T(8,128)(2,1)S(1)}, u32[]{:S(2)}, u32[]{:S(2)}) %collective-permute-start.2) | collective-permute-done | bytes 294944 | tf_op jit(solution)/shard_map/ppermute | solution.py:1208
  28.2 1.9 %collective-permute-start.6 = (bf16[6,64,128]{2,1,0:T(8,128)(2,1)S(1)}, bf16[6,64,128]{2,1,0:T(8,128)(2,1)S(1)}, u32[]{:S(2)}, u32[]{:S(2)}) collective-permute-start(bf16[6,64,128]{2,1,0:T(8,128)(2,1)S(1)} %get-tuple-element.129), channel_id=1, source_target_pairs={{0,1},{1,0},{2,3},{3,2},{4,5},{5,4},{6,7},{7,6},{8,9},{9,8},{10,11... | collective-permute-start | bytes 294920 | tf_op jit(solution)/shard_map/ppermute | solution.py:1204
  30.1 0.2 collective-permute-start.9
  30.4 1.5 collective-permute-start.8
  31.9 6.6 %vals_other.1 = (bf16[640,1536]{1,0:T(8,128)(2,1)S(1)}, bf16[672,1536]{1,0:T(8,128)(2,1)S(1)}, bf16[640,1536]{1,0:T(8,128)(2,1)S(1)}, bf16[12,6,128,128]{3,2,1,0...) custom-call(s32[8]{0:T(128)S(1)} %get-tuple-element.113.info, ...), custom_call_target="tpu_custom_call", output_to_operand_aliasing={{0}: (9, {}), {1}: (10, {}), {2}: (11, {}), {3}: (12, {})} | custom-call | flops 9900000256 | bytes 9000000 | tf_op jit(solution)/shard_map/vals_other/pallas_call | solution.py:1319
  38.5 1.3 copy-done.28
  39.8 0.3 collective-permute-start.5
  40.1 7.8 %scan_other.1 = (bf16[640,1536]{1,0:T(8,128)(2,1)S(1)}, bf16[12,6,128,128]{3,2,1,0:T(8,128)(2,1)S(1)}) custom-call(s32[8]{0:T(128)S(1)} %get-tuple-element.113.info, bf16[640,1536]{1,0:T(8,128)(2,1)S(1)} %get-tuple-element.124.xc_ref, bf16[12,6,128,128]{3,2,1,0:T(8,128)(2,1)S(1)} %get-tuple-element.125.s_ref, ...), custom_call_target="tpu_custom_call" | custom-call | flops 11000000512 | bytes 10000000 | tf_op jit(solution)/shard_map/scan_other/pallas_call | solution.py:1348
  47.9 0.1 collective-permute-start.10
  48.1 0.0 copy-start.1
  48.1 0.0 copy-start.3
  48.1 7.8 %scan_own.1 = (bf16[640,1536]{1,0:T(8,128)(2,1)S(1)}, bf16[12,6,128,128]{3,2,1,0:T(8,128)(2,1)S(1)}) custom-call(s32[8]{0:T(128)S(1)} %get-tuple-element.113.info, bf16[640,1536]{1,0:T(8,128)(2,1)S(1)} %get-tuple-element.124.xc_ref, bf16[12,6,128,128]{3,2,1,0:T(8,128)(2,1)S(1)} %get-tuple-element.125.s_ref, ...), custom_call_target="tpu_custom_call", output_to_operand_aliasing={{0}: (7, {}), {1}: (8, {})} | custom-call | flops 11000000512 | bytes 10000000 | tf_op jit(solution)/shard_map/scan_own/pallas_call | solution.py:1348
  55.9 1.4 copy-done.30
  57.3 16.7 %gated.1 = (bf16[640,768]{1,0:T(8,128)(2,1)}, bf16[640,1536]{1,0:T(8,128)(2,1)S(1)}, bf16[2,384,1536]{2,1,0:T(8,128)(2,1)}, bf16[2,384,1536]{2,1,0:T(8,128)(2,1)...) custom-call(bf16[640,768]{1,0:T(8,128)(2,1)S(1)} %bitcast.57, ...), custom_call_target="tpu_custom_call" | custom-call | flops 18699999232 | bytes 17000000 | tf_op jit(solution)/shard_map/gated/pallas_call | solution.py:1363
  74.1 1.3 copy-done.10
  75.4 0.5 collective-permute-start.11
  75.9 1.5 copy-done.11
  77.4 1.3 copy-done.14
  78.7 1.2 copy-done.17
  79.9 0.8 copy-done.45
  80.8 2.4 %gstate_own.1 = (bf16[12,6,128,128]{3,2,1,0:T(8,128)(2,1)S(1)}, bf16[6,64,128]{2,1,0:T(8,128)(2,1)S(1)}) custom-call(s32[8]{0:T(128)S(1)} %get-tuple-element.113.info, bf16[640,1536]{1,0:T(8,128)(2,1)S(1)} %copy-done.11, f32[4,5,128,128]{3,2,1,0:T(8,128)S(1)} %copy-done.14, f32[3,5,128,128]{3,2,1,0:T(8,128)S(1)} %copy-done.17, f32[128,128]{1,0:T(8,128)S(1)} %copy-done.45), custom_call_target="tpu_custom_call" | custom-call | flops 5500000256 | bytes 5000000 | tf_op jit(solution)/shard_map/gstate_own/pallas_call | solution.py:1403
  83.1 1.8 collective-permute-start.13
  84.9 2.6 %gstate_other.1 = (bf16[12,6,128,128]{3,2,1,0:T(8,128)(2,1)S(1)}, bf16[6,64,128]{2,1,0:T(8,128)(2,1)S(1)}) custom-call(s32[8]{0:T(128)S(1)} %get-tuple-element.113.info, bf16[640,1536]{1,0:T(8,128)(2,1)S(1)} %copy-done.11, f32[4,5,128,128]{3,2,1,0:T(8,128)S(1)} %copy-done.14, f32[3,5,128,128]{3,2,1,0:T(8,128)S(1)} %copy-done.17, ...), custom_call_target="tpu_custom_call", output_to_operand_aliasing={{0}: (5, {})} | custom-call | flops 5500000256 | bytes 5000000 | tf_op jit(solution)/shard_map/gstate_other/pallas_call | solution.py:1403
  87.6 0.0 copy-start.49
  87.6 2.5 %fusion.3 = (bf16[4,48,1536]{2,1,0:T(8,128)(2,1)S(1)}, bf16[4,48,1536]{2,1,0:T(8,128)(2,1)S(1)}, bf16[4,48,1536]{2,1,0:T(8,128)(2,1)S(1)}, bf16[4,48,1536]{2,1,0:T(8,128)(2,1)S(1)}) fusion(bf16[2,4,2,48,1536]{4,3,2,1,0:T(8,128)(2,1)} %bitcast.12, s32[]{:T(128)S(6)} %select_n.40, bf16[2,4,2,48,1536]{4,3,2,1,0:T(8,128)(2,1)S(1)} %bitcast.61, s32[]{:T(128)S(6)} %select_n.39), kind=kLoop, calls=%fused_computation.8 | loop fusion | flops 4718592 | bytes 7077896 | tf_op jit(solution)/shard_map/convert_element_type | solution.py:1389
  90.1 0.4 collective-permute-start.12
  90.4 1.0 collective-permute-start.14
  91.4 1.3 collective-permute-start.15
  92.7 1.2 collective-permute-start.16
  94.0 11.3 %gscan_other.1 = (bf16[640,1536]{1,0:T(8,128)(2,1)S(1)}, f32[5,128,128]{2,1,0:T(8,128)S(1)}, f32[5,128,128]{2,1,0:T(8,128)S(1)}, f32[5,128,128]{2,1,0:T(8,128)S(...) custom-call(s32[8]{0:T(128)S(1)} %get-tuple-element.113.info, ...), custom_call_target="tpu_custom_call" | custom-call | flops 18699999232 | bytes 17000000 | tf_op jit(solution)/shard_map/gscan_other/pallas_call | solution.py:1430
  105.4 1.8 collective-permute-start.17
  107.1 11.2 %gscan_own.1 = (bf16[640,1536]{1,0:T(8,128)(2,1)S(1)}, f32[5,128,128]{2,1,0:T(8,128)S(1)}, f32[5,128,128]{2,1,0:T(8,128)S(1)}, f32[5,128,128]{2,1,0:T(8,128)S(1)...) custom-call(s32[8]{0:T(128)S(1)} %get-tuple-element.113.info, ...), custom_call_target="tpu_custom_call", output_to_operand_aliasing={{0}: (13, {}), {6}: (14, {}), {7}: (15, {})} | custom-call | flops 18699999232 | bytes 17000000 | tf_op jit(solution)/shard_map/gscan_own/pallas_call | solution.py:1430
  118.4 0.4 collective-permute-start.18
  118.7 1.7 collective-permute-done.15
  120.4 0.3 add_convert_fusion.plane_a
  120.7 1.6 collective-permute-done.18.edge_b
  122.3 13.3 %back.1 = (bf16[640,1536]{1,0:T(8,128)(2,1)S(1)}, bf16[2,384,768]{2,1,0:T(8,128)(2,1)S(1)}, bf16[2,384,768]{2,1,0:T(8,128)(2,1)S(1)}, f32[2,16,768]{2,1,0:T(8,128)S(1)}) custom-call(s32[8]{0:T(128)S(1)} %get-tuple-element.113.info, bf16[640,1536]{1,0:T(8,128)(2,1)S(1)} %get-tuple-element.161.gmix, bf16[16,768]{1,0:T(8,128)(2,1)S(1)} %collective-permute-done.17.edge_a, ...), custom_call_target="tpu_custom_call" | custom-call | flops 13200000000 | bytes 12000000 | tf_op jit(solution)/shard_map/back/pallas_call | solution.py:1467
  135.6 0.1 collective-permute-start.20
  135.7 0.0 copy-start.4
  135.7 0.0 copy-start.16
  135.8 0.0 copy-start.43
  135.8 4.0 %join.1 = (f32[672,256]{1,0:T(8,128)S(1)}, bf16[640,128]{1,0:T(8,128)(2,1)S(1)}, f32[16,128]{1,0:T(8,128)S(1)}, f32[16,256]{1,0:T(8,128)S(1)}) custom-call(s32[8]{0:T(128)S(1)} %get-tuple-element.113.info, f32[5,128,128]{2,1,0:T(8,128)S(1)} %get-tuple-element.171.ggt, f32[5,128,128]{2,1,0:T(8,128)S(1)} %get-tuple-element.172.gb, ...), custom_call_target="tpu_custom_call" | custom-call | flops 6600000000 | bytes 6000000 | tf_op jit(solution)/shard_map/join/pallas_call | solution.py:1453
  139.8 0.3 collective-permute-start.19
  140.1 3.4 %collective-permute-done.19.edge = f32[16,256]{1,0:T(8,128)S(1)} collective-permute-done((f32[16,256]{1,0:T(8,128)S(1)}, f32[16,256]{1,0:T(8,128)S(1)}, u32[]{:S(2)}, u32[]{:S(2)}) %collective-permute-start.19) | collective-permute-done | bytes 16416 | tf_op jit(solution)/shard_map/ppermute | solution.py:1204
  143.6 8.5 %last.1 = (bf16[2,384,384]{2,1,0:T(8,128)(2,1)S(1)}, bf16[2,384,384]{2,1,0:T(8,128)(2,1)S(1)}, f32[2,16,768]{2,1,0:T(8,128)S(1)}, f32[640,768]{1,0:T(8,128)}) custom-call(s32[8]{0:T(128)S(1)} %get-tuple-element.113.info, bf16[640,1536]{1,0:T(8,128)(2,1)S(1)} %get-tuple-element.167.gvals, bf16[640,1536]{1,0:T(8,128)(2,1)S(1)} %copy-done.16, ...), custom_call_target="tpu_custom_call" | custom-call | flops 8800000000 | bytes 8000000 | tf_op jit(solution)/shard_map/last/pallas_call | solution.py:1482
  152.2 30.0 %collect.1 = (f32[48,1152]{1,0:T(8,128)S(1)}, f32[16,768]{1,0:T(8,128)S(1)}, f32[48,1536]{1,0:T(8,128)S(1)}) custom-call(bf16[2,384,768]{2,1,0:T(8,128)(2,1)S(1)} %get-tuple-element.191.keep, bf16[2,384,768]{2,1,0:T(8,128)(2,1)S(1)} %collective-permute-done.20.got_v, bf16[2,384,384]{2,1,0:T(8,128)(2,1)S(1)} %get-tuple-element.193.keep_bc, ...), custom_call_target="tpu_custom_call" | custom-call | tf_op jit(solution)/shard_map/collect/pallas_call | solution.py:1501
  182.2 2.2 %finish.1 = (f32[12,48,130]{2,1,0:T(8,128)}, f32[12,48,64]{2,1,0:T(8,128)}, f32[48,256]{1,0:T(8,128)}, f32[7,4,12]{2,1,0:T(4,128)}, f32[7,16]{1,0:T(8,128)}, /*i...) custom-call(f32[16,768]{1,0:T(8,128)S(1)} %get-tuple-element.197.tiny, ...), custom_call_target="tpu_custom_call" | custom-call | tf_op jit(solution)/shard_map/finish/pallas_call | solution.py:1530
  (104 shorter events, 0.2 us)
Async XLA Ops:
  0.6 4.8 %copy-start = (bf16[768,12,130]{0,2,1:T(8,128)(2,1)S(1)}, bf16[768,12,130]{0,2,1:T(8,128)(2,1)}, u32[]{:S(2)}) copy-start(bf16[768,12,130]{0,2,1:T(8,128)(2,1)} %param.16) | copy-start | bytes 7188484
  2.5 8.1 %collective-permute-start.1 = (f32[48,768]{1,0:T(8,128)}, f32[48,768]{1,0:T(8,128)}, u32[]{:S(2)}, u32[]{:S(2)}) collective-permute-start(f32[48,768]{1,0:T(8,128)} %small.1.small_a), channel_id=1, source_target_pairs={{0,1},{1,0},{2,3},{3,2},{4,5},{5,4},{6,7},{7,6},{8,9},{9,8},{10,11... | collective-permute-start | bytes 442376 | tf_op jit(solution)/shard_map/ppermute | solution.py:1204
  6.3 4.2 %copy-start.51 = (f32[768]{0:T(1024)S(1)}, f32[768]{0:T(1024)}, u32[]{:S(2)}) copy-start(f32[768]{0:T(1024)} %param.15) | copy-start | bytes 9220
  6.3 4.2 %copy-start.2 = (bf16[1,640,768]{2,1,0:T(8,128)(2,1)S(1)}, bf16[1,640,768]{2,1,0:T(8,128)(2,1)}, u32[]{:S(2)}) copy-start(bf16[1,640,768]{2,1,0:T(8,128)(2,1)} %param.14) | copy-start | bytes 2949124
  6.3 4.3 %copy-start.7 = (f32[7,256]{1,0:T(8,128)S(1)}, f32[7,256]{1,0:T(8,128)}, u32[]{:S(2)}) copy-start(f32[7,256]{1,0:T(8,128)} %taps_ref.1) | copy-start | bytes 21508
  6.3 4.3 %copy-start.8 = (s32[1,1280]{1,0:T(1,128)S(1)}, s32[1,1280]{1,0:T(1,128)}, u32[]{:S(2)}) copy-start(s32[1,1280]{1,0:T(1,128)} %live_ref.1) | copy-start | bytes 15364
  6.4 4.3 %copy-start.9 = (s32[1,4]{1,0:T(1,128)S(1)}, s32[1,4]{1,0:T(1,128)}, u32[]{:S(2)}) copy-start(s32[1,4]{1,0:T(1,128)} %starts.1) | copy-start | bytes 52
  6.4 12.1 %collective-permute-start = (bf16[192,768]{1,0:T(8,128)(2,1)}, bf16[192,768]{1,0:T(8,128)(2,1)}, u32[]{:S(2)}, u32[]{:S(2)}) collective-permute-start(bf16[192,768]{1,0:T(8,128)(2,1)} %bitcast.3), channel_id=1, source_target_pairs={{0,1},{1,0},{2,3},{3,2},{4,5},{5,4},{6,7},{7,6},{8,9},{9,8},{10,11... | collective-permute-start | bytes 884744 | tf_op jit(solution)/shard_map/ppermute | solution.py:1204
  6.5 4.2 %copy-start.5 = (bf16[768,256]{1,0:T(8,128)(2,1)S(1)}, bf16[768,256]{1,0:T(8,128)(2,1)}, u32[]{:S(2)}) copy-start(bf16[768,256]{1,0:T(8,128)(2,1)} %wbc_ref.1) | copy-start | bytes 1179652
  6.5 4.2 %copy-start.6 = (f32[48,768]{1,0:T(8,128)S(1)}, f32[48,768]{1,0:T(8,128)}, u32[]{:S(2)}) copy-start(f32[48,768]{1,0:T(8,128)} %small.1.small_a) | copy-start | bytes 442372
  8.6 21.6 %collective-permute-start.7 = (bf16[192,1536]{1,0:T(8,128)(2,1)S(1)}, bf16[192,1536]{1,0:T(8,128)(2,1)S(1)}, u32[]{:S(2)}, u32[]{:S(2)}) collective-permute-start(bf16[192,1536]{1,0:T(8,128)(2,1)S(1)} %pad_maximum_fusion), channel_id=1, source_target_pairs={{0,1},{1,0},{2,3},{3,2},{4,5},{5,4},{6,7},{7,6},{8,9},{9,8},{10,11... | collective-permute-start | bytes 1769480 | tf_op jit(solution)/shard_map/ppermute | solution.py:1204
  18.4 7.9 %copy-start.37 = (bf16[768,256]{1,0:T(8,128)(2,1)}, bf16[768,256]{1,0:T(8,128)(2,1)S(1)}, u32[]{:S(2)}) copy-start(bf16[768,256]{1,0:T(8,128)(2,1)S(1)} %get-tuple-element.186.wbc) | copy-start | bytes 1179652
  18.4 7.9 %copy-start.39 = (f32[640,1]{1,0:T(8,128)}, f32[640,1]{1,0:T(8,128)S(1)}, u32[]{:S(2)}) copy-start(f32[640,1]{1,0:T(8,128)S(1)} %get-tuple-element.187.rs) | copy-start | bytes 7684
  18.4 13.4 %copy-start.35 = (f32[2,5,128,128]{3,2,1,0:T(8,128)}, f32[2,5,128,128]{3,2,1,0:T(8,128)S(1)}, u32[]{:S(2)}) copy-start(f32[2,5,128,128]{3,2,1,0:T(8,128)S(1)} %get-tuple-element.116.refs_2_.refs_5_.wt) | copy-start | bytes 1966084
  18.4 13.4 %copy-start.46 = (f32[8,1536]{1,0:T(8,128)}, f32[8,1536]{1,0:T(8,128)S(1)}, u32[]{:S(2)}) copy-start(f32[8,1536]{1,0:T(8,128)S(1)} %get-tuple-element.115.refs_1_.refs_4_.taps) | copy-start | bytes 147460
  18.4 29.6 %copy-start.13 = (f32[4,5,128,128]{3,2,1,0:T(8,128)}, f32[4,5,128,128]{3,2,1,0:T(8,128)S(1)}, u32[]{:S(2)}) copy-start(f32[4,5,128,128]{3,2,1,0:T(8,128)S(1)} %get-tuple-element.127.tb.coltt.rowst) | copy-start | bytes 3932164
  18.4 29.6 %copy-start.44 = (f32[128,128]{1,0:T(8,128)}, f32[128,128]{1,0:T(8,128)S(1)}, u32[]{:S(2)}) copy-start(f32[128,128]{1,0:T(8,128)S(1)} %get-tuple-element.117.refs_3_.refs_6_.dpt) | copy-start | bytes 196612
  18.4 29.6 %copy-start.48 = (f32[8,1536]{1,0:T(8,128)}, f32[8,1536]{1,0:T(8,128)S(1)}, u32[]{:S(2)}) copy-start(f32[8,1536]{1,0:T(8,128)S(1)} %get-tuple-element.128.skip) | copy-start | bytes 147460
  18.5 38.9 %copy-start.24 = (bf16[672,768]{1,0:T(8,128)(2,1)}, bf16[672,768]{1,0:T(8,128)(2,1)S(1)}, u32[]{:S(2)}) copy-start(bf16[672,768]{1,0:T(8,128)(2,1)S(1)} %get-tuple-element.112.normed) | copy-start | bytes 3096580
  18.5 13.4 %collective-permute-start.3 = (bf16[192,768]{1,0:T(8,128)(2,1)}, bf16[192,768]{1,0:T(8,128)(2,1)S(1)}, u32[]{:S(2)}, u32[]{:S(2)}) collective-permute-start(bf16[192,768]{1,0:T(8,128)(2,1)} %collective-permute-done.refs_0_), channel_id=1, source_target_pairs={{0,2},{2,0},{4,6},{6,4},{8,10},{10,8},{12,14},{14,12},{16,18},{18,... | collective-permute-start | bytes 884744 | tf_op jit(solution)/shard_map/ppermute | solution.py:1208
  18.6 9.6 %collective-permute-start.2 = (bf16[192,768]{1,0:T(8,128)(2,1)}, bf16[192,768]{1,0:T(8,128)(2,1)S(1)}, u32[]{:S(2)}, u32[]{:S(2)}) collective-permute-start(bf16[192,768]{1,0:T(8,128)(2,1)} %collective-permute-done.refs_0_), channel_id=1, source_target_pairs={{0,4},{2,6},{4,0},{6,2},{8,12},{10,14},{12,8},{14,10},{16,20},{18,... | collective-permute-start | bytes 884744 | tf_op jit(solution)/shard_map/ppermute | solution.py:1208
  28.2 3.7 %collective-permute-start.4 = (bf16[192,768]{1,0:T(8,128)(2,1)S(1)}, bf16[192,768]{1,0:T(8,128)(2,1)S(1)}, u32[]{:S(2)}, u32[]{:S(2)}) collective-permute-start(bf16[192,768]{1,0:T(8,128)(2,1)S(1)} %collective-permute-done.2.refs_1_), channel_id=1, source_target_pairs={{0,2},{2,0},{4,6},{6,4},{8,10},{10,8},{12,14},{14,12},{16,18},{18,... | collective-permute-start | bytes 884744 | tf_op jit(solution)/shard_map/ppermute | solution.py:1208
  28.2 11.9 %collective-permute-start.6 = (bf16[6,64,128]{2,1,0:T(8,128)(2,1)S(1)}, bf16[6,64,128]{2,1,0:T(8,128)(2,1)S(1)}, u32[]{:S(2)}, u32[]{:S(2)}) collective-permute-start(bf16[6,64,128]{2,1,0:T(8,128)(2,1)S(1)} %get-tuple-element.129), channel_id=1, source_target_pairs={{0,1},{1,0},{2,3},{3,2},{4,5},{5,4},{6,7},{7,6},{8,9},{9,8},{10,11... | collective-permute-start | bytes 294920 | tf_op jit(solution)/shard_map/ppermute | solution.py:1204
  30.1 27.2 %collective-permute-start.9 = (bf16[192,1536]{1,0:T(8,128)(2,1)S(1)}, bf16[192,1536]{1,0:T(8,128)(2,1)S(1)}, u32[]{:S(2)}, u32[]{:S(2)}) collective-permute-start(bf16[192,1536]{1,0:T(8,128)(2,1)S(1)} %collective-permute-done.7.p0), channel_id=1, source_target_pairs={{0,2},{2,0},{4,6},{6,4},{8,10},{10,8},{12,14},{14,12},{16,18},{18,... | collective-permute-start | bytes 1769480 | tf_op jit(solution)/shard_map/ppermute | solution.py:1208
  30.4 17.6 %collective-permute-start.8 = (bf16[192,1536]{1,0:T(8,128)(2,1)S(1)}, bf16[192,1536]{1,0:T(8,128)(2,1)S(1)}, u32[]{:S(2)}, u32[]{:S(2)}) collective-permute-start(bf16[192,1536]{1,0:T(8,128)(2,1)S(1)} %collective-permute-done.7.p0), channel_id=1, source_target_pairs={{0,4},{2,6},{4,0},{6,2},{8,12},{10,14},{12,8},{14,10},{16,20},{18,... | collective-permute-start | bytes 1769480 | tf_op jit(solution)/shard_map/ppermute | solution.py:1208
  39.8 8.1 %copy-start.19 = (bf16[768,768]{1,0:T(8,128)(2,1)}, bf16[768,768]{1,0:T(8,128)(2,1)S(1)}, u32[]{:S(2)}) copy-start(bf16[768,768]{1,0:T(8,128)(2,1)S(1)} %get-tuple-element.169.wv_b) | copy-start | bytes 3538948
  39.8 8.1 %copy-start.22 = (bf16[672,1536]{1,0:T(8,128)(2,1)}, bf16[672,1536]{1,0:T(8,128)(2,1)S(1)}, u32[]{:S(2)}) copy-start(bf16[672,1536]{1,0:T(8,128)(2,1)S(1)} %get-tuple-element.164.vm) | copy-start | bytes 6193156
  39.8 8.3 %copy-start.26 = (bf16[640,1536]{1,0:T(8,128)(2,1)}, bf16[640,1536]{1,0:T(8,128)(2,1)S(1)}, u32[]{:S(2)}) copy-start(bf16[640,1536]{1,0:T(8,128)(2,1)S(1)} %get-tuple-element.124.xc_ref) | copy-start | bytes 5898244
  39.8 8.2 %collective-permute-start.5 = (bf16[6,64,128]{2,1,0:T(8,128)(2,1)S(1)}, bf16[6,64,128]{2,1,0:T(8,128)(2,1)S(1)}, u32[]{:S(2)}, u32[]{:S(2)}) collective-permute-start(bf16[6,64,128]{2,1,0:T(8,128)(2,1)S(1)} %get-tuple-element.126), channel_id=1, source_target_pairs={{0,1},{1,0},{2,3},{3,2},{4,5},{5,4},{6,7},{7,6},{8,9},{9,8},{10,11... | collective-permute-start | bytes 294920 | tf_op jit(solution)/shard_map/ppermute | solution.py:1204
  47.9 9.4 %collective-permute-start.10 = (bf16[192,1536]{1,0:T(8,128)(2,1)S(1)}, bf16[192,1536]{1,0:T(8,128)(2,1)S(1)}, u32[]{:S(2)}, u32[]{:S(2)}) collective-permute-start(bf16[192,1536]{1,0:T(8,128)(2,1)S(1)} %collective-permute-done.8.p1), channel_id=1, source_target_pairs={{0,2},{2,0},{4,6},{6,4},{8,10},{10,8},{12,14},{14,12},{16,18},{18,... | collective-permute-start | bytes 1769480 | tf_op jit(solution)/shard_map/ppermute | solution.py:1208
  48.1 9.3 %copy-start.1 = (bf16[12,64,768]{2,1,0:T(8,128)(2,1)S(1)}, bf16[12,64,768]{2,1,0:T(8,128)(2,1)}, u32[]{:S(2)}) copy-start(bf16[12,64,768]{2,1,0:T(8,128)(2,1)} %param.24) | copy-start | bytes 3538948
  48.1 9.3 %copy-start.3 = (bf16[1,640,768]{2,1,0:T(8,128)(2,1)S(1)}, bf16[1,640,768]{2,1,0:T(8,128)(2,1)}, u32[]{:S(2)}) copy-start(bf16[1,640,768]{2,1,0:T(8,128)(2,1)} %param.25) | copy-start | bytes 2949124
  75.4 12.1 %collective-permute-start.11 = (bf16[2,384,1536]{2,1,0:T(8,128)(2,1)}, bf16[2,384,1536]{2,1,0:T(8,128)(2,1)}, u32[]{:S(2)}, u32[]{:S(2)}) collective-permute-start(bf16[2,384,1536]{2,1,0:T(8,128)(2,1)} %get-tuple-element.143), channel_id=1, source_target_pairs={{0,2},{2,0},{4,6},{6,4},{8,10},{10,8},{12,14},{14,12},{16,18},{18,... | collective-permute-start | bytes 7077896 | tf_op jit(solution)/shard_map/ppermute | solution.py:1208
  83.1 10.8 %collective-permute-start.13 = (bf16[6,64,128]{2,1,0:T(8,128)(2,1)S(1)}, bf16[6,64,128]{2,1,0:T(8,128)(2,1)S(1)}, u32[]{:S(2)}, u32[]{:S(2)}) collective-permute-start(bf16[6,64,128]{2,1,0:T(8,128)(2,1)S(1)} %get-tuple-element.146), channel_id=1, source_target_pairs={{0,1},{1,0},{2,3},{3,2},{4,5},{5,4},{6,7},{7,6},{8,9},{9,8},{10,11... | collective-permute-start | bytes 294920 | tf_op jit(solution)/shard_map/ppermute | solution.py:1204
  84.9 9.0 %copy-start.29 = (bf16[640,1536]{1,0:T(8,128)(2,1)S(1)}, bf16[640,1536]{1,0:T(8,128)(2,1)}, u32[]{:S(2)}) copy-start(bf16[640,1536]{1,0:T(8,128)(2,1)} %copy-done.28) | copy-start | bytes 5898244
  84.9 9.0 %copy-start.31 = (bf16[12,6,128,128]{3,2,1,0:T(8,128)(2,1)S(1)}, bf16[12,6,128,128]{3,2,1,0:T(8,128)(2,1)}, u32[]{:S(2)}) copy-start(bf16[12,6,128,128]{3,2,1,0:T(8,128)(2,1)} %copy-done.30) | copy-start | bytes 7077892
  87.5 6.4 %copy-start.12 = (bf16[640,1536]{1,0:T(8,128)(2,1)S(1)}, bf16[640,1536]{1,0:T(8,128)(2,1)}, u32[]{:S(2)}) copy-start(bf16[640,1536]{1,0:T(8,128)(2,1)} %copy-done.10) | copy-start | bytes 5898244
  87.5 6.4 %copy-start.15 = (f32[4,5,128,128]{3,2,1,0:T(8,128)S(1)}, f32[4,5,128,128]{3,2,1,0:T(8,128)}, u32[]{:S(2)}) copy-start(f32[4,5,128,128]{3,2,1,0:T(8,128)} %copy-done.13) | copy-start | bytes 3932164
  87.6 6.4 %copy-start.18 = (f32[3,5,128,128]{3,2,1,0:T(8,128)S(1)}, f32[3,5,128,128]{3,2,1,0:T(8,128)}, u32[]{:S(2)}) copy-start(f32[3,5,128,128]{3,2,1,0:T(8,128)} %get-tuple-element.138.cet.tc) | copy-start | bytes 2949124
  87.6 6.4 %copy-start.27 = (bf16[640,1536]{1,0:T(8,128)(2,1)S(1)}, bf16[640,1536]{1,0:T(8,128)(2,1)}, u32[]{:S(2)}) copy-start(bf16[640,1536]{1,0:T(8,128)(2,1)} %copy-done.26) | copy-start | bytes 5898244
  87.6 6.4 %copy-start.36 = (f32[2,5,128,128]{3,2,1,0:T(8,128)S(1)}, f32[2,5,128,128]{3,2,1,0:T(8,128)}, u32[]{:S(2)}) copy-start(f32[2,5,128,128]{3,2,1,0:T(8,128)} %copy-done.35) | copy-start | bytes 1966084
  87.6 6.4 %copy-start.49 = (f32[8,1536]{1,0:T(8,128)S(1)}, f32[8,1536]{1,0:T(8,128)}, u32[]{:S(2)}) copy-start(f32[8,1536]{1,0:T(8,128)} %copy-done.48) | copy-start | bytes 147460
  90.1 17.1 %collective-permute-start.12 = (bf16[6,64,128]{2,1,0:T(8,128)(2,1)S(1)}, bf16[6,64,128]{2,1,0:T(8,128)(2,1)S(1)}, u32[]{:S(2)}, u32[]{:S(2)}) collective-permute-start(bf16[6,64,128]{2,1,0:T(8,128)(2,1)S(1)} %get-tuple-element.145), channel_id=1, source_target_pairs={{0,1},{1,0},{2,3},{3,2},{4,5},{5,4},{6,7},{7,6},{8,9},{9,8},{10,11... | collective-permute-start | bytes 294920 | tf_op jit(solution)/shard_map/ppermute | solution.py:1204
  90.4 28.3 %collective-permute-start.14 = (bf16[4,48,1536]{2,1,0:T(8,128)(2,1)S(1)}, bf16[4,48,1536]{2,1,0:T(8,128)(2,1)S(1)}, u32[]{:S(2)}, u32[]{:S(2)}) collective-permute-start(bf16[4,48,1536]{2,1,0:T(8,128)(2,1)S(1)} %get-tuple-element.158), channel_id=1, source_target_pairs={{0,4},{2,6},{4,0},{6,2},{8,12},{10,14},{12,8},{14,10},{16,20},{18,... | collective-permute-start | bytes 1769480 | tf_op jit(solution)/shard_map/ppermute | solution.py:1208
  91.4 29.0 %collective-permute-start.15 = (bf16[4,48,1536]{2,1,0:T(8,128)(2,1)S(1)}, bf16[4,48,1536]{2,1,0:T(8,128)(2,1)S(1)}, u32[]{:S(2)}, u32[]{:S(2)}) collective-permute-start(bf16[4,48,1536]{2,1,0:T(8,128)(2,1)S(1)} %get-tuple-element.159), channel_id=1, source_target_pairs={{0,1},{1,0},{2,3},{3,2},{4,5},{5,4},{6,7},{7,6},{8,9},{9,8},{10,11... | collective-permute-start | bytes 1769480 | tf_op jit(solution)/shard_map/ppermute | solution.py:1204
  92.7 27.7 %collective-permute-start.16 = (bf16[4,48,1536]{2,1,0:T(8,128)(2,1)S(1)}, bf16[4,48,1536]{2,1,0:T(8,128)(2,1)S(1)}, u32[]{:S(2)}, u32[]{:S(2)}) collective-permute-start(bf16[4,48,1536]{2,1,0:T(8,128)(2,1)S(1)} %get-tuple-element.160), channel_id=1, source_target_pairs={{0,5},{1,4},{2,7},{3,6},{4,1},{5,0},{6,3},{7,2},{8,13},{9,12},{10,... | collective-permute-start | bytes 1769480 | tf_op jit(solution)/shard_map/ppermute | solution.py:1213
  105.4 15.3 %collective-permute-start.17 = (bf16[16,768]{1,0:T(8,128)(2,1)S(1)}, bf16[16,768]{1,0:T(8,128)(2,1)S(1)}, u32[]{:S(2)}, u32[]{:S(2)}) collective-permute-start(bf16[16,768]{1,0:T(8,128)(2,1)S(1)} %get-tuple-element.162), channel_id=1, source_target_pairs={{0,1},{1,0},{2,3},{3,2},{4,5},{5,4},{6,7},{7,6},{8,9},{9,8},{10,11... | collective-permute-start | bytes 73736 | tf_op jit(solution)/shard_map/ppermute | solution.py:1204
  107.1 15.1 %copy-start.25 = (bf16[672,768]{1,0:T(8,128)(2,1)S(1)}, bf16[672,768]{1,0:T(8,128)(2,1)}, u32[]{:S(2)}) copy-start(bf16[672,768]{1,0:T(8,128)(2,1)} %copy-done.24) | copy-start | bytes 3096580
  118.3 3.9 %copy-start.23 = (bf16[672,1536]{1,0:T(8,128)(2,1)S(1)}, bf16[672,1536]{1,0:T(8,128)(2,1)}, u32[]{:S(2)}) copy-start(bf16[672,1536]{1,0:T(8,128)(2,1)} %copy-done.22) | copy-start | bytes 6193156
  118.3 3.9 %copy-start.47 = (f32[8,1536]{1,0:T(8,128)S(1)}, f32[8,1536]{1,0:T(8,128)}, u32[]{:S(2)}) copy-start(f32[8,1536]{1,0:T(8,128)} %copy-done.46) | copy-start | bytes 147460
  118.4 3.9 %collective-permute-start.18 = (bf16[16,768]{1,0:T(8,128)(2,1)S(1)}, bf16[16,768]{1,0:T(8,128)(2,1)S(1)}, u32[]{:S(2)}, u32[]{:S(2)}) collective-permute-start(bf16[16,768]{1,0:T(8,128)(2,1)S(1)} %get-tuple-element.163), channel_id=1, source_target_pairs={{0,1},{1,0},{2,3},{3,2},{4,5},{5,4},{6,7},{7,6},{8,9},{9,8},{10,11... | collective-permute-start | bytes 73736 | tf_op jit(solution)/shard_map/ppermute | solution.py:1204
  122.3 13.4 %copy-start.32 = (f32[640,384]{1,0:T(8,128)S(1)}, f32[640,384]{1,0:T(8,128)}, u32[]{:S(2)}) copy-start(f32[640,384]{1,0:T(8,128)} %get-tuple-element.179.sig) | copy-start | bytes 2949124
  122.3 13.4 %copy-start.34 = (f32[672,256]{1,0:T(8,128)S(1)}, f32[672,256]{1,0:T(8,128)}, u32[]{:S(2)}) copy-start(f32[672,256]{1,0:T(8,128)} %get-tuple-element.178.dsl) | copy-start | bytes 2064388
  122.3 13.4 %copy-start.41 = (bf16[640,256]{1,0:T(8,128)(2,1)S(1)}, bf16[640,256]{1,0:T(8,128)(2,1)}, u32[]{:S(2)}) copy-start(bf16[640,256]{1,0:T(8,128)(2,1)} %get-tuple-element.177.maps) | copy-start | bytes 983044
  135.6 16.6 %collective-permute-start.20 = (bf16[2,384,768]{2,1,0:T(8,128)(2,1)S(1)}, bf16[2,384,768]{2,1,0:T(8,128)(2,1)S(1)}, u32[]{:S(2)}, u32[]{:S(2)}) collective-permute-start(bf16[2,384,768]{2,1,0:T(8,128)(2,1)S(1)} %get-tuple-element.192), channel_id=1, source_target_pairs={{0,2},{2,0},{4,6},{6,4},{8,10},{10,8},{12,14},{14,12},{16,18},{18,... | collective-permute-start | bytes 3538952 | tf_op jit(solution)/shard_map/ppermute | solution.py:1208
  135.7 7.9 %copy-start.4 = (bf16[1,640,768]{2,1,0:T(8,128)(2,1)S(1)}, bf16[1,640,768]{2,1,0:T(8,128)(2,1)}, u32[]{:S(2)}) copy-start(bf16[1,640,768]{2,1,0:T(8,128)(2,1)} %param.25) | copy-start | bytes 2949124
  135.7 7.8 %copy-start.16 = (bf16[640,1536]{1,0:T(8,128)(2,1)S(1)}, bf16[640,1536]{1,0:T(8,128)(2,1)}, u32[]{:S(2)}) copy-start(bf16[640,1536]{1,0:T(8,128)(2,1)} %get-tuple-element.168.ggate) | copy-start | bytes 5898244
  135.7 7.8 %copy-start.20 = (bf16[768,768]{1,0:T(8,128)(2,1)S(1)}, bf16[768,768]{1,0:T(8,128)(2,1)}, u32[]{:S(2)}) copy-start(bf16[768,768]{1,0:T(8,128)(2,1)} %copy-done.19) | copy-start | bytes 3538948
  135.7 7.8 %copy-start.21 = (bf16[768,768]{1,0:T(8,128)(2,1)S(1)}, bf16[768,768]{1,0:T(8,128)(2,1)}, u32[]{:S(2)}) copy-start(bf16[768,768]{1,0:T(8,128)(2,1)} %get-tuple-element.170.wg_b) | copy-start | bytes 3538948
  135.8 7.8 %copy-start.33 = (f32[672,256]{1,0:T(8,128)S(1)}, f32[672,256]{1,0:T(8,128)}, u32[]{:S(2)}) copy-start(f32[672,256]{1,0:T(8,128)} %get-tuple-element.182.bcm) | copy-start | bytes 2064388
  135.8 7.8 %copy-start.38 = (bf16[768,256]{1,0:T(8,128)(2,1)S(1)}, bf16[768,256]{1,0:T(8,128)(2,1)}, u32[]{:S(2)}) copy-start(bf16[768,256]{1,0:T(8,128)(2,1)} %copy-done.37) | copy-start | bytes 1179652
  135.8 7.8 %copy-start.40 = (f32[640,1]{1,0:T(8,128)S(1)}, f32[640,1]{1,0:T(8,128)}, u32[]{:S(2)}) copy-start(f32[640,1]{1,0:T(8,128)} %copy-done.39) | copy-start | bytes 7684
  135.8 7.8 %copy-start.43 = (bf16[128,768]{1,0:T(8,128)(2,1)S(1)}, bf16[128,768]{1,0:T(8,128)(2,1)}, u32[]{:S(2)}) copy-start(bf16[128,768]{1,0:T(8,128)(2,1)} %copy-done.42) | copy-start | bytes 589828
  139.8 3.7 %collective-permute-start.19 = (f32[16,256]{1,0:T(8,128)S(1)}, f32[16,256]{1,0:T(8,128)S(1)}, u32[]{:S(2)}, u32[]{:S(2)}) collective-permute-start(f32[16,256]{1,0:T(8,128)S(1)} %get-tuple-element.181), channel_id=1, source_target_pairs={{0,1},{1,0},{2,3},{3,2},{4,5},{5,4},{6,7},{7,6},{8,9},{9,8},{10,11... | collective-permute-start | bytes 49160 | tf_op jit(solution)/shard_map/ppermute | solution.py:1204
  (9 other events, 12.2 us)
where the time goes:
time: 185 us; the launch traced here: 184 us
  Pallas kernels  139 us (75%)
  starting transfers between devices  19.6 us (11%)
  local copies, waits for them, and re-layouts  11.7 us (6%)
  waiting for transfers between devices  8.59 us (5%)
  other arithmetic  3.76 us (2%)
    pallas_call x1, Pallas kernels, split_positions(): pl.pallas_call(collect_kernel, out_shape=[sds((share, cols), F32), sds((1...  30 us
    pallas_call x2, Pallas kernels, gscan(): pl.pallas_call(functools.partial(gscan_kernel, length, first), grid=(hp,)...  22.5 us
    pallas_call x1, Pallas kernels, split_positions(): pl.pallas_call(functools.partial(gate_kernel, nb), out_shape=[pltpu.HBM((...  16.7 us
    pallas_call x2, Pallas kernels, scan(): pl.pallas_call(functools.partial(scan_kernel, length, first), grid=(hp,),...  15.6 us
    pallas_call x1, Pallas kernels, split_positions(): pl.pallas_call(functools.partial(back_kernel, length, pairs // 2), out_sh...  13.3 us
    ppermute x11, starting transfers between devices, swap(): return lax.ppermute(v, 'narrow', [(0, 1), (1, 0)])  13.2 us
    pallas_call x2, Pallas kernels, vals(): pl.pallas_call(functools.partial(vals_kernel, length, other), grid=(steps...  12.6 us
    unnamed x104, local copies, waits for them, and re-layouts  9.72 us
  transfers between devices with their start and end apart: 21, of which 4 were waited for; matrix products, arithmetic and copies ran while one was open for 3% of the time, Pallas kernels for 41%

commit v1 on v0

--- a/solution.py
+++ b/solution.py
@@ -590,9 +590,8 @@
 
 
 def gate_kernel(
-    tiles, x_ref, g_ref, normed, y_ref, wout_a, w_ref, p0, p1, p2, p3, gain,
-    out_h, gy_o, keep_h, send_h, ggate_h, ggain_o, wgo_h, hn_s, other_s, gated_s, act_s, dact_s, ghn_s,
-    out_o, keep_o, send_o, ggate_o, sems,
+    tiles, info, x_ref, g_ref, normed, y_ref, wout_a, w_ref, p0, p1, p2, p3, gain, tb, tc, dpt,
+    out_h, gy_o, ggate_o, hn_s, ggain_o, wgo_h, gs_o, bnd_o, other_s, gated_s, act_s, dact_s, ghn_s, loc_s, out_o, sems,
 ):
     late = []
 
@@ -607,6 +606,8 @@
     assemble(other_s, (p0, p1, p2, p3))
     send(other_s.at[:, dm:], wgo_h)
     ggain_o[...] = jnp.zeros_like(ggain_o)
+    first = iota((BLOCK, 128), 1) < 64
+    top = iota((BLOCK, 128), 0) < 64
 
     @pl.loop(0, tiles)
     def _(i):
@@ -655,12 +656,47 @@
         for lo in range(0, chans, 128):
             cols = slice(lo, lo + 128)
             ggated = inv * ghn_s[:, cols] - gated_s[:, cols] * cross
-            gy_o[rows, cols] = (ggated * act_s[:, cols]).astype(BF16)
+            gy = (ggated * act_s[:, cols]).astype(BF16)
+            gy_o[rows, cols] = gy
             ggate_o[rows, cols] = (ggated * y_ref[rows, cols].astype(F32) * dact_s[:, cols]).astype(BF16)
+            got = []
+            for h in range(lo // HD, lo // HD + 2):
+                e = jnp.where(top, jnp.exp(tb[0, i, h : h + 1, :]), jnp.exp(tb[0, i, 64 + h : 65 + h, :]))
+                got.append((tc[2, i] * e).astype(BF16))
+            got = mm(jnp.concatenate(got, axis=0), gy)
+            loc_s[i, :, cols] = jnp.where(first, got[0:BLOCK, :], got[BLOCK:, :])
 
     send(out_o, out_h)
-    send(ggate_o, ggate_h)
-    length = g_ref.shape[0]
+
+    @pl.loop(0, chans // 128)
+    def _(j):
+        cols = pl.ds(pl.multiple_of(j * 128, 128), 128)
+        state = jnp.zeros((64, 128), F32)
+        gs_o[j, tiles, 0:64, :] = state.astype(BF16)
+        for b in range(tiles - 1, -1, -1):
+            state = pair_rows(dpt, j, 0, b, 0) * state + loc_s[b, 0:64, cols]
+            gs_o[j, b, 0:64, :] = state.astype(BF16)
+        end_f = state
+        state = jnp.zeros((64, 128), F32)
+        gs_o[j, 0, 64:128, :] = state.astype(BF16)
+        for b in range(tiles):
+            state = pair_rows(dpt, j, 0, b, 1) * state + loc_s[b, 64:128, cols]
+            gs_o[j, b + 1, 64:128, :] = state.astype(BF16)
+        bnd_o[j] = jnp.where(info[7] == 1, end_f, state).astype(BF16)
+
+    for one in late:
+        one.wait()
+
+
+def wsum_kernel(g_ref, normed, hn, ggate, keep_h, send_h, keep_o, send_o, sems):
+    length, dm = g_ref.shape
+    half = hn.shape[1] // 2
+    late = []
+
+    def send(src, dst):
+        late.append(pltpu.make_async_copy(src, dst, sems.at[len(late)]))
+        late[-1].start()
+
     gt = g_ref[...].T
     nt_ = normed[HALO : HALO + length, :].T
     for k in range(2):
@@ -668,53 +704,20 @@
             cols = slice(k * half + p * 256, k * half + (p + 1) * 256)
             dst = slice(p * 256, (p + 1) * 256)
             dst2 = slice(half + p * 256, half + (p + 1) * 256)
-            by_core(mm(gt, hn_s[:, cols]), keep_o.at[k, :, dst], send_o.at[k, :, dst])
-            by_core(mm(nt_, ggate_o[:, cols]), keep_o.at[k, :, dst2], send_o.at[k, :, dst2])
+            by_core(mm(gt, hn[:, cols]), keep_o.at[k, :, dst], send_o.at[k, :, dst])
+            by_core(mm(nt_, ggate[:, cols]), keep_o.at[k, :, dst2], send_o.at[k, :, dst2])
         send(send_o.at[k], send_h.at[k])
         send(keep_o.at[k], keep_h.at[k])
     for one in late:
         one.wait()
 
 
-def gstate_kernel(length, first_pair, info, gy_ref, coltt, cet, dpt, *refs):
-    nb = length // BLOCK
-    gs_o, bnd_o = refs[-2:]
-    j = pl.program_id(0) + first_pair
-    lane = iota((BLOCK, 128), 1)
-    top = iota((BLOCK, 128), 0) < 64
-    loc = []
-    for b in range(nb):
-        blk = slice(b * BLOCK, (b + 1) * BLOCK)
-        gy = gy_ref[blk, :]
-        got = []
-        for i in range(2):
-            h = 2 * j + i
-            e = jnp.where(top, jnp.exp(coltt[b, pl.ds(h, 1), :]), jnp.exp(coltt[b, pl.ds(64 + h, 1), :]))
-            got.append((cet[b] * e).astype(BF16))
-        got = mm(jnp.concatenate(got, axis=0), gy)
-        loc.append(jnp.where(lane < 64, got[0:BLOCK, :], got[BLOCK:, :]))
-    state = jnp.zeros((64, 128), F32)
-    gs_o[0, nb, 0:64, :] = state.astype(BF16)
-    for b in range(nb - 1, -1, -1):
-        state = pair_rows(dpt, j, 0, b, 0) * state + loc[b][0:64, :]
-        gs_o[0, b, 0:64, :] = state.astype(BF16)
-    end_f = state
-    state = jnp.zeros((64, 128), F32)
-    gs_o[0, 0, 64:128, :] = state.astype(BF16)
-    for b in range(nb):
-        state = pair_rows(dpt, j, 0, b, 1) * state + loc[b][64:128, :]
-        gs_o[0, b + 1, 64:128, :] = state.astype(BF16)
-    bnd_o[0] = jnp.where(info[7] == 1, end_f, state).astype(BF16)
-
-
 def gscan_kernel(
-    length, first_pair, info, xc_ref, ds_ref, gy_ref, st_ref, gs_ref, gs0_ref, dpt, rowst, wt, coltt, tc, skip,
-    *refs,
+    length, info, xc_ref, ds_ref, gy_ref, st_ref, gs_ref, gs0_ref, dpt, rowst, wt, coltt, tc, skip,
+    gmix_o, ggt_o, gb_o, gct_o, k_o, r_o, phi_o, gskip_o, edge_o, gst_s,
 ):
     nb = length // BLOCK
-    gmix_o, ggt_o, gb_o, gct_o, k_o, r_o, phi_o, gskip_o, edge_o, gst_s = refs[-10:]
-    step = pl.program_id(0)
-    j = step + first_pair
+    j = pl.program_id(0)
     right = (info[7] == 1).astype(F32)
     s0 = gs0_ref[0].astype(F32)
     sub = iota((BLOCK, BLOCK), 0)
@@ -723,10 +726,10 @@
     later = lane > sub
     top = sub < 64
 
-    @pl.when(step == 0)
+    @pl.when(j == 0)
     def _():
-        for k, acc in enumerate((ggt_o, gb_o, gct_o, k_o, r_o)):
-            acc[...] = jnp.zeros_like(acc) if first_pair else refs[3 + k][...]
+        for acc in (ggt_o, gb_o, gct_o, k_o, r_o):
+            acc[...] = jnp.zeros_like(acc)
 
     base = row_base(4, [[(0, 128)], [(128, 256)], [(256, 320)], [(320, 384)]])
 
@@ -900,7 +903,7 @@
 
 
 def back_kernel(
-    length, steps, info, gmix, edge_a, edge_b, vm, normed, taps, ggain, gskip,
+    length, steps, info, gmix, edge, vm, normed, taps, ggain, gskip,
     gvals_o, keep_o, send_o, tiny_o, ext_s, vm_s, seg_s, turned_s,
 ):
     ext = length + 2 * HALO
@@ -915,7 +918,6 @@
 
     @pl.loop(0, steps)
     def _(j):
-        near = j < per
         half = j // per
         at = (j % per) * 256
         both = []
@@ -923,7 +925,8 @@
             here = pl.ds(pl.multiple_of(at + 128 * p, 128), 128)
             cols = pl.ds(pl.multiple_of(j * 256 + 128 * p, 128), 128)
             ext_s[own, :] = gmix[:, cols].astype(F32)
-            halo = jnp.where(near, edge_a[:, here].astype(F32), edge_b[:, here].astype(F32))
+            far = pl.ds(pl.multiple_of(((j + per) % steps) * 256 + 128 * p, 128), 128)
+            halo = edge[:, far].astype(F32)
             ext_s[0:HALO, :] = jnp.where(right, halo, 0.0)
             ext_s[HALO + length : ext, :] = jnp.where(right, 0.0, halo)
             vm_s[...] = vm[:, cols].astype(F32)
@@ -1297,7 +1300,6 @@
         name="front",
     )(starts, live, x, pre_gain.reshape(1, dm), w_bc, conv_bc, small_own, small_other)
 
-    wv_first, normed = lax.optimization_barrier((wv_first, normed))
     wv_over_x = flip(wv_first, 2, wide)
 
     def states(first):
@@ -1334,7 +1336,6 @@
         )(info, normed, *weights, taps, tab_a, dpt, *before)
 
     *own_vals, bnd_own = vals(False, (w_turned,), ())
-    bnd_own, wv_over_x = lax.optimization_barrier((bnd_own, wv_over_x))
     wv_pieces = wv_first, wv_over_x, flip(wv_first, 1, wide), flip(wv_over_x, 1, wide)
     xc, vm, ds, s_loc, bnd_other, wv_other = vals(True, wv_pieces, own_vals)
 
@@ -1359,23 +1360,33 @@
 
     y, s_true = scan(0, swap(bnd_other), scan(hp, swap(bnd_own), ()))
 
-    gw_shape = (2, dm // 2, dm + ch)
-    out, gy, keep_a, send_a, ggate, ggain, wg_other = pl.pallas_call(
+    out, gy, ggate, hn, ggain, wg_other, gs_loc, gbnd = pl.pallas_call(
         functools.partial(gate_kernel, nb),
         out_shape=[
-            pltpu.HBM((length, dm), BF16), act_shape, pltpu.HBM(gw_shape, BF16), pltpu.HBM(gw_shape, BF16),
-            pltpu.HBM((length, chans), BF16), sds((8, chans), F32), pltpu.HBM((ch, dm), BF16),
+            pltpu.HBM((length, dm), BF16), act_shape, act_shape, act_shape, sds((8, chans), F32), pltpu.HBM((ch, dm), BF16),
+            state_shape, sds((pairs, 64, 128), BF16),
         ],
-        in_specs=[VMEM] * 11,
-        out_specs=[HBM, VMEM, HBM, HBM, HBM, VMEM, HBM],
-        scratch_shapes=[pltpu.VMEM((length, chans), BF16), pltpu.VMEM((ch, 2 * dm), BF16)]
+        in_specs=[SMEM] + [VMEM] * 14,
+        out_specs=[HBM, VMEM, VMEM, VMEM, VMEM, HBM, VMEM, VMEM],
+        scratch_shapes=[pltpu.VMEM((ch, 2 * dm), BF16)]
         + [pltpu.VMEM((BLOCK, chans), F32)] * 4
-        + [pltpu.VMEM((length, dm), BF16), pltpu.VMEM(gw_shape, BF16), pltpu.VMEM(gw_shape, BF16)]
-        + [pltpu.VMEM((length, chans), BF16), pltpu.SemaphoreType.DMA((7,))],
-        compiler_params=params(False, 22),
-        cost_estimate=cost(17),
+        + [pltpu.VMEM((nb, BLOCK, chans), F32), pltpu.VMEM((length, dm), BF16), pltpu.SemaphoreType.DMA((2,))],
+        compiler_params=params(False, 18),
+        cost_estimate=cost(16),
         name="gated",
-    )(x, g, normed, y, wo, w_turned, *wog_pieces, gain)
+    )(info, x, g, normed, y, wo, w_turned, *wog_pieces, gain, tab_b, tab_c, dpt)
+
+    gw_shape = (2, dm // 2, dm + ch)
+    keep_a, send_a = pl.pallas_call(
+        wsum_kernel,
+        out_shape=[pltpu.HBM(gw_shape, BF16)] * 2,
+        in_specs=[VMEM] * 4,
+        out_specs=[HBM] * 2,
+        scratch_shapes=[pltpu.VMEM(gw_shape, BF16)] * 2 + [pltpu.SemaphoreType.DMA((4,))],
+        compiler_params=params(False, 10),
+        cost_estimate=cost(5),
+        name="wsum",
+    )(g, normed, hn, ggate)
 
     def meet(keep, got):
         cols = keep.shape[-1]
@@ -1398,57 +1409,29 @@
     def table(k):
         return pl.BlockSpec((None,) + sq, lambda j: (k, 0, 0, 0))
 
-    def gstate(first, before):
-        specs = [SMEM, columns(length, first), table(0), table(2), whole((128, 128), 1)] + [ANY] * len(before)
-        return pl.pallas_call(
-            functools.partial(gstate_kernel, length, first),
-            grid=(hp,),
-            out_shape=[state_shape, bnd_shape],
-            in_specs=specs,
-            out_specs=[states(first), bnd_spec],
-            input_output_aliases=aliases(specs, before),
-            compiler_params=params(True, 4),
-            cost_estimate=cost(5),
-            name="gstate_other" if first else "gstate_own",
-        )(info, gy, tab_b, tab_c, dpt, *before)
-
-    gs_loc, gbnd_own = gstate(0, ())
-    gs_loc, gbnd_other = gstate(hp, (gs_loc,))
-
-    gs_loc, gbnd_other, *a_pieces = lax.optimization_barrier((gs_loc, gbnd_other, *a_pieces))
+    sums = [whole(sq, 1), whole(sq, 1), whole(sq, 1), whole(pos, 1), whole(sq, 1)]
+    gmix, ggt, gb, gct, ksum, rsum, phi, gskip, edge = pl.pallas_call(
+        functools.partial(gscan_kernel, length),
+        grid=(pairs,),
+        out_shape=[
+            act_shape, sds(sq, F32), sds(sq, F32), sds(sq, F32), sds(pos, F32), sds(sq, F32), sds((16, chans), F32),
+            sds((8, chans), F32), sds((HALO, chans), BF16),
+        ],
+        in_specs=[
+            SMEM, columns(length), columns(length), columns(length), states(0), states(0),
+            pl.BlockSpec((1, 64, 128), lambda j: ((j + hp) % pairs, 0, 0)), whole((128, 128), 1), table(1), table(0), table(0),
+            whole((3,) + sq, 1), columns(8),
+        ],
+        out_specs=[columns(length)] + sums + [columns(16), columns(8), columns(HALO)],
+        scratch_shapes=[pltpu.VMEM((nb + 1, 128, 128), BF16)],
+        compiler_params=params(True, 8),
+        cost_estimate=cost(22),
+        name="gscan",
+    )(info, xc, ds, gy, s_true, gs_loc, swap(gbnd), dpt, tab_b, tab_a, tab_b, tab_c, skip)
+    edge = swap(edge)
+
+    gmix, *a_pieces = lax.optimization_barrier((gmix, *a_pieces))
     a_plane = plane(*a_pieces)
-
-    def gscan(first, gs0, before):
-        sums = [whole(sq, 1), whole(sq, 1), whole(sq, 1), whole(pos, 1), whole(sq, 1)]
-        specs = [
-            SMEM, columns(length, first), columns(length, first), columns(length, first), states(first), states(first),
-            bnd_spec, whole((128, 128), 1), table(1), table(0), table(0), whole((3,) + sq, 1), columns(8, first),
-        ]
-        at = len(specs)
-        if before:
-            specs += [ANY] * 3 + sums
-        return pl.pallas_call(
-            functools.partial(gscan_kernel, length, first),
-            grid=(hp,),
-            out_shape=[
-                act_shape, sds(sq, F32), sds(sq, F32), sds(sq, F32), sds(pos, F32), sds(sq, F32), sds((16, chans), F32),
-                sds((8, chans), F32), sds((HALO, ch), BF16),
-            ],
-            in_specs=specs,
-            out_specs=[columns(length, first)] + sums + [columns(16, first), columns(8, first), columns(HALO)],
-            scratch_shapes=[pltpu.VMEM((nb + 1, 128, 128), BF16)],
-            input_output_aliases={at: 0, at + 1: 6, at + 2: 7} if before else {},
-            compiler_params=params(True, 7),
-            cost_estimate=cost(17),
-            name="gscan_other" if first else "gscan_own",
-        )(info, xc, ds, gy, s_true, gs_loc, gs0, dpt, tab_b, tab_a, tab_b, tab_c, skip, *before)
-
-    gmix, ggt, gb, gct, ksum, rsum, phi, gskip, edge_other = gscan(hp, swap(gbnd_own), ())
-    gmix, ggt, gb, gct, ksum, rsum, phi, gskip, edge_own = gscan(
-        0, swap(gbnd_other), (gmix, phi, gskip, ggt, gb, gct, ksum, rsum)
-    )
-
-    gmix, ggt, a_plane = lax.optimization_barrier((gmix, ggt, a_plane))
 
     gmb, gv, small, edge_bc = pl.pallas_call(
         functools.partial(join_kernel, length, heads),
@@ -1461,13 +1444,12 @@
         name="join",
     )(info, ggt, gb, gct, ksum, rsum, phi, maps, dsl, sig)
 
-    edge_a, edge_b = swap(edge_other), swap(edge_own)
     edge_bc = swap(edge_bc)
     sum_shape = (2, dm // 2, ch)
     gvals, keep_v, send_v, tiny = pl.pallas_call(
         functools.partial(back_kernel, length, pairs // 2),
         out_shape=[act_shape, sds(sum_shape, BF16), sds(sum_shape, BF16), sds((2, 16, ch), F32)],
-        in_specs=[SMEM] + [VMEM] * 8,
+        in_specs=[SMEM] + [VMEM] * 7,
         out_specs=[VMEM] * 4,
         scratch_shapes=[
             pltpu.VMEM((ext, 128), F32), pltpu.VMEM((ext, 128), F32), pltpu.VMEM((ext, 128), jnp.int32),
@@ -1476,7 +1458,7 @@
         compiler_params=params(False, 10),
         cost_estimate=cost(12),
         name="back",
-    )(info, gmix, edge_a, edge_b, vm, normed, taps, ggain, gskip)
+    )(info, gmix, edge, vm, normed, taps, ggain, gskip)
 
     got_v = flip(send_v, 1, wide)
     keep_bc, send_bc, tiny, grad_in = pl.pallas_call(

time: 185 us -> 174 us (0.941)
  local copies, waits for them, and re-layouts: 11.7 us -> 3.88 us
  starting transfers between devices: 19.6 us -> 17.4 us
    unnamed x104 -> x34, local copies, waits for them, and re-layouts: 9.72 us -> 1.96 us
    ppermute x11 -> x9, waiting for transfers between devices: 6.69 us -> 9.03 us  [swap(): return lax.ppermute(v, 'narrow', [(0, 1), (1, 0)])]
    ppermute x11 -> x9, starting transfers between devices: 13.2 us -> 11.8 us  [swap(): return lax.ppermute(v, 'narrow', [(0, 1), (1, 0)])]
    pallas_call x4 -> x2, Pallas kernels: 27.5 us -> 27.5 us  [the longest x1 22.2 us: split_positions(): pl.pallas_call(functools.partial(gscan_kernel, length), grid=(pairs,), ou...]
  transfers between devices with their start and end apart: 21 -> 19, of which waited for: 4 -> 4; matrix products, arithmetic and copies ran while one was open for 3% -> 3% of each run, Pallas kernels for 41% -> 51%
where the time goes in v1:
time: 174 us; the launch traced here: 173 us
  Pallas kernels  139 us (80%)
  starting transfers between devices  17.4 us (10%)
  waiting for transfers between devices  9.69 us (6%)
  local copies, waits for them, and re-layouts  3.88 us (2%)
  other arithmetic  2.77 us (2%)
    pallas_call x1, Pallas kernels, split_positions(): pl.pallas_call(collect_kernel, out_shape=[sds((share, cols), F32), sds((1...  30.3 us
    pallas_call x1, Pallas kernels, split_positions(): pl.pallas_call(functools.partial(gscan_kernel, length), grid=(pairs,), ou...  22.2 us
    pallas_call x2, Pallas kernels, scan(): pl.pallas_call(functools.partial(scan_kernel, length, first), grid=(hp,),...  15.7 us
    pallas_call x1, Pallas kernels, split_positions(): pl.pallas_call(functools.partial(gate_kernel, nb), out_shape=[pltpu.HBM((...  15.5 us
    pallas_call x1, Pallas kernels, split_positions(): pl.pallas_call(functools.partial(back_kernel, length, pairs // 2), out_sh...  13.2 us
    pallas_call x2, Pallas kernels, vals(): pl.pallas_call(functools.partial(vals_kernel, length, other), grid=(steps...  12.8 us
    ppermute x9, starting transfers between devices, swap(): return lax.ppermute(v, 'narrow', [(0, 1), (1, 0)])  11.8 us
    ppermute x9, waiting for transfers between devices, swap(): return lax.ppermute(v, 'narrow', [(0, 1), (1, 0)])  9.03 us
  transfers between devices with their start and end apart: 19, of which 4 were waited for; matrix products, arithmetic and copies ran while one was open for 3% of the time, Pallas kernels for 51%

profile of v1, /device:TPU:0, one launch (start us, length us, event | category | flops | bytes accessed | tf_op | source)
XLA Modules:
  0.0 173.5 jit_solution(4048426437189728008)
XLA Ops:
  0.6 0.0 copy-start
  0.7 1.9 %small.1.small_a = f32[48,768]{1,0:T(8,128)} custom-call(f32[12,7,64]{2,1,0:T(8,128)} %bitcast.67, f32[12,64]{1,0:T(8,128)} %gain.1, f32[2,12]{1,0:T(2,128)} %bitcast.70, f32[12]{0:T(128)} %alog.1, f32[12]{0:T(128)} %skip.1, bf16[12,130,768]{2,1,0:T(8,128)(2,1)} %bitcast.48, bf16[640,768]{1,0:T(8,128)(2,1)} %bitcast.54, bf16[640,768]{1,0:T(8,128)(2,1)} %bitcast.55), custom_call_target="tpu_custom_call" | custom-call | flops 2200000000 | bytes 2000000 | tf_op jit(solution)/shard_map/small/pallas_call | solution.py:1247
  2.5 3.0 %collective-permute-start = (f32[48,768]{1,0:T(8,128)}, f32[48,768]{1,0:T(8,128)}, u32[]{:S(2)}, u32[]{:S(2)}) collective-permute-start(f32[48,768]{1,0:T(8,128)} %small.1.small_a), channel_id=1, source_target_pairs={{0,1},{1,0},{2,3},{3,2},{4,5},{5,4},{6,7},{7,6},{8,9},{9,8},{10,11... | collective-permute-start | bytes 442376 | tf_op jit(solution)/shard_map/ppermute | solution.py:1207
  5.5 0.9 constant_dynamic-slice_fusion
  6.4 0.0 copy-start.8
  6.4 0.1 collective-permute-start.1
  6.5 1.1 constant_dynamic-slice_fusion.1
  7.5 1.8 %pad_maximum_fusion = bf16[192,1536]{1,0:T(8,128)(2,1)} fusion(bf16[192,768]{1,0:T(8,128)(2,1)} %bitcast.64, bf16[192,768]{1,0:T(8,128)(2,1)S(1)} %constant_dynamic-slice_fusion.1), kind=kLoop, calls=%fused_computation.9 | loop fusion | flops 1179648 | bytes 1179648 | tf_op jit(solution)/shard_map/concatenate | solution.py:1274
  9.3 1.9 %collective-permute-start.7 = (bf16[192,1536]{1,0:T(8,128)(2,1)}, bf16[192,1536]{1,0:T(8,128)(2,1)}, u32[]{:S(2)}, u32[]{:S(2)}) collective-permute-start(bf16[192,1536]{1,0:T(8,128)(2,1)} %pad_maximum_fusion), channel_id=1, source_target_pairs={{0,1},{1,0},{2,3},{3,2},{4,5},{5,4},{6,7},{7,6},{8,9},{9,8},{10,11... | collective-permute-start | bytes 1769480 | tf_op jit(solution)/shard_map/ppermute | solution.py:1207
  11.3 5.4 %collective-permute-done.1.refs_0_ = bf16[192,768]{1,0:T(8,128)(2,1)} collective-permute-done((bf16[192,768]{1,0:T(8,128)(2,1)}, bf16[192,768]{1,0:T(8,128)(2,1)}, u32[]{:S(2)}, u32[]{:S(2)}) %collective-permute-start.1) | collective-permute-done | bytes 294944 | tf_op jit(solution)/shard_map/ppermute | solution.py:1207
  16.6 2.0 %collective-permute-start.2 = (bf16[192,768]{1,0:T(8,128)(2,1)}, bf16[192,768]{1,0:T(8,128)(2,1)S(1)}, u32[]{:S(2)}, u32[]{:S(2)}) collective-permute-start(bf16[192,768]{1,0:T(8,128)(2,1)} %collective-permute-done.1.refs_0_), channel_id=1, source_target_pairs={{0,4},{2,6},{4,0},{6,2},{8,12},{10,14},{12,8},{14,10},{16,20},{18,... | collective-permute-start | bytes 884744 | tf_op jit(solution)/shard_map/ppermute | solution.py:1211
  18.6 0.0 collective-permute-done.small_b
  18.7 0.0 copy-start.4
  18.7 1.0 copy-done.4
  19.7 0.9 copy-done.5
  20.6 7.1 %front.1 = (s32[8]{0:T(128)S(1)}, f32[8,1536]{1,0:T(8,128)S(1)}, f32[8,1536]{1,0:T(8,128)S(1)}, f32[8,1536]{1,0:T(8,128)S(1)}, bf16[128,768]{1,0:T(8,128)(2,1)S(...) custom-call(s32[1,4]{1,0:T(1,128)S(1)} %copy-done.8, ...), custom_call_target="tpu_custom_call" | custom-call | flops 6600000000 | bytes 6000000 | tf_op jit(solution)/shard_map/front/pallas_call | solution.py:1286
  27.6 0.1 collective-permute-start.3
  27.7 0.0 collective-permute-done.2.refs_1_
  27.7 0.5 collective-permute-start.4
  28.2 6.1 %vals_own.1 = (bf16[640,1536]{1,0:T(8,128)(2,1)S(1)}, bf16[672,1536]{1,0:T(8,128)(2,1)S(1)}, bf16[640,1536]{1,0:T(8,128)(2,1)S(1)}, bf16[12,6,128,128]{3,2,1,0:T(8,128)(2,1)S(1)}, bf16[6,64,128]{2,1,0:T(8,128)(2,1)S(1)}) custom-call(s32[8]{0:T(128)S(1)} %get-tuple-element.93.info, bf16[672,768]{1,0:T(8,128)(2,1)S(1)} %get-tuple-element.94.normed, ...), custom_call_target="tpu_custom_call" | custom-call | flops 9900000256 | bytes 9000000 | tf_op jit(solution)/shard_map/vals_own/pallas_call | solution.py:1321
  34.4 1.8 %collective-permute-start.6 = (bf16[6,64,128]{2,1,0:T(8,128)(2,1)S(1)}, bf16[6,64,128]{2,1,0:T(8,128)(2,1)S(1)}, u32[]{:S(2)}, u32[]{:S(2)}) collective-permute-start(bf16[6,64,128]{2,1,0:T(8,128)(2,1)S(1)} %get-tuple-element.107), channel_id=1, source_target_pairs={{0,1},{1,0},{2,3},{3,2},{4,5},{5,4},{6,7},{7,6},{8,9},{9,8},{10,11... | collective-permute-start | bytes 294920 | tf_op jit(solution)/shard_map/ppermute | solution.py:1207
  36.1 0.0 collective-permute-done.7.p0
  36.1 0.0 collective-permute-start.9
  36.1 0.5 collective-permute-start.8
  36.7 0.0 collective-permute-done.3.refs_2_
  36.7 0.0 collective-permute-done.4.refs_3_
  36.7 6.7 %vals_other.1 = (bf16[640,1536]{1,0:T(8,128)(2,1)S(1)}, bf16[672,1536]{1,0:T(8,128)(2,1)S(1)}, bf16[640,1536]{1,0:T(8,128)(2,1)S(1)}, bf16[12,6,128,128]{3,2,1,0...) custom-call(s32[8]{0:T(128)S(1)} %get-tuple-element.93.info, ...), custom_call_target="tpu_custom_call", output_to_operand_aliasing={{0}: (9, {}), {1}: (10, {}), {2}: (11, {}), {3}: (12, {})} | custom-call | flops 9900000256 | bytes 9000000 | tf_op jit(solution)/shard_map/vals_other/pallas_call | solution.py:1321
  43.4 0.2 collective-permute-start.5
  43.6 0.0 collective-permute-done.6.s0_ref
  43.6 7.8 %scan_other.1 = (bf16[640,1536]{1,0:T(8,128)(2,1)S(1)}, bf16[12,6,128,128]{3,2,1,0:T(8,128)(2,1)S(1)}) custom-call(s32[8]{0:T(128)S(1)} %get-tuple-element.93.info, bf16[640,1536]{1,0:T(8,128)(2,1)S(1)} %get-tuple-element.102.xc_ref, bf16[12,6,128,128]{3,2,1,0:T(8,128)(2,1)S(1)} %get-tuple-element.103.s_ref, ...), custom_call_target="tpu_custom_call" | custom-call | flops 11000000512 | bytes 10000000 | tf_op jit(solution)/shard_map/scan_other/pallas_call | solution.py:1349
  51.4 0.6 collective-permute-done.8.p1
  52.1 0.0 collective-permute-start.10
  52.1 0.0 collective-permute-done.5.s0_ref
  52.1 0.0 copy-start.3
  52.1 0.0 copy-start.12
  52.1 7.9 %scan_own.1 = (bf16[640,1536]{1,0:T(8,128)(2,1)S(1)}, bf16[12,6,128,128]{3,2,1,0:T(8,128)(2,1)S(1)}) custom-call(s32[8]{0:T(128)S(1)} %get-tuple-element.93.info, bf16[640,1536]{1,0:T(8,128)(2,1)S(1)} %get-tuple-element.102.xc_ref, bf16[12,6,128,128]{3,2,1,0:T(8,128)(2,1)S(1)} %get-tuple-element.103.s_ref, ...), custom_call_target="tpu_custom_call", output_to_operand_aliasing={{0}: (7, {}), {1}: (8, {})} | custom-call | flops 11000000512 | bytes 10000000 | tf_op jit(solution)/shard_map/scan_own/pallas_call | solution.py:1349
  60.0 0.0 collective-permute-done.9.p2
  60.0 0.0 collective-permute-done.10.p3
  60.0 15.5 %gated.1 = (bf16[640,768]{1,0:T(8,128)(2,1)}, bf16[640,1536]{1,0:T(8,128)(2,1)S(1)}, bf16[640,1536]{1,0:T(8,128)(2,1)S(1)}, bf16[640,1536]{1,0:T(8,128)(2,1)S(1)...) custom-call(s32[8]{0:T(128)S(1)} %get-tuple-element.93.info, ...), custom_call_target="tpu_custom_call" | custom-call | flops 17600000000 | bytes 16000000 | tf_op jit(solution)/shard_map/gated/pallas_call | solution.py:1363
  75.5 1.4 collective-permute-start.11
  76.9 5.3 %wsum.1 = (bf16[2,384,1536]{2,1,0:T(8,128)(2,1)}, bf16[2,384,1536]{2,1,0:T(8,128)(2,1)}) custom-call(bf16[640,768]{1,0:T(8,128)(2,1)S(1)} %bitcast.60, bf16[672,768]{1,0:T(8,128)(2,1)S(1)} %get-tuple-element.94.normed, bf16[640,1536]{1,0:T(8,128)(2,1)S(1)} %get-tuple-element.120.hn, bf16[640,1536]{1,0:T(8,128)(2,1)S(1)} %get-tuple-element.121.ggate), custom_call_target="tpu_custom_call" | custom-call | flops 5500000256 | bytes 5000000 | tf_op jit(solution)/shard_map/wsum/pallas_call | solution.py:1380
  82.2 0.3 collective-permute-start.12
  82.5 0.4 collective-permute-done.11.gs0_ref
  82.9 22.2 %gscan.1 = (bf16[640,1536]{1,0:T(8,128)(2,1)S(1)}, f32[5,128,128]{2,1,0:T(8,128)S(1)}, f32[5,128,128]{2,1,0:T(8,128)S(1)}, f32[5,128,128]{2,1,0:T(8,128)S(1)}, f...) custom-call(s32[8]{0:T(128)S(1)} %get-tuple-element.93.info, ...), custom_call_target="tpu_custom_call" | custom-call | flops 24199999488 | bytes 22000000 | tf_op jit(solution)/shard_map/gscan/pallas_call | solution.py:1413
  105.2 4.1 %join.1 = (f32[672,256]{1,0:T(8,128)S(1)}, bf16[640,128]{1,0:T(8,128)(2,1)S(1)}, f32[16,128]{1,0:T(8,128)S(1)}, f32[16,256]{1,0:T(8,128)S(1)}) custom-call(s32[8]{0:T(128)S(1)} %get-tuple-element.93.info, f32[5,128,128]{2,1,0:T(8,128)S(1)} %get-tuple-element.132.ggt, f32[5,128,128]{2,1,0:T(8,128)S(1)} %get-tuple-element.133.gb, ...), custom_call_target="tpu_custom_call" | custom-call | flops 6600000000 | bytes 6000000 | tf_op jit(solution)/shard_map/join/pallas_call | solution.py:1436
  109.2 1.2 collective-permute-start.14
  110.4 0.9 collective-permute-start.13
  111.3 0.0 collective-permute-done.12
  111.3 0.7 fusion.3
  111.9 1.3 collective-permute-start.16
  113.2 1.4 collective-permute-start.17
  114.7 0.8 collective-permute-start.18
  115.5 0.0 collective-permute-done.13.edge
  115.5 13.2 %back.1 = (bf16[640,1536]{1,0:T(8,128)(2,1)S(1)}, bf16[2,384,768]{2,1,0:T(8,128)(2,1)S(1)}, bf16[2,384,768]{2,1,0:T(8,128)(2,1)S(1)}, f32[2,16,768]{2,1,0:T(8,128)S(1)}) custom-call(s32[8]{0:T(128)S(1)} %get-tuple-element.93.info, bf16[640,1536]{1,0:T(8,128)(2,1)S(1)} %get-tuple-element.124.gmix, bf16[16,1536]{1,0:T(8,128)(2,1)S(1)} %collective-permute-done.13.edge, ...), custom_call_target="tpu_custom_call" | custom-call | flops 13200000000 | bytes 12000000 | tf_op jit(solution)/shard_map/back/pallas_call | solution.py:1449
  128.7 0.1 collective-permute-start.15
  128.8 0.0 collective-permute-done.14.edge
  128.8 8.5 %last.1 = (bf16[2,384,384]{2,1,0:T(8,128)(2,1)S(1)}, bf16[2,384,384]{2,1,0:T(8,128)(2,1)S(1)}, f32[2,16,768]{2,1,0:T(8,128)S(1)}, f32[640,768]{1,0:T(8,128)}) custom-call(s32[8]{0:T(128)S(1)} %get-tuple-element.93.info, bf16[640,1536]{1,0:T(8,128)(2,1)S(1)} %get-tuple-element.129.gvals, bf16[640,1536]{1,0:T(8,128)(2,1)S(1)} %get-tuple-element.121.ggate, ...), custom_call_target="tpu_custom_call" | custom-call | flops 8800000000 | bytes 8000000 | tf_op jit(solution)/shard_map/last/pallas_call | solution.py:1464
  137.4 0.0 collective-permute-done.16
  137.4 3.2 %collective-permute-done.17 = bf16[4,48,1536]{2,1,0:T(8,128)(2,1)S(1)} collective-permute-done((bf16[4,48,1536]{2,1,0:T(8,128)(2,1)S(1)}, bf16[4,48,1536]{2,1,0:T(8,128)(2,1)S(1)}, u32[]{:S(2)}, u32[]{:S(2)}) %collective-permute-start.17) | collective-permute-done | bytes 589856 | tf_op jit(solution)/shard_map/ppermute | solution.py:1207
  140.6 0.0 collective-permute-done.18
  140.6 0.3 add_convert_fusion.plane_a
  140.9 0.0 collective-permute-done.15.got_v
  140.9 30.3 %collect.1 = (f32[48,1152]{1,0:T(8,128)S(1)}, f32[16,768]{1,0:T(8,128)S(1)}, f32[48,1536]{1,0:T(8,128)S(1)}) custom-call(bf16[2,384,768]{2,1,0:T(8,128)(2,1)S(1)} %get-tuple-element.152.keep, bf16[2,384,768]{2,1,0:T(8,128)(2,1)S(1)} %collective-permute-done.15.got_v, bf16[2,384,384]{2,1,0:T(8,128)(2,1)S(1)} %get-tuple-element.154.keep_bc, ...), custom_call_target="tpu_custom_call" | custom-call | tf_op jit(solution)/shard_map/collect/pallas_call | solution.py:1483
  171.2 2.2 %finish.1 = (f32[12,48,130]{2,1,0:T(8,128)}, f32[12,48,64]{2,1,0:T(8,128)}, f32[48,256]{1,0:T(8,128)}, f32[7,4,12]{2,1,0:T(4,128)}, f32[7,16]{1,0:T(8,128)}, /*i...) custom-call(f32[16,768]{1,0:T(8,128)S(1)} %get-tuple-element.161.tiny, ...), custom_call_target="tpu_custom_call" | custom-call | tf_op jit(solution)/shard_map/finish/pallas_call | solution.py:1512
  (28 shorter events, 0.1 us)
Async XLA Ops:
  0.6 4.8 %copy-start = (bf16[768,12,130]{0,2,1:T(8,128)(2,1)S(1)}, bf16[768,12,130]{0,2,1:T(8,128)(2,1)}, u32[]{:S(2)}) copy-start(bf16[768,12,130]{0,2,1:T(8,128)(2,1)} %param.16) | copy-start | bytes 7188484
  2.5 16.1 %collective-permute-start = (f32[48,768]{1,0:T(8,128)}, f32[48,768]{1,0:T(8,128)}, u32[]{:S(2)}, u32[]{:S(2)}) collective-permute-start(f32[48,768]{1,0:T(8,128)} %small.1.small_a), channel_id=1, source_target_pairs={{0,1},{1,0},{2,3},{3,2},{4,5},{5,4},{6,7},{7,6},{8,9},{9,8},{10,11... | collective-permute-start | bytes 442376 | tf_op jit(solution)/shard_map/ppermute | solution.py:1207
  6.3 4.9 %copy-start.16 = (f32[768]{0:T(1024)S(1)}, f32[768]{0:T(1024)}, u32[]{:S(2)}) copy-start(f32[768]{0:T(1024)} %param.15) | copy-start | bytes 9220
  6.3 12.3 %copy-start.2 = (bf16[1,640,768]{2,1,0:T(8,128)(2,1)S(1)}, bf16[1,640,768]{2,1,0:T(8,128)(2,1)}, u32[]{:S(2)}) copy-start(bf16[1,640,768]{2,1,0:T(8,128)(2,1)} %param.14) | copy-start | bytes 2949124
  6.3 12.3 %copy-start.6 = (f32[7,256]{1,0:T(8,128)S(1)}, f32[7,256]{1,0:T(8,128)}, u32[]{:S(2)}) copy-start(f32[7,256]{1,0:T(8,128)} %taps_ref.1) | copy-start | bytes 21508
  6.3 12.3 %copy-start.7 = (s32[1,1280]{1,0:T(1,128)S(1)}, s32[1,1280]{1,0:T(1,128)}, u32[]{:S(2)}) copy-start(s32[1,1280]{1,0:T(1,128)} %live_ref.1) | copy-start | bytes 15364
  6.4 12.3 %copy-start.8 = (s32[1,4]{1,0:T(1,128)S(1)}, s32[1,4]{1,0:T(1,128)}, u32[]{:S(2)}) copy-start(s32[1,4]{1,0:T(1,128)} %starts.1) | copy-start | bytes 52
  6.4 10.3 %collective-permute-start.1 = (bf16[192,768]{1,0:T(8,128)(2,1)}, bf16[192,768]{1,0:T(8,128)(2,1)}, u32[]{:S(2)}, u32[]{:S(2)}) collective-permute-start(bf16[192,768]{1,0:T(8,128)(2,1)} %bitcast.6), channel_id=1, source_target_pairs={{0,1},{1,0},{2,3},{3,2},{4,5},{5,4},{6,7},{7,6},{8,9},{9,8},{10,11... | collective-permute-start | bytes 884744 | tf_op jit(solution)/shard_map/ppermute | solution.py:1207
  9.3 26.8 %collective-permute-start.7 = (bf16[192,1536]{1,0:T(8,128)(2,1)}, bf16[192,1536]{1,0:T(8,128)(2,1)}, u32[]{:S(2)}, u32[]{:S(2)}) collective-permute-start(bf16[192,1536]{1,0:T(8,128)(2,1)} %pad_maximum_fusion), channel_id=1, source_target_pairs={{0,1},{1,0},{2,3},{3,2},{4,5},{5,4},{6,7},{7,6},{8,9},{9,8},{10,11... | collective-permute-start | bytes 1769480 | tf_op jit(solution)/shard_map/ppermute | solution.py:1207
  16.6 11.1 %collective-permute-start.2 = (bf16[192,768]{1,0:T(8,128)(2,1)}, bf16[192,768]{1,0:T(8,128)(2,1)S(1)}, u32[]{:S(2)}, u32[]{:S(2)}) collective-permute-start(bf16[192,768]{1,0:T(8,128)(2,1)} %collective-permute-done.1.refs_0_), channel_id=1, source_target_pairs={{0,4},{2,6},{4,0},{6,2},{8,12},{10,14},{12,8},{14,10},{16,20},{18,... | collective-permute-start | bytes 884744 | tf_op jit(solution)/shard_map/ppermute | solution.py:1211
  18.7 1.0 copy-start.4
  19.7 0.9 copy-start.5
  27.6 9.0 %collective-permute-start.3 = (bf16[192,768]{1,0:T(8,128)(2,1)}, bf16[192,768]{1,0:T(8,128)(2,1)S(1)}, u32[]{:S(2)}, u32[]{:S(2)}) collective-permute-start(bf16[192,768]{1,0:T(8,128)(2,1)} %collective-permute-done.1.refs_0_), channel_id=1, source_target_pairs={{0,2},{2,0},{4,6},{6,4},{8,10},{10,8},{12,14},{14,12},{16,18},{18,... | collective-permute-start | bytes 884744 | tf_op jit(solution)/shard_map/ppermute | solution.py:1211
  27.7 8.9 %collective-permute-start.4 = (bf16[192,768]{1,0:T(8,128)(2,1)S(1)}, bf16[192,768]{1,0:T(8,128)(2,1)S(1)}, u32[]{:S(2)}, u32[]{:S(2)}) collective-permute-start(bf16[192,768]{1,0:T(8,128)(2,1)S(1)} %collective-permute-done.2.refs_1_), channel_id=1, source_target_pairs={{0,2},{2,0},{4,6},{6,4},{8,10},{10,8},{12,14},{14,12},{16,18},{18,... | collective-permute-start | bytes 884744 | tf_op jit(solution)/shard_map/ppermute | solution.py:1211
  34.4 9.2 %collective-permute-start.6 = (bf16[6,64,128]{2,1,0:T(8,128)(2,1)S(1)}, bf16[6,64,128]{2,1,0:T(8,128)(2,1)S(1)}, u32[]{:S(2)}, u32[]{:S(2)}) collective-permute-start(bf16[6,64,128]{2,1,0:T(8,128)(2,1)S(1)} %get-tuple-element.107), channel_id=1, source_target_pairs={{0,1},{1,0},{2,3},{3,2},{4,5},{5,4},{6,7},{7,6},{8,9},{9,8},{10,11... | collective-permute-start | bytes 294920 | tf_op jit(solution)/shard_map/ppermute | solution.py:1207
  36.1 23.9 %collective-permute-start.9 = (bf16[192,1536]{1,0:T(8,128)(2,1)}, bf16[192,1536]{1,0:T(8,128)(2,1)S(1)}, u32[]{:S(2)}, u32[]{:S(2)}) collective-permute-start(bf16[192,1536]{1,0:T(8,128)(2,1)} %collective-permute-done.7.p0), channel_id=1, source_target_pairs={{0,2},{2,0},{4,6},{6,4},{8,10},{10,8},{12,14},{14,12},{16,18},{18,... | collective-permute-start | bytes 1769480 | tf_op jit(solution)/shard_map/ppermute | solution.py:1211
  36.1 16.0 %collective-permute-start.8 = (bf16[192,1536]{1,0:T(8,128)(2,1)}, bf16[192,1536]{1,0:T(8,128)(2,1)S(1)}, u32[]{:S(2)}, u32[]{:S(2)}) collective-permute-start(bf16[192,1536]{1,0:T(8,128)(2,1)} %collective-permute-done.7.p0), channel_id=1, source_target_pairs={{0,4},{2,6},{4,0},{6,2},{8,12},{10,14},{12,8},{14,10},{16,20},{18,... | collective-permute-start | bytes 1769480 | tf_op jit(solution)/shard_map/ppermute | solution.py:1211
  43.4 8.7 %collective-permute-start.5 = (bf16[6,64,128]{2,1,0:T(8,128)(2,1)S(1)}, bf16[6,64,128]{2,1,0:T(8,128)(2,1)S(1)}, u32[]{:S(2)}, u32[]{:S(2)}) collective-permute-start(bf16[6,64,128]{2,1,0:T(8,128)(2,1)S(1)} %get-tuple-element.104), channel_id=1, source_target_pairs={{0,1},{1,0},{2,3},{3,2},{4,5},{5,4},{6,7},{7,6},{8,9},{9,8},{10,11... | collective-permute-start | bytes 294920 | tf_op jit(solution)/shard_map/ppermute | solution.py:1207
  52.1 7.9 %collective-permute-start.10 = (bf16[192,1536]{1,0:T(8,128)(2,1)S(1)}, bf16[192,1536]{1,0:T(8,128)(2,1)S(1)}, u32[]{:S(2)}, u32[]{:S(2)}) collective-permute-start(bf16[192,1536]{1,0:T(8,128)(2,1)S(1)} %collective-permute-done.8.p1), channel_id=1, source_target_pairs={{0,2},{2,0},{4,6},{6,4},{8,10},{10,8},{12,14},{14,12},{16,18},{18,... | collective-permute-start | bytes 1769480 | tf_op jit(solution)/shard_map/ppermute | solution.py:1211
  52.1 7.9 %copy-start.1 = (bf16[12,64,768]{2,1,0:T(8,128)(2,1)S(1)}, bf16[12,64,768]{2,1,0:T(8,128)(2,1)}, u32[]{:S(2)}) copy-start(bf16[12,64,768]{2,1,0:T(8,128)(2,1)} %param.24) | copy-start | bytes 3538948
  52.1 7.9 %copy-start.3 = (bf16[1,640,768]{2,1,0:T(8,128)(2,1)S(1)}, bf16[1,640,768]{2,1,0:T(8,128)(2,1)}, u32[]{:S(2)}) copy-start(bf16[1,640,768]{2,1,0:T(8,128)(2,1)} %param.25) | copy-start | bytes 2949124
  52.1 7.9 %copy-start.12 = (f32[3,5,128,128]{3,2,1,0:T(8,128)S(1)}, f32[3,5,128,128]{3,2,1,0:T(8,128)}, u32[]{:S(2)}) copy-start(f32[3,5,128,128]{3,2,1,0:T(8,128)} %get-tuple-element.112.tc) | copy-start | bytes 2949124
  75.5 7.4 %collective-permute-start.11 = (bf16[12,64,128]{2,1,0:T(8,128)(2,1)S(1)}, bf16[12,64,128]{2,1,0:T(8,128)(2,1)S(1)}, u32[]{:S(2)}, u32[]{:S(2)}) collective-permute-start(bf16[12,64,128]{2,1,0:T(8,128)(2,1)S(1)} %get-tuple-element.118), channel_id=1, source_target_pairs={{0,1},{1,0},{2,3},{3,2},{4,5},{5,4},{6,7},{7,6},{8,9},{9,8},{10,11... | collective-permute-start | bytes 589832 | tf_op jit(solution)/shard_map/ppermute | solution.py:1207
  82.2 29.0 %collective-permute-start.12 = (bf16[2,384,1536]{2,1,0:T(8,128)(2,1)}, bf16[2,384,1536]{2,1,0:T(8,128)(2,1)S(1)}, u32[]{:S(2)}, u32[]{:S(2)}) collective-permute-start(bf16[2,384,1536]{2,1,0:T(8,128)(2,1)} %get-tuple-element.123), channel_id=1, source_target_pairs={{0,2},{2,0},{4,6},{6,4},{8,10},{10,8},{12,14},{14,12},{16,18},{18,... | collective-permute-start | bytes 7077896 | tf_op jit(solution)/shard_map/ppermute | solution.py:1211
  82.9 22.2 %copy-start.10 = (f32[640,384]{1,0:T(8,128)S(1)}, f32[640,384]{1,0:T(8,128)}, u32[]{:S(2)}) copy-start(f32[640,384]{1,0:T(8,128)} %get-tuple-element.140.sig) | copy-start | bytes 2949124
  82.9 22.2 %copy-start.13 = (f32[672,256]{1,0:T(8,128)S(1)}, f32[672,256]{1,0:T(8,128)}, u32[]{:S(2)}) copy-start(f32[672,256]{1,0:T(8,128)} %get-tuple-element.139.dsl) | copy-start | bytes 2064388
  82.9 22.2 %copy-start.14 = (bf16[640,256]{1,0:T(8,128)(2,1)S(1)}, bf16[640,256]{1,0:T(8,128)(2,1)}, u32[]{:S(2)}) copy-start(bf16[640,256]{1,0:T(8,128)(2,1)} %get-tuple-element.138.maps) | copy-start | bytes 983044
  105.2 6.1 %copy-start.15 = (bf16[2,384,1536]{2,1,0:T(8,128)(2,1)S(1)}, bf16[2,384,1536]{2,1,0:T(8,128)(2,1)}, u32[]{:S(2)}) copy-start(bf16[2,384,1536]{2,1,0:T(8,128)(2,1)} %get-tuple-element.122) | copy-start | bytes 7077892
  109.2 19.6 %collective-permute-start.14 = (f32[16,256]{1,0:T(8,128)S(1)}, f32[16,256]{1,0:T(8,128)S(1)}, u32[]{:S(2)}, u32[]{:S(2)}) collective-permute-start(f32[16,256]{1,0:T(8,128)S(1)} %get-tuple-element.142), channel_id=1, source_target_pairs={{0,1},{1,0},{2,3},{3,2},{4,5},{5,4},{6,7},{7,6},{8,9},{9,8},{10,11... | collective-permute-start | bytes 49160 | tf_op jit(solution)/shard_map/ppermute | solution.py:1207
  110.4 5.1 %collective-permute-start.13 = (bf16[16,1536]{1,0:T(8,128)(2,1)S(1)}, bf16[16,1536]{1,0:T(8,128)(2,1)S(1)}, u32[]{:S(2)}, u32[]{:S(2)}) collective-permute-start(bf16[16,1536]{1,0:T(8,128)(2,1)S(1)} %get-tuple-element.125), channel_id=1, source_target_pairs={{0,1},{1,0},{2,3},{3,2},{4,5},{5,4},{6,7},{7,6},{8,9},{9,8},{10,11... | collective-permute-start | bytes 147464 | tf_op jit(solution)/shard_map/ppermute | solution.py:1207
  111.9 25.4 %collective-permute-start.16 = (bf16[4,48,1536]{2,1,0:T(8,128)(2,1)S(1)}, bf16[4,48,1536]{2,1,0:T(8,128)(2,1)S(1)}, u32[]{:S(2)}, u32[]{:S(2)}) collective-permute-start(bf16[4,48,1536]{2,1,0:T(8,128)(2,1)S(1)} %get-tuple-element.158), channel_id=1, source_target_pairs={{0,4},{2,6},{4,0},{6,2},{8,12},{10,14},{12,8},{14,10},{16,20},{18,... | collective-permute-start | bytes 1769480 | tf_op jit(solution)/shard_map/ppermute | solution.py:1211
  113.2 27.4 %collective-permute-start.17 = (bf16[4,48,1536]{2,1,0:T(8,128)(2,1)S(1)}, bf16[4,48,1536]{2,1,0:T(8,128)(2,1)S(1)}, u32[]{:S(2)}, u32[]{:S(2)}) collective-permute-start(bf16[4,48,1536]{2,1,0:T(8,128)(2,1)S(1)} %get-tuple-element.159), channel_id=1, source_target_pairs={{0,1},{1,0},{2,3},{3,2},{4,5},{5,4},{6,7},{7,6},{8,9},{9,8},{10,11... | collective-permute-start | bytes 1769480 | tf_op jit(solution)/shard_map/ppermute | solution.py:1207
  114.7 25.9 %collective-permute-start.18 = (bf16[4,48,1536]{2,1,0:T(8,128)(2,1)S(1)}, bf16[4,48,1536]{2,1,0:T(8,128)(2,1)S(1)}, u32[]{:S(2)}, u32[]{:S(2)}) collective-permute-start(bf16[4,48,1536]{2,1,0:T(8,128)(2,1)S(1)} %get-tuple-element.160), channel_id=1, source_target_pairs={{0,5},{1,4},{2,7},{3,6},{4,1},{5,0},{6,3},{7,2},{8,13},{9,12},{10,... | collective-permute-start | bytes 1769480 | tf_op jit(solution)/shard_map/ppermute | solution.py:1216
  115.5 13.3 %copy-start.9 = (bf16[768,768]{1,0:T(8,128)(2,1)S(1)}, bf16[768,768]{1,0:T(8,128)(2,1)}, u32[]{:S(2)}) copy-start(bf16[768,768]{1,0:T(8,128)(2,1)} %get-tuple-element.131.wg_b) | copy-start | bytes 3538948
  115.5 13.3 %copy-start.11 = (f32[672,256]{1,0:T(8,128)S(1)}, f32[672,256]{1,0:T(8,128)}, u32[]{:S(2)}) copy-start(f32[672,256]{1,0:T(8,128)} %get-tuple-element.143.bcm) | copy-start | bytes 2064388
  128.7 12.2 %collective-permute-start.15 = (bf16[2,384,768]{2,1,0:T(8,128)(2,1)S(1)}, bf16[2,384,768]{2,1,0:T(8,128)(2,1)S(1)}, u32[]{:S(2)}, u32[]{:S(2)}) collective-permute-start(bf16[2,384,768]{2,1,0:T(8,128)(2,1)S(1)} %get-tuple-element.153), channel_id=1, source_target_pairs={{0,2},{2,0},{4,6},{6,4},{8,10},{10,8},{12,14},{14,12},{16,18},{18,... | collective-permute-start | bytes 3538952 | tf_op jit(solution)/shard_map/ppermute | solution.py:1211

commit v2 on v1

--- a/solution.py
+++ b/solution.py
@@ -688,28 +688,42 @@
         one.wait()
 
 
-def wsum_kernel(g_ref, normed, hn, ggate, keep_h, send_h, keep_o, send_o, sems):
+def wsum_kernel(g_ref, normed, hn, ggate, mine_o, x_o, y_o, d_o, keep_s, send_s, got_s, out_sem, in_sem):
     length, dm = g_ref.shape
     half = hn.shape[1] // 2
-    late = []
-
-    def send(src, dst):
-        late.append(pltpu.make_async_copy(src, dst, sems.at[len(late)]))
-        late[-1].start()
-
-    gt = g_ref[...].T
-    nt_ = normed[HALO : HALO + length, :].T
+    share = mine_o.shape[1]
+    w = lax.axis_index("wide")
+    core = (w + 1 - 2 * (w % 2), lax.axis_index("narrow"))
+    xx = (w // 2) % 2
+    mesh_ids = pl.DeviceIdType.MESH
+    barrier = pltpu.get_barrier_semaphore()
+    pl.semaphore_signal(barrier, inc=1, device_id=core, device_id_type=mesh_ids)
+    turned = (g_ref[...].T, normed[HALO : HALO + length, :].T)
+    going = []
     for k in range(2):
-        for p in range(half // 256):
-            cols = slice(k * half + p * 256, k * half + (p + 1) * 256)
-            dst = slice(p * 256, (p + 1) * 256)
-            dst2 = slice(half + p * 256, half + (p + 1) * 256)
-            by_core(mm(gt, hn[:, cols]), keep_o.at[k, :, dst], send_o.at[k, :, dst])
-            by_core(mm(nt_, ggate[:, cols]), keep_o.at[k, :, dst2], send_o.at[k, :, dst2])
-        send(send_o.at[k], send_h.at[k])
-        send(keep_o.at[k], keep_h.at[k])
-    for one in late:
+        for part, source in enumerate((hn, ggate)):
+            for p in range(half // 256):
+                cols = slice(k * half + p * 256, k * half + (p + 1) * 256)
+                dst = slice(part * half + p * 256, part * half + (p + 1) * 256)
+                by_core(mm(turned[part], source[:, cols]), keep_s.at[k, :, dst], send_s.at[k, :, dst])
+            if not going:
+                pl.semaphore_wait(barrier, 1)
+            cols = slice(part * half, (part + 1) * half)
+            one = pltpu.make_async_remote_copy(
+                src_ref=send_s.at[k, :, cols], dst_ref=got_s.at[k, :, cols], send_sem=out_sem.at[k, part],
+                recv_sem=in_sem.at[k, part], device_id=core, device_id_type=mesh_ids,
+            )
+            one.start()
+            going.append((k, cols, one))
+    for k, cols, one in going:
         one.wait()
+        near_o, far_o = ((mine_o, x_o), (y_o, d_o))[k]
+        for q in range(4):
+            rows = slice(q * 2 * share, (q + 1) * 2 * share)
+            both = (keep_s[k, rows, cols].astype(F32) + got_s[k, rows, cols].astype(F32)).astype(BF16)
+            low, high = both[0:share, :], both[share:, :]
+            near_o[q, :, cols] = jnp.where(xx == 0, low, high)
+            far_o[q, :, cols] = jnp.where(xx == 0, high, low)
 
 
 def gscan_kernel(
@@ -889,22 +903,22 @@
     own = slice(HALO, HALO + length)
     seg0 = seg_s[own, :]
     mine = grad[own, :]
+    here = data[own, :].astype(F32)
     total = mine * tap[3:4, :]
     gtap = [None] * 7
-    gtap[3] = jnp.sum(mine * data[own, :], axis=0, keepdims=True)
+    gtap[3] = jnp.sum(mine * here, axis=0, keepdims=True)
     for k in (0, 1, 2, 4, 5, 6):
         lo = HALO + 3 - k
         same = seg_s[lo : lo + length, :] == seg0
-        total = total + jnp.where(same, grad[lo : lo + length, :], 0.0) * tap[k : k + 1, :]
-        up = HALO + k - 3
-        same = seg_s[up : up + length, :] == seg0
-        gtap[k] = jnp.sum(jnp.where(same, data[up : up + length, :], 0.0) * mine, axis=0, keepdims=True)
+        moved = jnp.where(same, grad[lo : lo + length, :], 0.0)
+        total = total + moved * tap[k : k + 1, :]
+        gtap[k] = jnp.sum(moved * here, axis=0, keepdims=True)
     return jnp.where(live, total, 0.0), gtap
 
 
 def back_kernel(
     length, steps, info, gmix, edge, vm, normed, taps, ggain, gskip,
-    gvals_o, keep_o, send_o, tiny_o, ext_s, vm_s, seg_s, turned_s,
+    gvals_o, keep_o, send_o, tiny_o, ext_s, seg_s, turned_s,
 ):
     ext = length + 2 * HALO
     off, count = info[5], info[4]
@@ -929,8 +943,7 @@
             halo = edge[:, far].astype(F32)
             ext_s[0:HALO, :] = jnp.where(right, halo, 0.0)
             ext_s[HALO + length : ext, :] = jnp.where(right, 0.0, halo)
-            vm_s[...] = vm[:, cols].astype(F32)
-            gvals, gtap = back_conv(length, seg_s, live, ext_s, vm_s, taps[:, cols])
+            gvals, gtap = back_conv(length, seg_s, live, ext_s, vm[:, cols], taps[:, cols])
             both.append(gvals.astype(BF16))
             for t in range(7):
                 tiny_o[half, t : t + 1, here] = gtap[t]
@@ -940,56 +953,6 @@
         gvals_o[:, pl.ds(pl.multiple_of(j * 256, 256), 256)] = both
         here = pl.ds(pl.multiple_of(at, 256), 256)
         by_core(mm(turned_s[...], both), keep_o.at[half, :, here], send_o.at[half, :, here])
-
-
-def last_kernel(
-    length, hl, info, gvals, ggate, w_ref, wv_b, wg_b, normed, gmb, edge, bcm, taps_bc, gv, wdt, wbc, x_ref, g_ref, rs, pre,
-    small, tiny, keep_o, send_o, tiny_o, gin_o, ext_s, vm_s, seg_s,
-):
-    ext = length + 2 * HALO
-    ch = hl * HD
-    off, count = info[5], info[4]
-    own = slice(HALO, HALO + length)
-    seg_s[...] = seg_at(info, iota((ext, 128), 0) + (off - HALO))
-    live = iota((length, 128), 0) + off < count
-    tiny_o[...] = tiny[...]
-    for half in range(2):
-        tiny_o[half, 10:11, 0:128] = small[8 * half : 8 * half + 1, :]
-        tiny_o[half, 10:11, 128:256] = small[8 * half + 1 : 8 * half + 2, :]
-    both = []
-    for k in range(2):
-        cols = slice(k * 128, (k + 1) * 128)
-        ext_s[...] = gmb[:, cols]
-        lo = HALO // 2
-        hi = length + lo
-        got = edge[:, cols]
-        ext_s[lo : lo + HALO, :] += jnp.where(info[7] == 1, got, 0.0)
-        ext_s[hi : hi + HALO, :] += jnp.where(info[7] == 1, 0.0, got)
-        vm_s[...] = bcm[:, cols]
-        gbc, gtap = back_conv(length, seg_s, live, ext_s, vm_s, taps_bc[:, cols])
-        for t in range(7):
-            at = (t % 3) * 256 + k * 128
-            for half in range(2):
-                tiny_o[half, 11 + t // 3 : 12 + t // 3, at : at + 128] = gtap[t]
-        both.append(gbc.astype(BF16))
-    gbc = jnp.concatenate(both + [gv[...]], axis=1)
-    gw = tn(normed[own, :], gbc)
-    by_core(gw, keep_o.at[0], send_o.at[0])
-    turned = pltpu.roll(gw[:, 256:], 128 - hl, 1)
-    by_core(jnp.concatenate([gw[:, 0:256], turned], axis=1), keep_o.at[1], send_o.at[1])
-    wv_a = jnp.concatenate([w_ref[h, HD : 2 * HD, :] for h in range(hl)], axis=0)
-    wg_a = jnp.concatenate([w_ref[h, 0:HD, :] for h in range(hl)], axis=0)
-    gn = mm(gvals[:, 0:ch], wv_a) + mm(gvals[:, ch:], wv_b[...])
-    gn = gn + mm(ggate[:, 0:ch], wg_a) + mm(ggate[:, ch:], wg_b[...])
-    gn = gn + nt(gbc[:, 0:256], wbc[...]) + mm(gv[...], wdt[...])
-    x = x_ref[...].astype(F32)
-    r = rs[...]
-    wp = gn * pre[...]
-    mean = jnp.mean(wp * x, axis=1, keepdims=True)
-    gin_o[...] = g_ref[...].astype(F32) + r * wp - x * (r * r * r * mean)
-    gpre = jnp.sum(gn * x * r, axis=0, keepdims=True)
-    for half in range(2):
-        tiny_o[half, 9:10, 0 : gpre.shape[1]] = gpre
 
 
 def finish_kernel(hl, tiny, total, wb, heads_o, wout_o, bc_o, conv_o, convbc_o, pre_o, bias_o, rate_o, skip_o, gain_o):
@@ -1038,17 +1001,17 @@
 
 
 def collect_kernel(
-    keep, got_v, keep_bc, send_bc, tiny, plane_a, out_o, tiny_o, a_o,
-    core_s, left_s, right_s, left_out, left_in, right_out, right_in, left2_out, left2_in, right2_out, right2_in,
-    zsend_s, zgot_s, tcore_s, tsum_s, tgot_s, tz_s, tzgot_s, agot_s,
-    core_sem, one_sem, two_sem, tiny_sem, z_sem, core_rem, one_rem, two_rem, tiny_rem, z_rem,
+    length, hl, info, gvals, ggate, w_ref, wv_b, wg_b, normed, gmb, edge, bcm, taps_bc, gv, wdt, wbc, x_ref, g_ref, rs, pre,
+    small, tiny, keep, send, plane_a, out_o, tiny_o, a_o, gin_o, ext_s, seg_s, keepbc_s, sendbc_s, tinyin_s, acc_s, *refs,
 ):
+    value, maps = refs[0:13], refs[13:26]
+    tcore_s, tsum_s, tgot_s, tz_s, tzgot_s, agot_s = refs[26:32]
+    sems = (refs[32:37], refs[37:42])
     w = lax.axis_index("wide")
     n = lax.axis_index("narrow")
     c, xx, z = w % 2, (w // 2) % 2, w // 4
-    share, cols = out_o.shape
-    chv = keep.shape[2]
-    cut = left_s.shape[3]
+    share = out_o.shape[0]
+    ch = keep.shape[2]
     core = (w + 1 - 2 * c, n)
     over_x = (w + 2 - 4 * xx, n)
     over_y = (w, 1 - n)
@@ -1061,36 +1024,20 @@
         pl.semaphore_signal(barrier, inc=1, device_id=other, device_id_type=mesh_ids)
     pl.semaphore_wait(barrier, 7)
 
-    def copy(src, dst, out_sem, in_sem, other):
+    def copy(src, dst, group, at, other):
         got = pltpu.make_async_remote_copy(
-            src_ref=src, dst_ref=dst, send_sem=out_sem, recv_sem=in_sem, device_id=other, device_id_type=mesh_ids
+            src_ref=src, dst_ref=dst, send_sem=sems[0][group].at[at], recv_sem=sems[1][group].at[at], device_id=other,
+            device_id_type=mesh_ids,
         )
         got.start()
         return got
 
     rows = [pl.ds(pl.multiple_of(((z + d) % 4) * (2 * share), 2 * share), 2 * share) for d in steps + (0,)]
-    first = [copy(tiny, tcore_s, core_sem.at[4], core_rem.at[4], core)]
-    for i in range(4):
-        first.append(copy(send_bc.at[:, rows[i], :], core_s.at[i], core_sem.at[i], core_rem.at[i], core))
-    a_copies = [
-        copy(plane_a.at[(z + steps[k]) % 4], agot_s.at[k], z_sem.at[2, k], z_rem.at[2, k], over_z[k]) for k in range(3)
-    ]
-    first[0].wait()
-    tsum_s[...] = tiny[...] + tcore_s[...]
-    small = []
-    for k, other in enumerate((over_x, over_y, over_d)):
-        half = 0 if k == 0 else 1
-        small.append(copy(tsum_s.at[half], tgot_s.at[k], tiny_sem.at[k], tiny_rem.at[k], other))
-    second = []
-    for i in range(4):
-        first[i + 1].wait()
-        both = jnp.concatenate(
-            [
-                keep[:, rows[i], :].astype(F32) + got_v[:, rows[i], :].astype(F32),
-                keep_bc[:, rows[i], :].astype(F32) + core_s[i].astype(F32),
-            ],
-            axis=2,
-        )
+
+    def split(kind, i, kept, bufs):
+        core_s, left_s, right_s, left_out, left_in, right_out, right_in = bufs[:7]
+        cut = left_s.shape[3]
+        both = kept[:, rows[i], :].astype(F32) + core_s[i].astype(F32)
         low, high = both[:, 0:share, :], both[:, share:, :]
         near = jnp.where(xx == 0, low, high)
         far = jnp.where(xx == 0, high, low)
@@ -1100,46 +1047,151 @@
         left_out[i] = far[:, :, 0:cut].astype(BF16)
         right_out[i, 0] = near[1, :, cut:].astype(BF16)
         right_out[i, 1] = far[1, :, cut:].astype(BF16)
-        second.append(
-            (
-                copy(left_out.at[i], left_in.at[i], one_sem.at[i, 0], one_rem.at[i, 0], over_x),
-                copy(right_out.at[i], right_in.at[i], one_sem.at[i, 1], one_rem.at[i, 1], over_y),
-            )
+        return (
+            copy(left_out.at[i], left_in.at[i], 1, (kind, i, 0), over_x),
+            copy(right_out.at[i], right_in.at[i], 1, (kind, i, 1), over_y),
         )
-    for one in small:
+
+    def cross_over(kind, i, going, bufs):
+        left_s, right_s, _, left_in, _, right_in, left2_out, left2_in, right2_out, right2_in = bufs[1:11]
+        going[0].wait()
+        left_s[i] = left_s[i] + left_in[i].astype(F32)
+        left2_out[i] = left_s[i, 1].astype(BF16)
+        go_left = copy(left2_out.at[i], left2_in.at[i], 2, (kind, i, 0), over_y)
+        going[1].wait()
+        right_s[i] = right_s[i] + right_in[i].astype(F32)
+        right2_out[i] = right_s[i, 1].astype(BF16)
+        return go_left, copy(right2_out.at[i], right2_in.at[i], 2, (kind, i, 1), over_x)
+
+    def deepen(kind, i, going, bufs, first):
+        left_s, right_s = bufs[1:3]
+        left2_in, right2_in = bufs[8], bufs[10]
+        z_out, z_in = bufs[11:13]
+        cut, cols = left_s.shape[3], z_out.shape[2]
+        going[0].wait()
+        going[1].wait()
+        left = left_s[i, 0] + left2_in[i].astype(F32)
+        right = right_s[i, 0] + right2_in[i].astype(F32)
+        if i == 3:
+            out_o[:, first : first + cut] = left
+            out_o[:, first + cut : first + cols] = right
+            return []
+        z_out[i, :, 0:cut] = left.astype(BF16)
+        z_out[i, :, cut:] = right.astype(BF16)
+        return [copy(z_out.at[i], z_in.at[i], 4, (kind, i), over_z[i])]
+
+    v_core = [copy(send.at[:, rows[i], :], value[0].at[i], 0, i, core) for i in range(4)]
+    a_copies = [copy(plane_a.at[(z + steps[k]) % 4], agot_s.at[k], 4, (3, k), over_z[k]) for k in range(3)]
+
+    ext = length + 2 * HALO
+    off, count = info[5], info[4]
+    own = slice(HALO, HALO + length)
+    seg_s[...] = seg_at(info, iota((ext, 128), 0) + (off - HALO))
+    live = iota((length, 128), 0) + off < count
+    tinyin_s[...] = tiny[...]
+    for half in range(2):
+        tinyin_s[half, 10:11, 0:128] = small[8 * half : 8 * half + 1, :]
+        tinyin_s[half, 10:11, 128:256] = small[8 * half + 1 : 8 * half + 2, :]
+    both = []
+    v_first, v_second, m_first, m_second, last = {}, {}, {}, {}, []
+
+    def v_split(i):
+        v_core[i].wait()
+        v_first[i] = split(0, i, keep, value)
+
+    def v_cross(i):
+        v_second[i] = cross_over(0, i, v_first[i], value)
+
+    def v_deepen(i):
+        last.extend(deepen(0, i, v_second[i], value, 0))
+
+    def m_split(i):
+        m_core[i].wait()
+        m_first[i] = split(1, i, keepbc_s, maps)
+
+    def m_cross(i):
+        m_second[i] = cross_over(1, i, m_first[i], maps)
+
+    def m_deepen(i):
+        last.extend(deepen(1, i, m_second[i], maps, ch))
+
+    for k in range(2):
+        cols = slice(k * 128, (k + 1) * 128)
+        ext_s[...] = gmb[:, cols]
+        lo = HALO // 2
+        hi = length + lo
+        got = edge[:, cols]
+        ext_s[lo : lo + HALO, :] += jnp.where(info[7] == 1, got, 0.0)
+        ext_s[hi : hi + HALO, :] += jnp.where(info[7] == 1, 0.0, got)
+        gbc, gtap = back_conv(length, seg_s, live, ext_s, bcm[:, cols], taps_bc[:, cols])
+        for t in range(7):
+            at = (t % 3) * 256 + k * 128
+            for half in range(2):
+                tinyin_s[half, 11 + t // 3 : 12 + t // 3, at : at + 128] = gtap[t]
+        both.append(gbc.astype(BF16))
+        if k == 0:
+            v_split(0)
+            v_split(1)
+    gbc = jnp.concatenate(both + [gv[...]], axis=1)
+    gw = tn(normed[own, :], gbc)
+    by_core(gw, keepbc_s.at[0], sendbc_s.at[0])
+    turned = pltpu.roll(gw[:, 256:], 128 - hl, 1)
+    by_core(jnp.concatenate([gw[:, 0:256], turned], axis=1), keepbc_s.at[1], sendbc_s.at[1])
+    m_core = [copy(sendbc_s.at[:, rows[i], :], maps[0].at[i], 0, 4 + i, core) for i in range(4)]
+    wv_a = jnp.concatenate([w_ref[h, HD : 2 * HD, :] for h in range(hl)], axis=0)
+    wg_a = jnp.concatenate([w_ref[h, 0:HD, :] for h in range(hl)], axis=0)
+    v_cross(0)
+    v_split(2)
+    acc_s[...] = mm(gvals[:, 0:ch], wv_a) + mm(gvals[:, ch:], wv_b[...])
+    v_cross(1)
+    v_deepen(0)
+    v_split(3)
+    m_split(0)
+    m_split(1)
+    gn = acc_s[...] + mm(ggate[:, 0:ch], wg_a) + mm(ggate[:, ch:], wg_b[...])
+    gn = gn + nt(gbc[:, 0:256], wbc[...]) + mm(gv[...], wdt[...])
+    acc_s[...] = gn
+    r = rs[...]
+    gpre = jnp.sum(gn * x_ref[...].astype(F32) * r, axis=0, keepdims=True)
+    for half in range(2):
+        tinyin_s[half, 9:10, 0 : gpre.shape[1]] = gpre
+    t_core = copy(tinyin_s, tcore_s, 0, 8, core)
+    v_cross(2)
+    v_deepen(1)
+    m_split(2)
+    m_cross(0)
+    v_cross(3)
+    v_deepen(2)
+    m_split(3)
+    m_cross(1)
+    m_deepen(0)
+    t_core.wait()
+    tsum_s[...] = tinyin_s[...] + tcore_s[...]
+    t_plane = [copy(tsum_s.at[min(k, 1)], tgot_s.at[k], 3, k, other) for k, other in enumerate((over_x, over_y, over_d))]
+    m_cross(2)
+    m_deepen(1)
+    m_cross(3)
+    m_deepen(2)
+    for one in t_plane:
         one.wait()
     tsum = tsum_s[0] + tgot_s[0] + tgot_s[1] + tgot_s[2]
     tz_s[...] = tsum
-    last = [copy(tz_s, tzgot_s.at[k], z_sem.at[1, k], z_rem.at[1, k], over_z[k]) for k in range(3)]
-    third = []
-    for i in range(4):
-        second[i][0].wait()
-        left_s[i] = left_s[i] + left_in[i].astype(F32)
-        left2_out[i] = left_s[i, 1].astype(BF16)
-        go_left = copy(left2_out.at[i], left2_in.at[i], two_sem.at[i, 0], two_rem.at[i, 0], over_y)
-        second[i][1].wait()
-        right_s[i] = right_s[i] + right_in[i].astype(F32)
-        right2_out[i] = right_s[i, 1].astype(BF16)
-        go_right = copy(right2_out.at[i], right2_in.at[i], two_sem.at[i, 1], two_rem.at[i, 1], over_x)
-        third.append((go_left, go_right))
-    for i in range(4):
-        third[i][0].wait()
-        third[i][1].wait()
-        left = left_s[i, 0] + left2_in[i].astype(F32)
-        right = right_s[i, 0] + right2_in[i].astype(F32)
-        if i < 3:
-            zsend_s[i, :, 0:cut] = left.astype(BF16)
-            zsend_s[i, :, cut:] = right.astype(BF16)
-            last.append(copy(zsend_s.at[i], zgot_s.at[i], z_sem.at[0, i], z_rem.at[0, i], over_z[i]))
-        else:
-            out_o[:, 0:cut] = left
-            out_o[:, cut:] = right
+    last += [copy(tz_s, tzgot_s.at[k], 4, (2, k), over_z[k]) for k in range(3)]
+    v_deepen(3)
+    m_deepen(3)
+    x = x_ref[...].astype(F32)
+    gn = acc_s[...]
+    wp = gn * pre[...]
+    mean = jnp.mean(wp * x, axis=1, keepdims=True)
+    gin_o[...] = g_ref[...].astype(F32) + r * wp - x * (r * r * r * mean)
     for one in a_copies:
         one.wait()
     a_o[...] = plane_a[z].astype(F32) + agot_s[0].astype(F32) + agot_s[1].astype(F32) + agot_s[2].astype(F32)
     for one in last:
         one.wait()
-    out_o[...] = out_o[...] + zgot_s[0].astype(F32) + zgot_s[1].astype(F32) + zgot_s[2].astype(F32)
+    for bufs, cols in ((value, slice(0, ch)), (maps, slice(ch, out_o.shape[1]))):
+        z_in = bufs[12]
+        out_o[:, cols] = out_o[:, cols] + z_in[0].astype(F32) + z_in[1].astype(F32) + z_in[2].astype(F32)
     tiny_o[...] = tsum + tzgot_s[0] + tzgot_s[1] + tzgot_s[2]
 
 
@@ -1241,7 +1293,6 @@
     share = dm // wide
     x = layer_in[0]
     g = cotangent[0]
-    xbit = (w // 2) % 2
 
     w_turned = jnp.transpose(w_heads, (1, 2, 0))
     small_own = pl.pallas_call(
@@ -1377,34 +1428,22 @@
     )(info, x, g, normed, y, wo, w_turned, *wog_pieces, gain, tab_b, tab_c, dpt)
 
     gw_shape = (2, dm // 2, dm + ch)
-    keep_a, send_a = pl.pallas_call(
+    piece = sds((4, share, dm + ch), BF16)
+    a_pieces = pl.pallas_call(
         wsum_kernel,
-        out_shape=[pltpu.HBM(gw_shape, BF16)] * 2,
+        out_shape=[piece] * 4,
         in_specs=[VMEM] * 4,
-        out_specs=[HBM] * 2,
-        scratch_shapes=[pltpu.VMEM(gw_shape, BF16)] * 2 + [pltpu.SemaphoreType.DMA((4,))],
-        compiler_params=params(False, 10),
-        cost_estimate=cost(5),
+        out_specs=[VMEM] * 4,
+        scratch_shapes=[pltpu.VMEM(gw_shape, BF16)] * 3 + [pltpu.SemaphoreType.DMA((2, 2))] * 2,
+        compiler_params=pltpu.CompilerParams(collective_id=1, has_side_effects=True, vmem_limit_bytes=16 * 2**20),
+        cost_estimate=cost(7),
         name="wsum",
     )(g, normed, hn, ggate)
 
-    def meet(keep, got):
-        cols = keep.shape[-1]
-        keep = keep.reshape(2, wide // 4, 2, share, cols)
-        got = got.reshape(2, wide // 4, 2, share, cols)
-
-        def piece(half, xx):
-            def cut(v):
-                return lax.dynamic_slice(v, (half, 0, xx, 0, 0), (1, wide // 4, 1, share, cols)).reshape(-1, share, cols)
-
-            return total(cut(keep), cut(got)).astype(BF16)
-
-        return piece(0, xbit), piece(0, 1 - xbit), piece(1, xbit), piece(1, 1 - xbit)
-
     def plane(mine, to_x, to_y, to_d):
         return total(mine, flip(to_x, 2, wide), swap(to_y), cross(to_d, 2, wide)).astype(mine.dtype)
 
-    a_pieces = meet(keep_a, flip(send_a, 1, wide))
+    a_plane = plane(*a_pieces)
 
     def table(k):
         return pl.BlockSpec((None,) + sq, lambda j: (k, 0, 0, 0))
@@ -1430,8 +1469,7 @@
     )(info, xc, ds, gy, s_true, gs_loc, swap(gbnd), dpt, tab_b, tab_a, tab_b, tab_c, skip)
     edge = swap(edge)
 
-    gmix, *a_pieces = lax.optimization_barrier((gmix, *a_pieces))
-    a_plane = plane(*a_pieces)
+    gmix, a_plane = lax.optimization_barrier((gmix, a_plane))
 
     gmb, gv, small, edge_bc = pl.pallas_call(
         functools.partial(join_kernel, length, heads),
@@ -1452,51 +1490,38 @@
         in_specs=[SMEM] + [VMEM] * 7,
         out_specs=[VMEM] * 4,
         scratch_shapes=[
-            pltpu.VMEM((ext, 128), F32), pltpu.VMEM((ext, 128), F32), pltpu.VMEM((ext, 128), jnp.int32),
-            pltpu.VMEM((dm, length), BF16),
+            pltpu.VMEM((ext, 128), F32), pltpu.VMEM((ext, 128), jnp.int32), pltpu.VMEM((dm, length), BF16),
         ],
         compiler_params=params(False, 10),
         cost_estimate=cost(12),
         name="back",
     )(info, gmix, edge, vm, normed, taps, ggain, gskip)
 
-    got_v = flip(send_v, 1, wide)
-    keep_bc, send_bc, tiny, grad_in = pl.pallas_call(
-        functools.partial(last_kernel, length, hl),
-        out_shape=[
-            sds((2, dm // 2, 384), BF16), sds((2, dm // 2, 384), BF16), sds((2, 16, ch), F32), sds((length, dm), F32),
-        ],
-        in_specs=[SMEM] + [VMEM] * 19,
+    def buffers(cols, cut):
+        rest = cols - cut
+        return (
+            [pltpu.VMEM((4, 2, 2 * share, cols), BF16), pltpu.VMEM((4, 2, share, cut), F32), pltpu.VMEM((4, 2, share, rest), F32)]
+            + [pltpu.VMEM((4, 2, share, cut), BF16)] * 2
+            + [pltpu.VMEM((4, 2, share, rest), BF16)] * 2
+            + [pltpu.VMEM((4, share, cut), BF16)] * 2
+            + [pltpu.VMEM((4, share, rest), BF16)] * 2
+            + [pltpu.VMEM((3, share, cols), BF16)] * 2
+        )
+
+    cols = ch + 384
+    wb, tiny, wa, grad_in = pl.pallas_call(
+        functools.partial(collect_kernel, length, hl),
+        out_shape=[sds((share, cols), F32), sds((16, ch), F32), sds((share, dm + ch), F32), sds((length, dm), F32)],
+        in_specs=[SMEM] + [VMEM] * 22,
         out_specs=[VMEM] * 4,
-        scratch_shapes=[pltpu.VMEM((ext, 128), F32), pltpu.VMEM((ext, 128), F32), pltpu.VMEM((ext, 128), jnp.int32)],
-        compiler_params=params(False, 12),
-        cost_estimate=cost(8),
-        name="last",
-    )(
-        info, gvals, ggate, w_turned, wv_other, wg_other, normed, gmb, edge_bc, bcm, taps_bc, gv, wdt_all, wbc, x, g, rs,
-        pre_gain.reshape(1, dm), small, tiny,
-    )
-
-    cols = ch + 384
-    cut = 5 * cols // 9
-    rest = cols - cut
-    wb, tiny, wa = pl.pallas_call(
-        collect_kernel,
-        out_shape=[sds((share, cols), F32), sds((16, ch), F32), sds((share, dm + ch), F32)],
-        in_specs=[VMEM] * 6,
-        out_specs=[VMEM] * 3,
         scratch_shapes=[
-            pltpu.VMEM((4, 2, 2 * share, 384), BF16),
-            pltpu.VMEM((4, 2, share, cut), F32),
-            pltpu.VMEM((4, 2, share, rest), F32),
+            pltpu.VMEM((ext, 128), F32), pltpu.VMEM((ext, 128), jnp.int32),
+            pltpu.VMEM((2, dm // 2, 384), BF16), pltpu.VMEM((2, dm // 2, 384), BF16), pltpu.VMEM((2, 16, ch), F32),
+            pltpu.VMEM((length, dm), F32),
         ]
-        + [pltpu.VMEM((4, 2, share, cut), BF16)] * 2
-        + [pltpu.VMEM((4, 2, share, rest), BF16)] * 2
-        + [pltpu.VMEM((4, share, cut), BF16)] * 2
-        + [pltpu.VMEM((4, share, rest), BF16)] * 2
+        + buffers(ch, ch // 2)
+        + buffers(384, 256)
         + [
-            pltpu.VMEM((3, share, cols), BF16),
-            pltpu.VMEM((3, share, cols), BF16),
             pltpu.VMEM((2, 16, ch), F32),
             pltpu.VMEM((2, 16, ch), F32),
             pltpu.VMEM((3, 16, ch), F32),
@@ -1504,10 +1529,13 @@
             pltpu.VMEM((3, 16, ch), F32),
             pltpu.VMEM((3, share, dm + ch), BF16),
         ]
-        + [pltpu.SemaphoreType.DMA(v) for v in ((5,), (4, 2), (4, 2), (3,), (3, 3)) * 2],
-        compiler_params=pltpu.CompilerParams(collective_id=0, has_side_effects=True, vmem_limit_bytes=14 * 2**20),
+        + [pltpu.SemaphoreType.DMA(v) for v in ((9,), (2, 4, 2), (2, 4, 2), (3,), (4, 3)) * 2],
+        compiler_params=pltpu.CompilerParams(collective_id=0, has_side_effects=True, vmem_limit_bytes=24 * 2**20),
         name="collect",
-    )(keep_v, got_v, keep_bc, send_bc, tiny, a_plane)
+    )(
+        info, gvals, ggate, w_turned, wv_other, wg_other, normed, gmb, edge_bc, bcm, taps_bc, gv, wdt_all, wbc, x, g, rs,
+        pre_gain.reshape(1, dm), small, tiny, keep_v, send_v, a_plane,
+    )
 
     g_w_heads, g_w_out, g_w_bc, g_conv_x, g_conv_bc, g_pre, g_bias, g_rate, g_skip, g_gain = pl.pallas_call(
         functools.partial(finish_kernel, hl),

time: 174 us -> 165 us (0.948)
  Pallas kernels: 139 us -> 131 us
    pallas_call x3 -> x2, Pallas kernels: 44.2 us -> 39 us  [the longest x1 31.5 us: split_positions(): pl.pallas_call(functools.partial(collect_kernel, length, hl), out_shape=[...]
    pallas_call x1, Pallas kernels: 13.2 us -> 11.2 us  [split_positions(): pl.pallas_call(functools.partial(back_kernel, length, pairs // 2), out_sh...]
    ppermute x9 -> x7, starting transfers between devices: 4.7 us -> 4.61 us  [flip(): return lax.ppermute(v, 'wide', [(i, i ^ bit) for i in range(wide)])]
  transfers between devices with their start and end apart: 19 -> 17, of which waited for: 4 -> 3; matrix products, arithmetic and copies ran while one was open for 3% -> 2% of each run, Pallas kernels for 51% -> 49%
where the time goes in v2:
time: 165 us; the launch traced here: 164 us
  Pallas kernels  131 us (79%)
  starting transfers between devices  17.2 us (10%)
  waiting for transfers between devices  9.27 us (6%)
  local copies, waits for them, and re-layouts  5.08 us (3%)
    pallas_call x1, Pallas kernels, split_positions(): pl.pallas_call(functools.partial(collect_kernel, length, hl), out_shape=[...  31.5 us
    pallas_call x1, Pallas kernels, split_positions(): pl.pallas_call(functools.partial(gscan_kernel, length), grid=(pairs,), ou...  21.7 us
    pallas_call x2, Pallas kernels, scan(): pl.pallas_call(functools.partial(scan_kernel, length, first), grid=(hp,),...  15.7 us
    pallas_call x1, Pallas kernels, split_positions(): pl.pallas_call(functools.partial(gate_kernel, nb), out_shape=[pltpu.HBM((...  15 us
    pallas_call x2, Pallas kernels, vals(): pl.pallas_call(functools.partial(vals_kernel, length, other), grid=(steps...  12.6 us
    pallas_call x1, Pallas kernels, split_positions(): pl.pallas_call(functools.partial(back_kernel, length, pairs // 2), out_sh...  11.2 us
    ppermute x9, starting transfers between devices, swap(): return lax.ppermute(v, 'narrow', [(0, 1), (1, 0)])  11 us
    ppermute x9, waiting for transfers between devices, swap(): return lax.ppermute(v, 'narrow', [(0, 1), (1, 0)])  8.74 us
  transfers between devices with their start and end apart: 17, of which 3 were waited for; matrix products, arithmetic and copies ran while one was open for 2% of the time, Pallas kernels for 49%

profile of v2, /device:TPU:0, one launch (start us, length us, event | category | flops | bytes accessed | tf_op | source)
XLA Modules:
  0.0 164.3 jit_solution(6672275266025286339)
XLA Ops:
  0.6 0.0 copy-start
  0.7 1.9 %small.1.small_a = f32[48,768]{1,0:T(8,128)} custom-call(f32[12,7,64]{2,1,0:T(8,128)} %bitcast.40, f32[12,64]{1,0:T(8,128)} %gain.1, f32[2,12]{1,0:T(2,128)} %bitcast.43, f32[12]{0:T(128)} %alog.1, f32[12]{0:T(128)} %skip.1, bf16[12,130,768]{2,1,0:T(8,128)(2,1)} %bitcast.22, bf16[640,768]{1,0:T(8,128)(2,1)} %bitcast.27, bf16[640,768]{1,0:T(8,128)(2,1)} %bitcast.28), custom_call_target="tpu_custom_call" | custom-call | flops 2200000000 | bytes 2000000 | tf_op jit(solution)/shard_map/small/pallas_call | solution.py:1298
  2.5 0.0 copy-start.9
  2.5 0.0 copy-start.10
  2.5 3.0 %collective-permute-start = (f32[48,768]{1,0:T(8,128)}, f32[48,768]{1,0:T(8,128)}, u32[]{:S(2)}, u32[]{:S(2)}) collective-permute-start(f32[48,768]{1,0:T(8,128)} %small.1.small_a), channel_id=1, source_target_pairs={{0,1},{1,0},{2,3},{3,2},{4,5},{5,4},{6,7},{7,6},{8,9},{9,8},{10,11... | collective-permute-start | bytes 442376 | tf_op jit(solution)/shard_map/ppermute | solution.py:1259
  5.6 0.0 copy-done
  5.6 0.9 constant_dynamic-slice_fusion
  6.4 0.0 collective-permute-start.1
  6.5 1.0 constant_dynamic-slice_fusion.1
  7.5 1.0 pad_maximum_fusion
  8.5 2.0 %collective-permute-start.7 = (bf16[192,1536]{1,0:T(8,128)(2,1)S(1)}, bf16[192,1536]{1,0:T(8,128)(2,1)S(1)}, u32[]{:S(2)}, u32[]{:S(2)}) collective-permute-start(bf16[192,1536]{1,0:T(8,128)(2,1)S(1)} %pad_maximum_fusion), channel_id=1, source_target_pairs={{0,1},{1,0},{2,3},{3,2},{4,5},{5,4},{6,7},{7,6},{8,9},{9,8},{10,11... | collective-permute-start | bytes 1769480 | tf_op jit(solution)/shard_map/ppermute | solution.py:1259
  10.5 0.0 copy-done.15
  10.5 6.4 %collective-permute-done.1.refs_0_ = bf16[192,768]{1,0:T(8,128)(2,1)} collective-permute-done((bf16[192,768]{1,0:T(8,128)(2,1)}, bf16[192,768]{1,0:T(8,128)(2,1)}, u32[]{:S(2)}, u32[]{:S(2)}) %collective-permute-start.1) | collective-permute-done | bytes 294944 | tf_op jit(solution)/shard_map/ppermute | solution.py:1259
  16.9 2.0 %collective-permute-start.2 = (bf16[192,768]{1,0:T(8,128)(2,1)}, bf16[192,768]{1,0:T(8,128)(2,1)S(1)}, u32[]{:S(2)}, u32[]{:S(2)}) collective-permute-start(bf16[192,768]{1,0:T(8,128)(2,1)} %collective-permute-done.1.refs_0_), channel_id=1, source_target_pairs={{0,4},{2,6},{4,0},{6,2},{8,12},{10,14},{12,8},{14,10},{16,20},{18,... | collective-permute-start | bytes 884744 | tf_op jit(solution)/shard_map/ppermute | solution.py:1263
  18.8 0.0 collective-permute-done.small_b
  18.9 0.0 copy-done.2
  18.9 0.0 copy-done.8
  18.9 0.0 copy-start.6
  18.9 1.0 copy-done.6
  19.9 0.9 copy-done.7
  20.8 7.1 %front.1 = (s32[8]{0:T(128)S(1)}, f32[8,1536]{1,0:T(8,128)S(1)}, f32[8,1536]{1,0:T(8,128)S(1)}, f32[8,1536]{1,0:T(8,128)S(1)}, bf16[128,768]{1,0:T(8,128)(2,1)S(...) custom-call(s32[1,4]{1,0:T(1,128)S(1)} %copy-done.10, ...), custom_call_target="tpu_custom_call" | custom-call | flops 6600000000 | bytes 6000000 | tf_op jit(solution)/shard_map/front/pallas_call | solution.py:1337
  27.9 0.1 collective-permute-start.3
  27.9 0.0 collective-permute-done.2.refs_1_
  27.9 0.5 collective-permute-start.4
  28.4 6.0 %vals_own.1 = (bf16[640,1536]{1,0:T(8,128)(2,1)S(1)}, bf16[672,1536]{1,0:T(8,128)(2,1)S(1)}, bf16[640,1536]{1,0:T(8,128)(2,1)S(1)}, bf16[12,6,128,128]{3,2,1,0:T(8,128)(2,1)S(1)}, bf16[6,64,128]{2,1,0:T(8,128)(2,1)S(1)}) custom-call(s32[8]{0:T(128)S(1)} %get-tuple-element.89.info, bf16[672,768]{1,0:T(8,128)(2,1)S(1)} %get-tuple-element.90.normed, ...), custom_call_target="tpu_custom_call" | custom-call | flops 9900000256 | bytes 9000000 | tf_op jit(solution)/shard_map/vals_own/pallas_call | solution.py:1372
  34.5 1.7 %collective-permute-start.6 = (bf16[6,64,128]{2,1,0:T(8,128)(2,1)S(1)}, bf16[6,64,128]{2,1,0:T(8,128)(2,1)S(1)}, u32[]{:S(2)}, u32[]{:S(2)}) collective-permute-start(bf16[6,64,128]{2,1,0:T(8,128)(2,1)S(1)} %get-tuple-element.103), channel_id=1, source_target_pairs={{0,1},{1,0},{2,3},{3,2},{4,5},{5,4},{6,7},{7,6},{8,9},{9,8},{10,11... | collective-permute-start | bytes 294920 | tf_op jit(solution)/shard_map/ppermute | solution.py:1259
  36.1 0.0 collective-permute-done.7.p0
  36.1 0.0 collective-permute-start.9
  36.1 0.5 collective-permute-start.8
  36.7 0.0 collective-permute-done.3.refs_2_
  36.7 0.0 collective-permute-done.4.refs_3_
  36.7 6.6 %vals_other.1 = (bf16[640,1536]{1,0:T(8,128)(2,1)S(1)}, bf16[672,1536]{1,0:T(8,128)(2,1)S(1)}, bf16[640,1536]{1,0:T(8,128)(2,1)S(1)}, bf16[12,6,128,128]{3,2,1,0...) custom-call(s32[8]{0:T(128)S(1)} %get-tuple-element.89.info, ...), custom_call_target="tpu_custom_call", output_to_operand_aliasing={{0}: (9, {}), {1}: (10, {}), {2}: (11, {}), {3}: (12, {})} | custom-call | flops 9900000256 | bytes 9000000 | tf_op jit(solution)/shard_map/vals_other/pallas_call | solution.py:1372
  43.3 0.2 collective-permute-start.5
  43.5 0.0 collective-permute-done.6.s0_ref
  43.5 7.8 %scan_other.1 = (bf16[640,1536]{1,0:T(8,128)(2,1)S(1)}, bf16[12,6,128,128]{3,2,1,0:T(8,128)(2,1)S(1)}) custom-call(s32[8]{0:T(128)S(1)} %get-tuple-element.89.info, bf16[640,1536]{1,0:T(8,128)(2,1)S(1)} %get-tuple-element.98.xc_ref, bf16[12,6,128,128]{3,2,1,0:T(8,128)(2,1)S(1)} %get-tuple-element.99.s_ref, ...), custom_call_target="tpu_custom_call" | custom-call | flops 11000000512 | bytes 10000000 | tf_op jit(solution)/shard_map/scan_other/pallas_call | solution.py:1400
  51.4 0.5 collective-permute-done.8.p1
  51.9 0.0 collective-permute-start.10
  51.9 0.0 collective-permute-done.5.s0_ref
  51.9 0.0 copy-start.5
  51.9 0.0 copy-start.12
  51.9 7.9 %scan_own.1 = (bf16[640,1536]{1,0:T(8,128)(2,1)S(1)}, bf16[12,6,128,128]{3,2,1,0:T(8,128)(2,1)S(1)}) custom-call(s32[8]{0:T(128)S(1)} %get-tuple-element.89.info, bf16[640,1536]{1,0:T(8,128)(2,1)S(1)} %get-tuple-element.98.xc_ref, bf16[12,6,128,128]{3,2,1,0:T(8,128)(2,1)S(1)} %get-tuple-element.99.s_ref, ...), custom_call_target="tpu_custom_call", output_to_operand_aliasing={{0}: (7, {}), {1}: (8, {})} | custom-call | flops 11000000512 | bytes 10000000 | tf_op jit(solution)/shard_map/scan_own/pallas_call | solution.py:1400
  59.8 0.0 collective-permute-done.9.p2
  59.8 0.0 collective-permute-done.10.p3
  59.8 15.0 %gated.1 = (bf16[640,768]{1,0:T(8,128)(2,1)}, bf16[640,1536]{1,0:T(8,128)(2,1)S(1)}, bf16[640,1536]{1,0:T(8,128)(2,1)S(1)}, bf16[640,1536]{1,0:T(8,128)(2,1)S(1)...) custom-call(s32[8]{0:T(128)S(1)} %get-tuple-element.89.info, ...), custom_call_target="tpu_custom_call" | custom-call | flops 17600000000 | bytes 16000000 | tf_op jit(solution)/shard_map/gated/pallas_call | solution.py:1414
  74.8 1.5 collective-permute-start.11
  76.4 7.5 %wsum.1 = (bf16[4,48,1536]{2,1,0:T(8,128)(2,1)S(1)}, bf16[4,48,1536]{2,1,0:T(8,128)(2,1)S(1)}, bf16[4,48,1536]{2,1,0:T(8,128)(2,1)S(1)}, bf16[4,48,1536]{2,1,0:T(8,128)(2,1)S(1)}) custom-call(bf16[640,768]{1,0:T(8,128)(2,1)S(1)} %bitcast.33, bf16[672,768]{1,0:T(8,128)(2,1)S(1)} %get-tuple-element.90.normed, bf16[640,1536]{1,0:T(8,128)(2,1)S(1)} %get-tuple-element.116.hn, ...), custom_call_target="tpu_custom_call" | custom-call | flops 7699999744 | bytes 7000000 | tf_op jit(solution)/shard_map/wsum/pallas_call | solution.py:1432
  83.8 1.6 collective-permute-start.12
  85.4 0.4 collective-permute-start.13
  85.8 1.6 collective-permute-start.14
  87.4 0.0 collective-permute-done.11.gs0_ref
  87.4 21.7 %gscan.1 = (bf16[640,1536]{1,0:T(8,128)(2,1)S(1)}, f32[5,128,128]{2,1,0:T(8,128)S(1)}, f32[5,128,128]{2,1,0:T(8,128)S(1)}, f32[5,128,128]{2,1,0:T(8,128)S(1)}, f...) custom-call(s32[8]{0:T(128)S(1)} %get-tuple-element.89.info, ...), custom_call_target="tpu_custom_call" | custom-call | flops 24199999488 | bytes 22000000 | tf_op jit(solution)/shard_map/gscan/pallas_call | solution.py:1452
  109.2 4.1 %join.1 = (f32[672,256]{1,0:T(8,128)S(1)}, bf16[640,128]{1,0:T(8,128)(2,1)S(1)}, f32[16,128]{1,0:T(8,128)S(1)}, f32[16,256]{1,0:T(8,128)S(1)}) custom-call(s32[8]{0:T(128)S(1)} %get-tuple-element.89.info, f32[5,128,128]{2,1,0:T(8,128)S(1)} %get-tuple-element.130.ggt, f32[5,128,128]{2,1,0:T(8,128)S(1)} %get-tuple-element.131.gb, ...), custom_call_target="tpu_custom_call" | custom-call | flops 6600000000 | bytes 6000000 | tf_op jit(solution)/shard_map/join/pallas_call | solution.py:1474
  113.3 0.6 collective-permute-start.16
  113.9 1.4 collective-permute-start.15
  115.3 0.0 collective-permute-done.12
  115.3 0.0 collective-permute-done.13
  115.3 0.0 collective-permute-done.14
  115.3 0.3 add_convert_fusion.plane_a
  115.6 2.4 %collective-permute-done.15.edge = bf16[16,1536]{1,0:T(8,128)(2,1)S(1)} collective-permute-done((bf16[16,1536]{1,0:T(8,128)(2,1)S(1)}, bf16[16,1536]{1,0:T(8,128)(2,1)S(1)}, u32[]{:S(2)}, u32[]{:S(2)}) %collective-permute-start.15) | collective-permute-done | bytes 49184 | tf_op jit(solution)/shard_map/ppermute | solution.py:1259
  118.0 11.2 %back.1 = (bf16[640,1536]{1,0:T(8,128)(2,1)S(1)}, bf16[2,384,768]{2,1,0:T(8,128)(2,1)S(1)}, bf16[2,384,768]{2,1,0:T(8,128)(2,1)S(1)}, f32[2,16,768]{2,1,0:T(8,128)S(1)}) custom-call(s32[8]{0:T(128)S(1)} %get-tuple-element.89.info, bf16[640,1536]{1,0:T(8,128)(2,1)S(1)} %get-tuple-element.122.gmix, bf16[16,1536]{1,0:T(8,128)(2,1)S(1)} %collective-permute-done.15.edge, ...), custom_call_target="tpu_custom_call" | custom-call | flops 13200000000 | bytes 12000000 | tf_op jit(solution)/shard_map/back/pallas_call | solution.py:1487
  129.2 0.0 collective-permute-done.16.edge
  129.2 31.5 %collect.1 = (f32[48,1152]{1,0:T(8,128)S(1)}, f32[16,768]{1,0:T(8,128)S(1)}, f32[48,1536]{1,0:T(8,128)S(1)}, f32[640,768]{1,0:T(8,128)S(1)}) custom-call(s32[8]{0:T(128)S(1)} %get-tuple-element.89.info, bf16[640,1536]{1,0:T(8,128)(2,1)S(1)} %get-tuple-element.127.gvals, bf16[640,1536]{1,0:T(8,128)(2,1)S(1)} %get-tuple-element.117.ggate, ...), custom_call_target="tpu_custom_call" | custom-call | tf_op jit(solution)/shard_map/collect/pallas_call | solution.py:1512
  160.8 2.2 %finish.1 = (f32[12,48,130]{2,1,0:T(8,128)}, f32[12,48,64]{2,1,0:T(8,128)}, f32[48,256]{1,0:T(8,128)}, f32[7,4,12]{2,1,0:T(4,128)}, f32[7,16]{1,0:T(8,128)}, /*i...) custom-call(f32[16,768]{1,0:T(8,128)S(1)} %get-tuple-element.153.tiny, ...), custom_call_target="tpu_custom_call" | custom-call | tf_op jit(solution)/shard_map/finish/pallas_call | solution.py:1540
  163.0 1.3 copy.39
  (21 shorter events, 0.0 us)
Async XLA Ops:
  0.6 4.9 %copy-start = (bf16[768,12,130]{0,2,1:T(8,128)(2,1)S(1)}, bf16[768,12,130]{0,2,1:T(8,128)(2,1)}, u32[]{:S(2)}) copy-start(bf16[768,12,130]{0,2,1:T(8,128)(2,1)} %param.16) | copy-start | bytes 7188484
  2.5 8.0 %copy-start.15 = (f32[768]{0:T(1024)S(1)}, f32[768]{0:T(1024)}, u32[]{:S(2)}) copy-start(f32[768]{0:T(1024)} %param.15) | copy-start | bytes 9220
  2.5 16.3 %copy-start.2 = (bf16[1,640,768]{2,1,0:T(8,128)(2,1)S(1)}, bf16[1,640,768]{2,1,0:T(8,128)(2,1)}, u32[]{:S(2)}) copy-start(bf16[1,640,768]{2,1,0:T(8,128)(2,1)} %param.14) | copy-start | bytes 2949124
  2.5 16.3 %copy-start.8 = (f32[7,256]{1,0:T(8,128)S(1)}, f32[7,256]{1,0:T(8,128)}, u32[]{:S(2)}) copy-start(f32[7,256]{1,0:T(8,128)} %taps_ref.1) | copy-start | bytes 21508
  2.5 16.3 %copy-start.9 = (s32[1,1280]{1,0:T(1,128)S(1)}, s32[1,1280]{1,0:T(1,128)}, u32[]{:S(2)}) copy-start(s32[1,1280]{1,0:T(1,128)} %live_ref.1) | copy-start | bytes 15364
  2.5 16.3 %copy-start.10 = (s32[1,4]{1,0:T(1,128)S(1)}, s32[1,4]{1,0:T(1,128)}, u32[]{:S(2)}) copy-start(s32[1,4]{1,0:T(1,128)} %starts.1) | copy-start | bytes 52
  2.5 16.3 %collective-permute-start = (f32[48,768]{1,0:T(8,128)}, f32[48,768]{1,0:T(8,128)}, u32[]{:S(2)}, u32[]{:S(2)}) collective-permute-start(f32[48,768]{1,0:T(8,128)} %small.1.small_a), channel_id=1, source_target_pairs={{0,1},{1,0},{2,3},{3,2},{4,5},{5,4},{6,7},{7,6},{8,9},{9,8},{10,11... | collective-permute-start | bytes 442376 | tf_op jit(solution)/shard_map/ppermute | solution.py:1259
  6.4 10.5 %collective-permute-start.1 = (bf16[192,768]{1,0:T(8,128)(2,1)}, bf16[192,768]{1,0:T(8,128)(2,1)}, u32[]{:S(2)}, u32[]{:S(2)}) collective-permute-start(bf16[192,768]{1,0:T(8,128)(2,1)} %bitcast.6), channel_id=1, source_target_pairs={{0,1},{1,0},{2,3},{3,2},{4,5},{5,4},{6,7},{7,6},{8,9},{9,8},{10,11... | collective-permute-start | bytes 884744 | tf_op jit(solution)/shard_map/ppermute | solution.py:1259
  8.5 27.6 %collective-permute-start.7 = (bf16[192,1536]{1,0:T(8,128)(2,1)S(1)}, bf16[192,1536]{1,0:T(8,128)(2,1)S(1)}, u32[]{:S(2)}, u32[]{:S(2)}) collective-permute-start(bf16[192,1536]{1,0:T(8,128)(2,1)S(1)} %pad_maximum_fusion), channel_id=1, source_target_pairs={{0,1},{1,0},{2,3},{3,2},{4,5},{5,4},{6,7},{7,6},{8,9},{9,8},{10,11... | collective-permute-start | bytes 1769480 | tf_op jit(solution)/shard_map/ppermute | solution.py:1259
  16.9 11.0 %collective-permute-start.2 = (bf16[192,768]{1,0:T(8,128)(2,1)}, bf16[192,768]{1,0:T(8,128)(2,1)S(1)}, u32[]{:S(2)}, u32[]{:S(2)}) collective-permute-start(bf16[192,768]{1,0:T(8,128)(2,1)} %collective-permute-done.1.refs_0_), channel_id=1, source_target_pairs={{0,4},{2,6},{4,0},{6,2},{8,12},{10,14},{12,8},{14,10},{16,20},{18,... | collective-permute-start | bytes 884744 | tf_op jit(solution)/shard_map/ppermute | solution.py:1263
  18.9 1.0 copy-start.6
  19.9 0.9 copy-start.7
  27.9 8.8 %collective-permute-start.3 = (bf16[192,768]{1,0:T(8,128)(2,1)}, bf16[192,768]{1,0:T(8,128)(2,1)S(1)}, u32[]{:S(2)}, u32[]{:S(2)}) collective-permute-start(bf16[192,768]{1,0:T(8,128)(2,1)} %collective-permute-done.1.refs_0_), channel_id=1, source_target_pairs={{0,2},{2,0},{4,6},{6,4},{8,10},{10,8},{12,14},{14,12},{16,18},{18,... | collective-permute-start | bytes 884744 | tf_op jit(solution)/shard_map/ppermute | solution.py:1263
  27.9 8.7 %collective-permute-start.4 = (bf16[192,768]{1,0:T(8,128)(2,1)S(1)}, bf16[192,768]{1,0:T(8,128)(2,1)S(1)}, u32[]{:S(2)}, u32[]{:S(2)}) collective-permute-start(bf16[192,768]{1,0:T(8,128)(2,1)S(1)} %collective-permute-done.2.refs_1_), channel_id=1, source_target_pairs={{0,2},{2,0},{4,6},{6,4},{8,10},{10,8},{12,14},{14,12},{16,18},{18,... | collective-permute-start | bytes 884744 | tf_op jit(solution)/shard_map/ppermute | solution.py:1263
  34.5 9.0 %collective-permute-start.6 = (bf16[6,64,128]{2,1,0:T(8,128)(2,1)S(1)}, bf16[6,64,128]{2,1,0:T(8,128)(2,1)S(1)}, u32[]{:S(2)}, u32[]{:S(2)}) collective-permute-start(bf16[6,64,128]{2,1,0:T(8,128)(2,1)S(1)} %get-tuple-element.103), channel_id=1, source_target_pairs={{0,1},{1,0},{2,3},{3,2},{4,5},{5,4},{6,7},{7,6},{8,9},{9,8},{10,11... | collective-permute-start | bytes 294920 | tf_op jit(solution)/shard_map/ppermute | solution.py:1259
  36.1 23.7 %collective-permute-start.9 = (bf16[192,1536]{1,0:T(8,128)(2,1)S(1)}, bf16[192,1536]{1,0:T(8,128)(2,1)S(1)}, u32[]{:S(2)}, u32[]{:S(2)}) collective-permute-start(bf16[192,1536]{1,0:T(8,128)(2,1)S(1)} %collective-permute-done.7.p0), channel_id=1, source_target_pairs={{0,2},{2,0},{4,6},{6,4},{8,10},{10,8},{12,14},{14,12},{16,18},{18,... | collective-permute-start | bytes 1769480 | tf_op jit(solution)/shard_map/ppermute | solution.py:1263
  36.1 15.7 %collective-permute-start.8 = (bf16[192,1536]{1,0:T(8,128)(2,1)S(1)}, bf16[192,1536]{1,0:T(8,128)(2,1)S(1)}, u32[]{:S(2)}, u32[]{:S(2)}) collective-permute-start(bf16[192,1536]{1,0:T(8,128)(2,1)S(1)} %collective-permute-done.7.p0), channel_id=1, source_target_pairs={{0,4},{2,6},{4,0},{6,2},{8,12},{10,14},{12,8},{14,10},{16,20},{18,... | collective-permute-start | bytes 1769480 | tf_op jit(solution)/shard_map/ppermute | solution.py:1263
  43.3 8.6 %collective-permute-start.5 = (bf16[6,64,128]{2,1,0:T(8,128)(2,1)S(1)}, bf16[6,64,128]{2,1,0:T(8,128)(2,1)S(1)}, u32[]{:S(2)}, u32[]{:S(2)}) collective-permute-start(bf16[6,64,128]{2,1,0:T(8,128)(2,1)S(1)} %get-tuple-element.100), channel_id=1, source_target_pairs={{0,1},{1,0},{2,3},{3,2},{4,5},{5,4},{6,7},{7,6},{8,9},{9,8},{10,11... | collective-permute-start | bytes 294920 | tf_op jit(solution)/shard_map/ppermute | solution.py:1259
  51.9 7.9 %collective-permute-start.10 = (bf16[192,1536]{1,0:T(8,128)(2,1)S(1)}, bf16[192,1536]{1,0:T(8,128)(2,1)S(1)}, u32[]{:S(2)}, u32[]{:S(2)}) collective-permute-start(bf16[192,1536]{1,0:T(8,128)(2,1)S(1)} %collective-permute-done.8.p1), channel_id=1, source_target_pairs={{0,2},{2,0},{4,6},{6,4},{8,10},{10,8},{12,14},{14,12},{16,18},{18,... | collective-permute-start | bytes 1769480 | tf_op jit(solution)/shard_map/ppermute | solution.py:1263
  51.9 7.9 %copy-start.3 = (bf16[1,640,768]{2,1,0:T(8,128)(2,1)S(1)}, bf16[1,640,768]{2,1,0:T(8,128)(2,1)}, u32[]{:S(2)}) copy-start(bf16[1,640,768]{2,1,0:T(8,128)(2,1)} %param.25) | copy-start | bytes 2949124
  51.9 7.9 %copy-start.5 = (bf16[12,64,768]{2,1,0:T(8,128)(2,1)S(1)}, bf16[12,64,768]{2,1,0:T(8,128)(2,1)}, u32[]{:S(2)}) copy-start(bf16[12,64,768]{2,1,0:T(8,128)(2,1)} %param.24) | copy-start | bytes 3538948
  51.9 7.9 %copy-start.12 = (f32[3,5,128,128]{3,2,1,0:T(8,128)S(1)}, f32[3,5,128,128]{3,2,1,0:T(8,128)}, u32[]{:S(2)}) copy-start(f32[3,5,128,128]{3,2,1,0:T(8,128)} %get-tuple-element.108.tc) | copy-start | bytes 2949124
  74.8 12.6 %collective-permute-start.11 = (bf16[12,64,128]{2,1,0:T(8,128)(2,1)S(1)}, bf16[12,64,128]{2,1,0:T(8,128)(2,1)S(1)}, u32[]{:S(2)}, u32[]{:S(2)}) collective-permute-start(bf16[12,64,128]{2,1,0:T(8,128)(2,1)S(1)} %get-tuple-element.114), channel_id=1, source_target_pairs={{0,1},{1,0},{2,3},{3,2},{4,5},{5,4},{6,7},{7,6},{8,9},{9,8},{10,11... | collective-permute-start | bytes 589832 | tf_op jit(solution)/shard_map/ppermute | solution.py:1259
  83.8 31.4 %collective-permute-start.12 = (bf16[4,48,1536]{2,1,0:T(8,128)(2,1)S(1)}, bf16[4,48,1536]{2,1,0:T(8,128)(2,1)S(1)}, u32[]{:S(2)}, u32[]{:S(2)}) collective-permute-start(bf16[4,48,1536]{2,1,0:T(8,128)(2,1)S(1)} %get-tuple-element.119), channel_id=1, source_target_pairs={{0,4},{2,6},{4,0},{6,2},{8,12},{10,14},{12,8},{14,10},{16,20},{18,... | collective-permute-start | bytes 1769480 | tf_op jit(solution)/shard_map/ppermute | solution.py:1263
  85.4 29.9 %collective-permute-start.13 = (bf16[4,48,1536]{2,1,0:T(8,128)(2,1)S(1)}, bf16[4,48,1536]{2,1,0:T(8,128)(2,1)S(1)}, u32[]{:S(2)}, u32[]{:S(2)}) collective-permute-start(bf16[4,48,1536]{2,1,0:T(8,128)(2,1)S(1)} %get-tuple-element.120), channel_id=1, source_target_pairs={{0,1},{1,0},{2,3},{3,2},{4,5},{5,4},{6,7},{7,6},{8,9},{9,8},{10,11... | collective-permute-start | bytes 1769480 | tf_op jit(solution)/shard_map/ppermute | solution.py:1259
  85.8 29.5 %collective-permute-start.14 = (bf16[4,48,1536]{2,1,0:T(8,128)(2,1)S(1)}, bf16[4,48,1536]{2,1,0:T(8,128)(2,1)S(1)}, u32[]{:S(2)}, u32[]{:S(2)}) collective-permute-start(bf16[4,48,1536]{2,1,0:T(8,128)(2,1)S(1)} %get-tuple-element.121), channel_id=1, source_target_pairs={{0,5},{1,4},{2,7},{3,6},{4,1},{5,0},{6,3},{7,2},{8,13},{9,12},{10,... | collective-permute-start | bytes 1769480 | tf_op jit(solution)/shard_map/ppermute | solution.py:1268
  87.4 21.8 %copy-start.11 = (f32[640,384]{1,0:T(8,128)S(1)}, f32[640,384]{1,0:T(8,128)}, u32[]{:S(2)}) copy-start(f32[640,384]{1,0:T(8,128)} %get-tuple-element.138.sig) | copy-start | bytes 2949124
  87.4 21.8 %copy-start.13 = (f32[672,256]{1,0:T(8,128)S(1)}, f32[672,256]{1,0:T(8,128)}, u32[]{:S(2)}) copy-start(f32[672,256]{1,0:T(8,128)} %get-tuple-element.137.dsl) | copy-start | bytes 2064388
  87.4 21.8 %copy-start.14 = (bf16[640,256]{1,0:T(8,128)(2,1)S(1)}, bf16[640,256]{1,0:T(8,128)(2,1)}, u32[]{:S(2)}) copy-start(bf16[640,256]{1,0:T(8,128)(2,1)} %get-tuple-element.136.maps) | copy-start | bytes 983044
  113.3 15.9 %collective-permute-start.16 = (f32[16,256]{1,0:T(8,128)S(1)}, f32[16,256]{1,0:T(8,128)S(1)}, u32[]{:S(2)}, u32[]{:S(2)}) collective-permute-start(f32[16,256]{1,0:T(8,128)S(1)} %get-tuple-element.140), channel_id=1, source_target_pairs={{0,1},{1,0},{2,3},{3,2},{4,5},{5,4},{6,7},{7,6},{8,9},{9,8},{10,11... | collective-permute-start | bytes 49160 | tf_op jit(solution)/shard_map/ppermute | solution.py:1259
  113.9 4.1 %collective-permute-start.15 = (bf16[16,1536]{1,0:T(8,128)(2,1)S(1)}, bf16[16,1536]{1,0:T(8,128)(2,1)S(1)}, u32[]{:S(2)}, u32[]{:S(2)}) collective-permute-start(bf16[16,1536]{1,0:T(8,128)(2,1)S(1)} %get-tuple-element.123), channel_id=1, source_target_pairs={{0,1},{1,0},{2,3},{3,2},{4,5},{5,4},{6,7},{7,6},{8,9},{9,8},{10,11... | collective-permute-start | bytes 147464 | tf_op jit(solution)/shard_map/ppermute | solution.py:1259
  118.0 11.2 %copy-start.1 = (bf16[768,768]{1,0:T(8,128)(2,1)S(1)}, bf16[768,768]{1,0:T(8,128)(2,1)}, u32[]{:S(2)}) copy-start(bf16[768,768]{1,0:T(8,128)(2,1)} %get-tuple-element.129.wg_b) | copy-start | bytes 3538948
  118.0 11.3 %copy-start.4 = (f32[672,256]{1,0:T(8,128)S(1)}, f32[672,256]{1,0:T(8,128)}, u32[]{:S(2)}) copy-start(f32[672,256]{1,0:T(8,128)} %get-tuple-element.141.bcm) | copy-start | bytes 2064388

commit v3 on v2

--- a/solution.py
+++ b/solution.py
@@ -970,29 +970,32 @@
         heads_o[h, :, 2 * HD + 1 :] = wb[:, ch + 320 + h : ch + 321 + h]
     bc_o[...] = pack_columns(wb[:, ch : ch + 256])
     rows = tiny[...]
+    parts = jnp.concatenate(thirds(rows), axis=0).astype(BF16)
+
+    def chosen_sums(first, last, chosen):
+        got = mm(parts[:, first:last], chosen.astype(F32).astype(BF16))
+        return got[0:16, :] + got[16:32, :] + got[32:48, :]
+
     src = iota((ch, 128), 0)
     dst = iota((ch, 128), 1)
     for q in range(lanes):
-        chosen = ((src == dst * HD + lanes * w + q) & (dst < hl)).astype(F32)
-        got = mm(rows, chosen, precision=HIGH)
+        got = chosen_sums(0, ch, (src == dst * HD + lanes * w + q) & (dst < hl))
         for k in range(7):
             conv_o[k, q : q + 1, :] = got[k : k + 1, 0:hl]
         gain_o[q : q + 1, :] = got[7:8, 0:hl]
-    chosen = ((src == share * w + dst) & (dst < share)).astype(F32)
-    pre_o[...] = mm(rows[8:16, :], chosen, precision=HIGH)[1:2, 0:share]
-    per = (src // HD == dst).astype(F32)
-    skip_o[...] = mm(rows[8:16, :], per, precision=HIGH)[0:1, 0:hl]
+    pre_o[...] = chosen_sums(0, ch, (src == share * w + dst) & (dst < share))[9:10, 0:share]
+    skip_o[...] = chosen_sums(0, ch, src // HD == dst)[8:9, 0:hl]
     size = convbc_o.shape[1]
     group = (size * w) // 64
     start = ((group % 2) * 2 + group // 2) * 64 + (size * w) % 64
     src = iota((256, 128), 0)
     dst = iota((256, 128), 1)
-    chosen = ((src == start + dst) & (dst < size)).astype(F32)
+    chosen = (src == start + dst) & (dst < size)
     for k in range(3):
-        part = mm(rows[8:16, 256 * k : 256 * (k + 1)], chosen, precision=HIGH)
+        part = chosen_sums(256 * k, 256 * (k + 1), chosen)
         for r in range(3):
             if 3 * r + k < 7:
-                convbc_o[3 * r + k : 3 * r + k + 1, :] = part[3 + r : 4 + r, 0:size]
+                convbc_o[3 * r + k : 3 * r + k + 1, :] = part[11 + r : 12 + r, 0:size]
     both = rows[10:11, 0:128]
     bias_o[0:1, :] = both[:, 0:hl]
     bias_o[1:2, :] = pltpu.roll(both, 64, 1)[:, 0:hl]
@@ -1440,10 +1443,8 @@
         name="wsum",
     )(g, normed, hn, ggate)
 
-    def plane(mine, to_x, to_y, to_d):
-        return total(mine, flip(to_x, 2, wide), swap(to_y), cross(to_d, 2, wide)).astype(mine.dtype)
-
-    a_plane = plane(*a_pieces)
+    mine, to_x, to_y, to_d = a_pieces
+    got_d = cross(to_d, 2, wide)
 
     def table(k):
         return pl.BlockSpec((None,) + sq, lambda j: (k, 0, 0, 0))
@@ -1469,7 +1470,8 @@
     )(info, xc, ds, gy, s_true, gs_loc, swap(gbnd), dpt, tab_b, tab_a, tab_b, tab_c, skip)
     edge = swap(edge)
 
-    gmix, a_plane = lax.optimization_barrier((gmix, a_plane))
+    gmix, ggt, got_d = lax.optimization_barrier((gmix, ggt, got_d))
+    a_plane = total(mine, flip(to_x, 2, wide), swap(to_y), got_d).astype(BF16)
 
     gmb, gv, small, edge_bc = pl.pallas_call(
         functools.partial(join_kernel, length, heads),

time: 165 us -> 163 us (0.988)
  waiting for transfers between devices: 9.27 us -> 6.91 us
    ppermute x9, waiting for transfers between devices: 8.74 us -> 6.38 us  [swap(): return lax.ppermute(v, 'narrow', [(0, 1), (1, 0)])]
  transfers between devices with their start and end apart: 17 -> 17, of which waited for: 3 -> 2; matrix products, arithmetic and copies ran while one was open for 2% -> 2% of each run, Pallas kernels for 49% -> 49%
where the time goes in v3:
time: 163 us; the launch traced here: 162 us
  Pallas kernels  130 us (80%)
  starting transfers between devices  17.2 us (11%)
  waiting for transfers between devices  6.91 us (4%)
  local copies, waits for them, and re-layouts  6.18 us (4%)
    pallas_call x1, Pallas kernels, split_positions(): pl.pallas_call(functools.partial(collect_kernel, length, hl), out_shape=[...  31.5 us
    pallas_call x1, Pallas kernels, split_positions(): pl.pallas_call(functools.partial(gscan_kernel, length), grid=(pairs,), ou...  21.8 us
    pallas_call x2, Pallas kernels, scan(): pl.pallas_call(functools.partial(scan_kernel, length, first), grid=(hp,),...  15.7 us
    pallas_call x1, Pallas kernels, split_positions(): pl.pallas_call(functools.partial(gate_kernel, nb), out_shape=[pltpu.HBM((...  15 us
    pallas_call x2, Pallas kernels, vals(): pl.pallas_call(functools.partial(vals_kernel, length, other), grid=(steps...  12.6 us
    ppermute x9, starting transfers between devices, swap(): return lax.ppermute(v, 'narrow', [(0, 1), (1, 0)])  12.1 us
    pallas_call x1, Pallas kernels, split_positions(): pl.pallas_call(functools.partial(back_kernel, length, pairs // 2), out_sh...  11.2 us
    pallas_call x1, Pallas kernels, split_positions(): pl.pallas_call(wsum_kernel, out_shape=[piece] * 4, in_specs=[VMEM] * 4, o...  7.48 us
  transfers between devices with their start and end apart: 17, of which 2 were waited for; matrix products, arithmetic and copies ran while one was open for 2% of the time, Pallas kernels for 49%

profile of v3, /device:TPU:0, one launch (start us, length us, event | category | flops | bytes accessed | tf_op | source)
XLA Modules:
  0.0 162.2 jit_solution(677281602206037319)
XLA Ops:
  0.7 1.9 %small.1.small_a = f32[48,768]{1,0:T(8,128)} custom-call(f32[12,7,64]{2,1,0:T(8,128)} %bitcast.40, f32[12,64]{1,0:T(8,128)} %gain.1, f32[2,12]{1,0:T(2,128)} %bitcast.43, f32[12]{0:T(128)} %alog.1, f32[12]{0:T(128)} %skip.1, bf16[12,130,768]{2,1,0:T(8,128)(2,1)} %bitcast.22, bf16[640,768]{1,0:T(8,128)(2,1)} %bitcast.27, bf16[640,768]{1,0:T(8,128)(2,1)} %bitcast.28), custom_call_target="tpu_custom_call" | custom-call | flops 2200000000 | bytes 2000000 | tf_op jit(solution)/shard_map/small/pallas_call | solution.py:1301
  2.5 0.0 copy-start.9
  2.5 0.0 copy-start.10
  2.5 3.0 %collective-permute-start = (f32[48,768]{1,0:T(8,128)}, f32[48,768]{1,0:T(8,128)}, u32[]{:S(2)}, u32[]{:S(2)}) collective-permute-start(f32[48,768]{1,0:T(8,128)} %small.1.small_a), channel_id=1, source_target_pairs={{0,1},{1,0},{2,3},{3,2},{4,5},{5,4},{6,7},{7,6},{8,9},{9,8},{10,11... | collective-permute-start | bytes 442376 | tf_op jit(solution)/shard_map/ppermute | solution.py:1262
  5.6 0.9 constant_dynamic-slice_fusion
  6.4 0.0 collective-permute-start.1
  6.5 1.0 constant_dynamic-slice_fusion.1
  7.5 1.0 pad_maximum_fusion
  8.5 2.0 %collective-permute-start.7 = (bf16[192,1536]{1,0:T(8,128)(2,1)S(1)}, bf16[192,1536]{1,0:T(8,128)(2,1)S(1)}, u32[]{:S(2)}, u32[]{:S(2)}) collective-permute-start(bf16[192,1536]{1,0:T(8,128)(2,1)S(1)} %pad_maximum_fusion), channel_id=1, source_target_pairs={{0,1},{1,0},{2,3},{3,2},{4,5},{5,4},{6,7},{7,6},{8,9},{9,8},{10,11... | collective-permute-start | bytes 1769480 | tf_op jit(solution)/shard_map/ppermute | solution.py:1262
  10.5 0.0 copy-done.15
  10.5 6.4 %collective-permute-done.1.refs_0_ = bf16[192,768]{1,0:T(8,128)(2,1)} collective-permute-done((bf16[192,768]{1,0:T(8,128)(2,1)}, bf16[192,768]{1,0:T(8,128)(2,1)}, u32[]{:S(2)}, u32[]{:S(2)}) %collective-permute-start.1) | collective-permute-done | bytes 294944 | tf_op jit(solution)/shard_map/ppermute | solution.py:1262
  16.9 2.0 %collective-permute-start.2 = (bf16[192,768]{1,0:T(8,128)(2,1)}, bf16[192,768]{1,0:T(8,128)(2,1)S(1)}, u32[]{:S(2)}, u32[]{:S(2)}) collective-permute-start(bf16[192,768]{1,0:T(8,128)(2,1)} %collective-permute-done.1.refs_0_), channel_id=1, source_target_pairs={{0,4},{2,6},{4,0},{6,2},{8,12},{10,14},{12,8},{14,10},{16,20},{18,... | collective-permute-start | bytes 884744 | tf_op jit(solution)/shard_map/ppermute | solution.py:1266
  18.8 0.0 collective-permute-done.small_b
  18.9 0.0 copy-done.8
  18.9 0.0 copy-start.6
  18.9 1.0 copy-done.6
  19.9 0.9 copy-done.7
  20.8 7.1 %front.1 = (s32[8]{0:T(128)S(1)}, f32[8,1536]{1,0:T(8,128)S(1)}, f32[8,1536]{1,0:T(8,128)S(1)}, f32[8,1536]{1,0:T(8,128)S(1)}, bf16[128,768]{1,0:T(8,128)(2,1)S(...) custom-call(s32[1,4]{1,0:T(1,128)S(1)} %copy-done.10, ...), custom_call_target="tpu_custom_call" | custom-call | flops 6600000000 | bytes 6000000 | tf_op jit(solution)/shard_map/front/pallas_call | solution.py:1340
  27.9 0.1 collective-permute-start.3
  27.9 0.0 collective-permute-done.2.refs_1_
  27.9 0.5 collective-permute-start.4
  28.4 6.0 %vals_own.1 = (bf16[640,1536]{1,0:T(8,128)(2,1)S(1)}, bf16[672,1536]{1,0:T(8,128)(2,1)S(1)}, bf16[640,1536]{1,0:T(8,128)(2,1)S(1)}, bf16[12,6,128,128]{3,2,1,0:T(8,128)(2,1)S(1)}, bf16[6,64,128]{2,1,0:T(8,128)(2,1)S(1)}) custom-call(s32[8]{0:T(128)S(1)} %get-tuple-element.90.info, bf16[672,768]{1,0:T(8,128)(2,1)S(1)} %get-tuple-element.91.normed, ...), custom_call_target="tpu_custom_call" | custom-call | flops 9900000256 | bytes 9000000 | tf_op jit(solution)/shard_map/vals_own/pallas_call | solution.py:1375
  34.5 1.7 %collective-permute-start.6 = (bf16[6,64,128]{2,1,0:T(8,128)(2,1)S(1)}, bf16[6,64,128]{2,1,0:T(8,128)(2,1)S(1)}, u32[]{:S(2)}, u32[]{:S(2)}) collective-permute-start(bf16[6,64,128]{2,1,0:T(8,128)(2,1)S(1)} %get-tuple-element.104), channel_id=1, source_target_pairs={{0,1},{1,0},{2,3},{3,2},{4,5},{5,4},{6,7},{7,6},{8,9},{9,8},{10,11... | collective-permute-start | bytes 294920 | tf_op jit(solution)/shard_map/ppermute | solution.py:1262
  36.1 0.0 collective-permute-done.7.p0
  36.1 0.0 collective-permute-start.9
  36.1 0.5 collective-permute-start.8
  36.7 0.0 collective-permute-done.3.refs_2_
  36.7 0.0 collective-permute-done.4.refs_3_
  36.7 6.6 %vals_other.1 = (bf16[640,1536]{1,0:T(8,128)(2,1)S(1)}, bf16[672,1536]{1,0:T(8,128)(2,1)S(1)}, bf16[640,1536]{1,0:T(8,128)(2,1)S(1)}, bf16[12,6,128,128]{3,2,1,0...) custom-call(s32[8]{0:T(128)S(1)} %get-tuple-element.90.info, ...), custom_call_target="tpu_custom_call", output_to_operand_aliasing={{0}: (9, {}), {1}: (10, {}), {2}: (11, {}), {3}: (12, {})} | custom-call | flops 9900000256 | bytes 9000000 | tf_op jit(solution)/shard_map/vals_other/pallas_call | solution.py:1375
  43.3 0.2 collective-permute-start.5
  43.5 0.0 collective-permute-done.6.s0_ref
  43.5 7.8 %scan_other.1 = (bf16[640,1536]{1,0:T(8,128)(2,1)S(1)}, bf16[12,6,128,128]{3,2,1,0:T(8,128)(2,1)S(1)}) custom-call(s32[8]{0:T(128)S(1)} %get-tuple-element.90.info, bf16[640,1536]{1,0:T(8,128)(2,1)S(1)} %get-tuple-element.99.xc_ref, bf16[12,6,128,128]{3,2,1,0:T(8,128)(2,1)S(1)} %get-tuple-element.100.s_ref, ...), custom_call_target="tpu_custom_call" | custom-call | flops 11000000512 | bytes 10000000 | tf_op jit(solution)/shard_map/scan_other/pallas_call | solution.py:1403
  51.4 0.5 collective-permute-done.8.p1
  51.9 0.0 collective-permute-start.10
  51.9 0.0 collective-permute-done.5.s0_ref
  51.9 0.0 copy-start.5
  51.9 0.0 copy-start.12
  51.9 7.9 %scan_own.1 = (bf16[640,1536]{1,0:T(8,128)(2,1)S(1)}, bf16[12,6,128,128]{3,2,1,0:T(8,128)(2,1)S(1)}) custom-call(s32[8]{0:T(128)S(1)} %get-tuple-element.90.info, bf16[640,1536]{1,0:T(8,128)(2,1)S(1)} %get-tuple-element.99.xc_ref, bf16[12,6,128,128]{3,2,1,0:T(8,128)(2,1)S(1)} %get-tuple-element.100.s_ref, ...), custom_call_target="tpu_custom_call", output_to_operand_aliasing={{0}: (7, {}), {1}: (8, {})} | custom-call | flops 11000000512 | bytes 10000000 | tf_op jit(solution)/shard_map/scan_own/pallas_call | solution.py:1403
  59.8 0.0 collective-permute-done.9.p2
  59.8 0.0 collective-permute-done.10.p3
  59.8 15.0 %gated.1 = (bf16[640,768]{1,0:T(8,128)(2,1)}, bf16[640,1536]{1,0:T(8,128)(2,1)S(1)}, bf16[640,1536]{1,0:T(8,128)(2,1)S(1)}, bf16[640,1536]{1,0:T(8,128)(2,1)S(1)...) custom-call(s32[8]{0:T(128)S(1)} %get-tuple-element.90.info, ...), custom_call_target="tpu_custom_call" | custom-call | flops 17600000000 | bytes 16000000 | tf_op jit(solution)/shard_map/gated/pallas_call | solution.py:1417
  74.8 1.5 collective-permute-start.11
  76.4 7.5 %wsum.1 = (bf16[4,48,1536]{2,1,0:T(8,128)(2,1)S(1)}, bf16[4,48,1536]{2,1,0:T(8,128)(2,1)S(1)}, bf16[4,48,1536]{2,1,0:T(8,128)(2,1)S(1)}, bf16[4,48,1536]{2,1,0:T(8,128)(2,1)S(1)}) custom-call(bf16[640,768]{1,0:T(8,128)(2,1)S(1)} %bitcast.33, bf16[672,768]{1,0:T(8,128)(2,1)S(1)} %get-tuple-element.91.normed, bf16[640,1536]{1,0:T(8,128)(2,1)S(1)} %get-tuple-element.118.hn, ...), custom_call_target="tpu_custom_call" | custom-call | flops 7699999744 | bytes 7000000 | tf_op jit(solution)/shard_map/wsum/pallas_call | solution.py:1435
  83.9 1.4 collective-permute-start.12
  85.3 0.7 collective-permute-start.15
  86.0 1.4 collective-permute-start.16
  87.4 0.0 collective-permute-done.11.gs0_ref
  87.4 21.8 %gscan.1 = (bf16[640,1536]{1,0:T(8,128)(2,1)S(1)}, f32[5,128,128]{2,1,0:T(8,128)S(1)}, f32[5,128,128]{2,1,0:T(8,128)S(1)}, f32[5,128,128]{2,1,0:T(8,128)S(1)}, f...) custom-call(s32[8]{0:T(128)S(1)} %get-tuple-element.90.info, ...), custom_call_target="tpu_custom_call" | custom-call | flops 24199999488 | bytes 22000000 | tf_op jit(solution)/shard_map/gscan/pallas_call | solution.py:1453
  109.2 0.7 collective-permute-start.13
  109.9 0.0 collective-permute-done.12
  109.9 4.0 %join.1 = (f32[672,256]{1,0:T(8,128)S(1)}, bf16[640,128]{1,0:T(8,128)(2,1)S(1)}, f32[16,128]{1,0:T(8,128)S(1)}, f32[16,256]{1,0:T(8,128)S(1)}) custom-call(s32[8]{0:T(128)S(1)} %get-tuple-element.90.info, f32[5,128,128]{2,1,0:T(8,128)S(1)} %get-tuple-element.129.ggt, f32[5,128,128]{2,1,0:T(8,128)S(1)} %get-tuple-element.130.gb, ...), custom_call_target="tpu_custom_call" | custom-call | flops 6600000000 | bytes 6000000 | tf_op jit(solution)/shard_map/join/pallas_call | solution.py:1476
  114.0 1.4 collective-permute-start.14
  115.4 0.0 collective-permute-done.13.edge
  115.4 11.2 %back.1 = (bf16[640,1536]{1,0:T(8,128)(2,1)S(1)}, bf16[2,384,768]{2,1,0:T(8,128)(2,1)S(1)}, bf16[2,384,768]{2,1,0:T(8,128)(2,1)S(1)}, f32[2,16,768]{2,1,0:T(8,128)S(1)}) custom-call(s32[8]{0:T(128)S(1)} %get-tuple-element.90.info, bf16[640,1536]{1,0:T(8,128)(2,1)S(1)} %get-tuple-element.121.gmix, bf16[16,1536]{1,0:T(8,128)(2,1)S(1)} %collective-permute-done.13.edge, ...), custom_call_target="tpu_custom_call" | custom-call | flops 13200000000 | bytes 12000000 | tf_op jit(solution)/shard_map/back/pallas_call | solution.py:1489
  126.7 0.0 copy-start.1
  126.7 0.0 collective-permute-done.15
  126.7 0.0 collective-permute-done.16
  126.7 0.3 add_convert_fusion.plane_a
  127.0 0.0 collective-permute-done.14.edge
  127.0 0.9 copy-done.1
  127.9 0.2 copy-done.4
  128.1 31.5 %collect.1 = (f32[48,1152]{1,0:T(8,128)S(1)}, f32[16,768]{1,0:T(8,128)S(1)}, f32[48,1536]{1,0:T(8,128)S(1)}, f32[640,768]{1,0:T(8,128)S(1)}) custom-call(s32[8]{0:T(128)S(1)} %get-tuple-element.90.info, bf16[640,1536]{1,0:T(8,128)(2,1)S(1)} %get-tuple-element.126.gvals, bf16[640,1536]{1,0:T(8,128)(2,1)S(1)} %get-tuple-element.119.ggate, ...), custom_call_target="tpu_custom_call" | custom-call | tf_op jit(solution)/shard_map/collect/pallas_call | solution.py:1514
  159.6 1.3 finish.1
  160.9 1.3 copy.39
  (21 shorter events, 0.0 us)
Async XLA Ops:
  0.6 4.9 %copy-start = (bf16[768,12,130]{0,2,1:T(8,128)(2,1)S(1)}, bf16[768,12,130]{0,2,1:T(8,128)(2,1)}, u32[]{:S(2)}) copy-start(bf16[768,12,130]{0,2,1:T(8,128)(2,1)} %param.16) | copy-start | bytes 7188484
  2.5 8.0 %copy-start.15 = (f32[768]{0:T(1024)S(1)}, f32[768]{0:T(1024)}, u32[]{:S(2)}) copy-start(f32[768]{0:T(1024)} %param.15) | copy-start | bytes 9220
  2.5 16.3 %copy-start.2 = (bf16[1,640,768]{2,1,0:T(8,128)(2,1)S(1)}, bf16[1,640,768]{2,1,0:T(8,128)(2,1)}, u32[]{:S(2)}) copy-start(bf16[1,640,768]{2,1,0:T(8,128)(2,1)} %param.14) | copy-start | bytes 2949124
  2.5 16.3 %copy-start.8 = (f32[7,256]{1,0:T(8,128)S(1)}, f32[7,256]{1,0:T(8,128)}, u32[]{:S(2)}) copy-start(f32[7,256]{1,0:T(8,128)} %taps_ref.1) | copy-start | bytes 21508
  2.5 16.3 %copy-start.9 = (s32[1,1280]{1,0:T(1,128)S(1)}, s32[1,1280]{1,0:T(1,128)}, u32[]{:S(2)}) copy-start(s32[1,1280]{1,0:T(1,128)} %live_ref.1) | copy-start | bytes 15364
  2.5 16.3 %copy-start.10 = (s32[1,4]{1,0:T(1,128)S(1)}, s32[1,4]{1,0:T(1,128)}, u32[]{:S(2)}) copy-start(s32[1,4]{1,0:T(1,128)} %starts.1) | copy-start | bytes 52
  2.5 16.3 %collective-permute-start = (f32[48,768]{1,0:T(8,128)}, f32[48,768]{1,0:T(8,128)}, u32[]{:S(2)}, u32[]{:S(2)}) collective-permute-start(f32[48,768]{1,0:T(8,128)} %small.1.small_a), channel_id=1, source_target_pairs={{0,1},{1,0},{2,3},{3,2},{4,5},{5,4},{6,7},{7,6},{8,9},{9,8},{10,11... | collective-permute-start | bytes 442376 | tf_op jit(solution)/shard_map/ppermute | solution.py:1262
  6.4 10.5 %collective-permute-start.1 = (bf16[192,768]{1,0:T(8,128)(2,1)}, bf16[192,768]{1,0:T(8,128)(2,1)}, u32[]{:S(2)}, u32[]{:S(2)}) collective-permute-start(bf16[192,768]{1,0:T(8,128)(2,1)} %bitcast.6), channel_id=1, source_target_pairs={{0,1},{1,0},{2,3},{3,2},{4,5},{5,4},{6,7},{7,6},{8,9},{9,8},{10,11... | collective-permute-start | bytes 884744 | tf_op jit(solution)/shard_map/ppermute | solution.py:1262
  8.5 27.6 %collective-permute-start.7 = (bf16[192,1536]{1,0:T(8,128)(2,1)S(1)}, bf16[192,1536]{1,0:T(8,128)(2,1)S(1)}, u32[]{:S(2)}, u32[]{:S(2)}) collective-permute-start(bf16[192,1536]{1,0:T(8,128)(2,1)S(1)} %pad_maximum_fusion), channel_id=1, source_target_pairs={{0,1},{1,0},{2,3},{3,2},{4,5},{5,4},{6,7},{7,6},{8,9},{9,8},{10,11... | collective-permute-start | bytes 1769480 | tf_op jit(solution)/shard_map/ppermute | solution.py:1262
  16.9 11.0 %collective-permute-start.2 = (bf16[192,768]{1,0:T(8,128)(2,1)}, bf16[192,768]{1,0:T(8,128)(2,1)S(1)}, u32[]{:S(2)}, u32[]{:S(2)}) collective-permute-start(bf16[192,768]{1,0:T(8,128)(2,1)} %collective-permute-done.1.refs_0_), channel_id=1, source_target_pairs={{0,4},{2,6},{4,0},{6,2},{8,12},{10,14},{12,8},{14,10},{16,20},{18,... | collective-permute-start | bytes 884744 | tf_op jit(solution)/shard_map/ppermute | solution.py:1266
  18.9 1.0 copy-start.6
  19.9 0.9 copy-start.7
  27.9 8.8 %collective-permute-start.3 = (bf16[192,768]{1,0:T(8,128)(2,1)}, bf16[192,768]{1,0:T(8,128)(2,1)S(1)}, u32[]{:S(2)}, u32[]{:S(2)}) collective-permute-start(bf16[192,768]{1,0:T(8,128)(2,1)} %collective-permute-done.1.refs_0_), channel_id=1, source_target_pairs={{0,2},{2,0},{4,6},{6,4},{8,10},{10,8},{12,14},{14,12},{16,18},{18,... | collective-permute-start | bytes 884744 | tf_op jit(solution)/shard_map/ppermute | solution.py:1266
  27.9 8.7 %collective-permute-start.4 = (bf16[192,768]{1,0:T(8,128)(2,1)S(1)}, bf16[192,768]{1,0:T(8,128)(2,1)S(1)}, u32[]{:S(2)}, u32[]{:S(2)}) collective-permute-start(bf16[192,768]{1,0:T(8,128)(2,1)S(1)} %collective-permute-done.2.refs_1_), channel_id=1, source_target_pairs={{0,2},{2,0},{4,6},{6,4},{8,10},{10,8},{12,14},{14,12},{16,18},{18,... | collective-permute-start | bytes 884744 | tf_op jit(solution)/shard_map/ppermute | solution.py:1266
  34.5 9.0 %collective-permute-start.6 = (bf16[6,64,128]{2,1,0:T(8,128)(2,1)S(1)}, bf16[6,64,128]{2,1,0:T(8,128)(2,1)S(1)}, u32[]{:S(2)}, u32[]{:S(2)}) collective-permute-start(bf16[6,64,128]{2,1,0:T(8,128)(2,1)S(1)} %get-tuple-element.104), channel_id=1, source_target_pairs={{0,1},{1,0},{2,3},{3,2},{4,5},{5,4},{6,7},{7,6},{8,9},{9,8},{10,11... | collective-permute-start | bytes 294920 | tf_op jit(solution)/shard_map/ppermute | solution.py:1262
  36.1 23.7 %collective-permute-start.9 = (bf16[192,1536]{1,0:T(8,128)(2,1)S(1)}, bf16[192,1536]{1,0:T(8,128)(2,1)S(1)}, u32[]{:S(2)}, u32[]{:S(2)}) collective-permute-start(bf16[192,1536]{1,0:T(8,128)(2,1)S(1)} %collective-permute-done.7.p0), channel_id=1, source_target_pairs={{0,2},{2,0},{4,6},{6,4},{8,10},{10,8},{12,14},{14,12},{16,18},{18,... | collective-permute-start | bytes 1769480 | tf_op jit(solution)/shard_map/ppermute | solution.py:1266
  36.1 15.7 %collective-permute-start.8 = (bf16[192,1536]{1,0:T(8,128)(2,1)S(1)}, bf16[192,1536]{1,0:T(8,128)(2,1)S(1)}, u32[]{:S(2)}, u32[]{:S(2)}) collective-permute-start(bf16[192,1536]{1,0:T(8,128)(2,1)S(1)} %collective-permute-done.7.p0), channel_id=1, source_target_pairs={{0,4},{2,6},{4,0},{6,2},{8,12},{10,14},{12,8},{14,10},{16,20},{18,... | collective-permute-start | bytes 1769480 | tf_op jit(solution)/shard_map/ppermute | solution.py:1266
  43.3 8.6 %collective-permute-start.5 = (bf16[6,64,128]{2,1,0:T(8,128)(2,1)S(1)}, bf16[6,64,128]{2,1,0:T(8,128)(2,1)S(1)}, u32[]{:S(2)}, u32[]{:S(2)}) collective-permute-start(bf16[6,64,128]{2,1,0:T(8,128)(2,1)S(1)} %get-tuple-element.101), channel_id=1, source_target_pairs={{0,1},{1,0},{2,3},{3,2},{4,5},{5,4},{6,7},{7,6},{8,9},{9,8},{10,11... | collective-permute-start | bytes 294920 | tf_op jit(solution)/shard_map/ppermute | solution.py:1262
  51.9 7.9 %collective-permute-start.10 = (bf16[192,1536]{1,0:T(8,128)(2,1)S(1)}, bf16[192,1536]{1,0:T(8,128)(2,1)S(1)}, u32[]{:S(2)}, u32[]{:S(2)}) collective-permute-start(bf16[192,1536]{1,0:T(8,128)(2,1)S(1)} %collective-permute-done.8.p1), channel_id=1, source_target_pairs={{0,2},{2,0},{4,6},{6,4},{8,10},{10,8},{12,14},{14,12},{16,18},{18,... | collective-permute-start | bytes 1769480 | tf_op jit(solution)/shard_map/ppermute | solution.py:1266
  51.9 7.9 %copy-start.3 = (bf16[1,640,768]{2,1,0:T(8,128)(2,1)S(1)}, bf16[1,640,768]{2,1,0:T(8,128)(2,1)}, u32[]{:S(2)}) copy-start(bf16[1,640,768]{2,1,0:T(8,128)(2,1)} %param.25) | copy-start | bytes 2949124
  51.9 7.9 %copy-start.5 = (bf16[12,64,768]{2,1,0:T(8,128)(2,1)S(1)}, bf16[12,64,768]{2,1,0:T(8,128)(2,1)}, u32[]{:S(2)}) copy-start(bf16[12,64,768]{2,1,0:T(8,128)(2,1)} %param.24) | copy-start | bytes 3538948
  51.9 7.9 %copy-start.12 = (f32[3,5,128,128]{3,2,1,0:T(8,128)S(1)}, f32[3,5,128,128]{3,2,1,0:T(8,128)}, u32[]{:S(2)}) copy-start(f32[3,5,128,128]{3,2,1,0:T(8,128)} %get-tuple-element.109.tc) | copy-start | bytes 2949124
  74.8 12.6 %collective-permute-start.11 = (bf16[12,64,128]{2,1,0:T(8,128)(2,1)S(1)}, bf16[12,64,128]{2,1,0:T(8,128)(2,1)S(1)}, u32[]{:S(2)}, u32[]{:S(2)}) collective-permute-start(bf16[12,64,128]{2,1,0:T(8,128)(2,1)S(1)} %get-tuple-element.115), channel_id=1, source_target_pairs={{0,1},{1,0},{2,3},{3,2},{4,5},{5,4},{6,7},{7,6},{8,9},{9,8},{10,11... | collective-permute-start | bytes 589832 | tf_op jit(solution)/shard_map/ppermute | solution.py:1262
  83.9 26.1 %collective-permute-start.12 = (bf16[4,48,1536]{2,1,0:T(8,128)(2,1)S(1)}, bf16[4,48,1536]{2,1,0:T(8,128)(2,1)S(1)}, u32[]{:S(2)}, u32[]{:S(2)}) collective-permute-start(bf16[4,48,1536]{2,1,0:T(8,128)(2,1)S(1)} %get-tuple-element.120), channel_id=1, source_target_pairs={{0,5},{1,4},{2,7},{3,6},{4,1},{5,0},{6,3},{7,2},{8,13},{9,12},{10,... | collective-permute-start | bytes 1769480 | tf_op jit(solution)/shard_map/ppermute | solution.py:1271
  85.3 41.4 %collective-permute-start.15 = (bf16[4,48,1536]{2,1,0:T(8,128)(2,1)S(1)}, bf16[4,48,1536]{2,1,0:T(8,128)(2,1)S(1)}, u32[]{:S(2)}, u32[]{:S(2)}) collective-permute-start(bf16[4,48,1536]{2,1,0:T(8,128)(2,1)S(1)} %get-tuple-element.151), channel_id=1, source_target_pairs={{0,4},{2,6},{4,0},{6,2},{8,12},{10,14},{12,8},{14,10},{16,20},{18,... | collective-permute-start | bytes 1769480 | tf_op jit(solution)/shard_map/ppermute | solution.py:1266
  86.0 40.7 %collective-permute-start.16 = (bf16[4,48,1536]{2,1,0:T(8,128)(2,1)S(1)}, bf16[4,48,1536]{2,1,0:T(8,128)(2,1)S(1)}, u32[]{:S(2)}, u32[]{:S(2)}) collective-permute-start(bf16[4,48,1536]{2,1,0:T(8,128)(2,1)S(1)} %get-tuple-element.152), channel_id=1, source_target_pairs={{0,1},{1,0},{2,3},{3,2},{4,5},{5,4},{6,7},{7,6},{8,9},{9,8},{10,11... | collective-permute-start | bytes 1769480 | tf_op jit(solution)/shard_map/ppermute | solution.py:1262
  87.4 22.5 %copy-start.11 = (f32[640,384]{1,0:T(8,128)S(1)}, f32[640,384]{1,0:T(8,128)}, u32[]{:S(2)}) copy-start(f32[640,384]{1,0:T(8,128)} %get-tuple-element.137.sig) | copy-start | bytes 2949124
  87.4 22.5 %copy-start.13 = (f32[672,256]{1,0:T(8,128)S(1)}, f32[672,256]{1,0:T(8,128)}, u32[]{:S(2)}) copy-start(f32[672,256]{1,0:T(8,128)} %get-tuple-element.136.dsl) | copy-start | bytes 2064388
  87.4 22.5 %copy-start.14 = (bf16[640,256]{1,0:T(8,128)(2,1)S(1)}, bf16[640,256]{1,0:T(8,128)(2,1)}, u32[]{:S(2)}) copy-start(bf16[640,256]{1,0:T(8,128)(2,1)} %get-tuple-element.135.maps) | copy-start | bytes 983044
  109.2 6.2 %collective-permute-start.13 = (bf16[16,1536]{1,0:T(8,128)(2,1)S(1)}, bf16[16,1536]{1,0:T(8,128)(2,1)S(1)}, u32[]{:S(2)}, u32[]{:S(2)}) collective-permute-start(bf16[16,1536]{1,0:T(8,128)(2,1)S(1)} %get-tuple-element.122), channel_id=1, source_target_pairs={{0,1},{1,0},{2,3},{3,2},{4,5},{5,4},{6,7},{7,6},{8,9},{9,8},{10,11... | collective-permute-start | bytes 147464 | tf_op jit(solution)/shard_map/ppermute | solution.py:1262
  114.0 13.0 %collective-permute-start.14 = (f32[16,256]{1,0:T(8,128)S(1)}, f32[16,256]{1,0:T(8,128)S(1)}, u32[]{:S(2)}, u32[]{:S(2)}) collective-permute-start(f32[16,256]{1,0:T(8,128)S(1)} %get-tuple-element.139), channel_id=1, source_target_pairs={{0,1},{1,0},{2,3},{3,2},{4,5},{5,4},{6,7},{7,6},{8,9},{9,8},{10,11... | collective-permute-start | bytes 49160 | tf_op jit(solution)/shard_map/ppermute | solution.py:1262
  126.7 1.3 copy-start.1
  126.7 1.4 copy-start.4
